TPU v7x, 32 devices: a whole 2x2x4 slice. The times are simulated.
32 devices in a mesh: dp: 8 (over y, x, core), seq: 4 (over z).
Axes of the slice: x: 2, y: 2, z: 4, core: 2. Of those that a mesh axis runs over, the one named last changes fastest.
Arguments:
- query_rows: bfloat16 [4096, 4096], P(('dp', 'seq')), parts along dimension 0, may hold values from -32 to 32
- key_rows: bfloat16 [4096, 4096], P(('dp', 'seq')), parts along dimension 0, may hold values from -32 to 32
- value_rows: bfloat16 [4096, 4096], P(('dp', 'seq')), parts along dimension 0, may hold values from -6 to 6
- query_tangent: bfloat16 [4096, 4096], P(('dp', 'seq')), parts along dimension 0, may hold values from -6 to 6
- key_tangent: bfloat16 [4096, 4096], P(('dp', 'seq')), parts along dimension 0, may hold values from -6 to 6
- value_tangent: bfloat16 [4096, 4096], P(('dp', 'seq')), parts along dimension 0, may hold values from -6 to 6
Outputs:
- attended: bfloat16 [4096, 4096], P(('dp', 'seq')), parts along dimension 0
- attended_tangent: bfloat16 [4096, 4096], P(('dp', 'seq')), parts along dimension 0
There are 8 independent parts, one for each index of `dp`. A program takes and returns all parts, laid end to end along the dimension named above; each array names one. Nothing has to cross between parts.
All inputs are finite; a program needn't handle non-finite values.
Results may differ from a plain program's by a relative error of at most 0.0049.
Values may be sent and summed in bfloat16 or wider, within the bound.
No kernel may reach another device: no remote copies, remote signals or barrier semaphores. Data moves between devices by JAX's collectives and lax.ppermute only.
A program may use at most 64 MiB of HBM per device.

v0:
```python
import math

import jax
import jax.numpy as jnp
from jax import lax
from jax.sharding import PartitionSpec as P

HEADS = 32
HEAD = 128


def attend(head_queries, head_keys, head_values, query_tangent, key_tangent, value_tangent):
    length, head_count, head_width = head_queries.shape
    block_rows = math.gcd(length, 512)
    block_count = length // block_rows
    score_scale = head_width ** (-0.5)
    query_blocks = head_queries.reshape(block_count, block_rows, head_count, head_width)
    tangent_blocks = query_tangent.reshape(block_count, block_rows, head_count, head_width)
    keys_joined = jnp.concatenate([head_keys, key_tangent], axis=2)
    values_joined = jnp.concatenate([head_values, value_tangent], axis=0)

    def one_block(pieces):
        query_block, tangent_block = pieces
        scores = (
            jnp.einsum("qhd,khd->hqk", query_block, head_keys, preferred_element_type=jnp.float32)
            * score_scale
        )
        paired = jnp.concatenate([tangent_block, query_block], axis=2)
        score_tangent = (
            jnp.einsum("qhd,khd->hqk", paired, keys_joined, preferred_element_type=jnp.float32)
            * score_scale
        )
        row_max = jnp.max(scores, axis=2, keepdims=True)
        raised = jnp.exp(scores - row_max)
        exact_weights = raised / jnp.sum(raised, axis=2, keepdims=True)
        weights = exact_weights.astype(jnp.bfloat16)
        output = jnp.einsum(
            "hqk,khd->qhd", weights, head_values, preferred_element_type=jnp.float32
        ).astype(jnp.bfloat16)
        mean_tangent = jnp.sum(exact_weights * score_tangent, axis=2, keepdims=True)
        weight_tangent = (exact_weights * (score_tangent - mean_tangent)).astype(jnp.bfloat16)
        stacked = jnp.concatenate([weight_tangent, weights], axis=2)
        tangent = jnp.einsum(
            "hqk,khd->qhd", stacked, values_joined, preferred_element_type=jnp.float32
        )
        return (output, tangent.astype(jnp.bfloat16))

    outputs, tangents = lax.map(one_block, (query_blocks, tangent_blocks))
    return (
        outputs.reshape(length, head_count, head_width),
        tangents.reshape(length, head_count, head_width),
    )


def attend_items(pieces):
    flat = tuple((piece[:, 0] for piece in pieces))
    head_output, head_tangent = attend(*flat)
    return (head_output[:, None], head_tangent[:, None])


def on_device(query_rows, key_rows, value_rows, query_tangent, key_tangent, value_tangent):
    local_rows = query_rows.shape[0]
    groups = lax.axis_size("seq")
    per_group = HEADS // groups
    split_queries = query_rows.reshape(local_rows, groups, per_group, HEAD)
    split_keys = key_rows.reshape(local_rows, groups, per_group, HEAD)
    split_values = value_rows.reshape(local_rows, groups, per_group, HEAD)
    split_dquery = query_tangent.reshape(local_rows, groups, per_group, HEAD)
    split_dkey = key_tangent.reshape(local_rows, groups, per_group, HEAD)
    split_dvalue = value_tangent.reshape(local_rows, groups, per_group, HEAD)
    head_output, head_tangent = attend_items(
        (
            lax.all_to_all(split_queries, "seq", split_axis=1, concat_axis=0, tiled=True),
            lax.all_to_all(split_keys, "seq", split_axis=1, concat_axis=0, tiled=True),
            lax.all_to_all(split_values, "seq", split_axis=1, concat_axis=0, tiled=True),
            lax.all_to_all(split_dquery, "seq", split_axis=1, concat_axis=0, tiled=True),
            lax.all_to_all(split_dkey, "seq", split_axis=1, concat_axis=0, tiled=True),
            lax.all_to_all(split_dvalue, "seq", split_axis=1, concat_axis=0, tiled=True),
        )
    )
    token_output, token_tangent = (
        lax.all_to_all(head_output, "seq", split_axis=0, concat_axis=1, tiled=True),
        lax.all_to_all(head_tangent, "seq", split_axis=0, concat_axis=1, tiled=True),
    )
    attended = token_output.reshape(local_rows, HEADS * HEAD)
    attended_tangent = token_tangent.reshape(local_rows, HEADS * HEAD)
    return (attended, attended_tangent)


def solution(mesh):
    return jax.shard_map(
        on_device,
        mesh=mesh,
        in_specs=(
            P(("dp", "seq"), None),
            P(("dp", "seq"), None),
            P(("dp", "seq"), None),
            P(("dp", "seq"), None),
            P(("dp", "seq"), None),
            P(("dp", "seq"), None),
        ),
        out_specs=(P(("dp", "seq"), None), P(("dp", "seq"), None)),
        check_vma=False,
    )
```

profile of v0, /device:TPU:0, one launch (start us, length us, event | category | flops | bytes accessed | tf_op | source)
XLA Modules:
  0.0 246.2 jit_solution(17491115689676001502)
XLA Ops:
  0.6 1.6 copy.32
  2.3 1.3 copy.33
  3.6 6.3 %all-to-all-start = ((bf16[128,4,8,128]{3,0,2,1:T(8,128)(2,1)}), bf16[128,4,8,128]{3,0,2,1:T(8,128)(2,1)S(1)}, u32[]{:S(2)}, u32[]{:S(2)}) async-start(bf16[128,4,8,128]{3,0,2,1:T(8,128)(2,1)} %copy.33), calls=%async_computation | async-start | bytes 2097152 | tf_op jit(solution)/shard_map/all_to_all | solution.py:73
  9.9 1.6 copy.35
  11.5 1.3 copy.36
  12.8 22.8 %all-to-all-done = bf16[128,4,8,128]{3,0,2,1:T(8,128)(2,1)S(1)} async-done(((bf16[128,4,8,128]{3,0,2,1:T(8,128)(2,1)}), bf16[128,4,8,128]{3,0,2,1:T(8,128)(2,1)S(1)}, u32[]{:S(2)}, u32[]{:S(2)}) %all-to-all-start) | async-done | bytes 1048608 | tf_op jit(solution)/shard_map/all_to_all | solution.py:73
  35.6 3.5 %all-to-all-start.1 = ((bf16[128,4,8,128]{3,0,2,1:T(8,128)(2,1)}), bf16[128,4,8,128]{3,0,2,1:T(8,128)(2,1)S(1)}, u32[]{:S(2)}, u32[]{:S(2)}) async-start(bf16[128,4,8,128]{3,0,2,1:T(8,128)(2,1)} %copy.36), calls=%async_computation.1 | async-start | bytes 2097152 | tf_op jit(solution)/shard_map/all_to_all | solution.py:74
  39.1 1.6 copy.47
  40.8 1.3 copy.48
  42.1 22.3 %all-to-all-done.1 = bf16[128,4,8,128]{3,0,2,1:T(8,128)(2,1)S(1)} async-done(((bf16[128,4,8,128]{3,0,2,1:T(8,128)(2,1)}), bf16[128,4,8,128]{3,0,2,1:T(8,128)(2,1)S(1)}, u32[]{:S(2)}, u32[]{:S(2)}) %all-to-all-start.1) | async-done | bytes 1048608 | tf_op jit(solution)/shard_map/all_to_all | solution.py:74
  64.3 3.5 %all-to-all-start.5 = ((bf16[128,4,8,128]{3,0,2,1:T(8,128)(2,1)}), bf16[128,4,8,128]{3,0,2,1:T(8,128)(2,1)S(1)}, u32[]{:S(2)}, u32[]{:S(2)}) async-start(bf16[128,4,8,128]{3,0,2,1:T(8,128)(2,1)} %copy.48), calls=%async_computation.5 | async-start | bytes 2097152 | tf_op jit(solution)/shard_map/all_to_all | solution.py:76
  67.9 2.3 copy.50
  70.1 2.3 copy.51
  72.4 20.6 %all-to-all-done.5 = bf16[128,4,8,128]{3,0,2,1:T(8,128)(2,1)S(1)} async-done(((bf16[128,4,8,128]{3,0,2,1:T(8,128)(2,1)}), bf16[128,4,8,128]{3,0,2,1:T(8,128)(2,1)S(1)}, u32[]{:S(2)}, u32[]{:S(2)}) %all-to-all-start.5) | async-done | bytes 1048608 | tf_op jit(solution)/shard_map/all_to_all | solution.py:76
  93.0 4.3 %all-to-all-start.6 = ((bf16[128,4,8,128]{3,0,2,1:T(8,128)(2,1)}), bf16[128,4,8,128]{3,0,2,1:T(8,128)(2,1)}, u32[]{:S(2)}, u32[]{:S(2)}) async-start(bf16[128,4,8,128]{3,0,2,1:T(8,128)(2,1)} %copy.51), calls=%async_computation.6 | async-start | bytes 2097152 | tf_op jit(solution)/shard_map/all_to_all | solution.py:77
  97.3 2.3 copy.38
  99.6 2.3 copy.39
  101.8 20.7 %all-to-all-done.6 = bf16[128,4,8,128]{3,0,2,1:T(8,128)(2,1)} async-done(((bf16[128,4,8,128]{3,0,2,1:T(8,128)(2,1)}), bf16[128,4,8,128]{3,0,2,1:T(8,128)(2,1)}, u32[]{:S(2)}, u32[]{:S(2)}) %all-to-all-start.6) | async-done | bytes 1048608 | tf_op jit(solution)/shard_map/all_to_all | solution.py:77
  122.6 4.3 %all-to-all-start.2 = ((bf16[128,4,8,128]{3,0,2,1:T(8,128)(2,1)}), bf16[128,4,8,128]{3,0,2,1:T(8,128)(2,1)}, u32[]{:S(2)}, u32[]{:S(2)}) async-start(bf16[128,4,8,128]{3,0,2,1:T(8,128)(2,1)} %copy.39), calls=%async_computation.2 | async-start | bytes 2097152 | tf_op jit(solution)/shard_map/all_to_all | solution.py:75
  126.9 2.3 copy.44
  129.1 2.3 copy.45
  131.4 0.0 copy-done.1
  131.4 0.1 copy.34
  131.5 0.1 copy.37
  131.6 1.3 copy.49
  132.9 1.3 copy.52
  134.2 4.5 %fusion.18 = f32[8,512,512]{1,2,0:T(8,128)} fusion(bf16[512,8,128]{2,0,1:T(8,128)(2,1)S(1)} %bitcast.58, bf16[512,8,128]{2,0,1:T(8,128)(2,1)S(1)} %bitcast.62, bf16[512,8,128]{2,0,1:T(8,128)(2,1)S(1)} %bitcast.63, bf16[512,8,128]{2,0,1:T(8,128)(2,1)S(1)} %bitcast.60), kind=kOutput, calls=%fused_computation.19 | convolution fusion | flops 1082130432 | bytes 12582912 | tf_op jit(solution)/shard_map/while/body/eval_jaxpr/qhd,khd->hqk/dot_general | solution.py:30
  138.7 4.9 %fusion.43 = (f32[8,512]{1,0:T(8,128)S(1)}, f32[8,512,512]{1,2,0:T(8,128)}) fusion(bf16[512,8,128]{2,0,1:T(8,128)(2,1)S(1)} %bitcast.59, bf16[512,8,128]{2,0,1:T(8,128)(2,1)S(1)} %bitcast.61), kind=kOutput, calls=%fused_computation.36 | convolution fusion | flops 543162880 | bytes 10502144 | tf_op jit(solution)/shard_map/while/body/eval_jaxpr/sub | solution.py:34
  143.7 8.5 %all-to-all-done.2 = bf16[128,4,8,128]{3,0,2,1:T(8,128)(2,1)} async-done(((bf16[128,4,8,128]{3,0,2,1:T(8,128)(2,1)}), bf16[128,4,8,128]{3,0,2,1:T(8,128)(2,1)}, u32[]{:S(2)}, u32[]{:S(2)}) %all-to-all-start.2) | async-done | bytes 1048608 | tf_op jit(solution)/shard_map/all_to_all | solution.py:75
  152.1 3.5 %all-to-all-start.4 = ((bf16[128,4,8,128]{3,0,2,1:T(8,128)(2,1)}), bf16[128,4,8,128]{3,0,2,1:T(8,128)(2,1)S(1)}, u32[]{:S(2)}, u32[]{:S(2)}) async-start(bf16[128,4,8,128]{3,0,2,1:T(8,128)(2,1)} %copy.45), calls=%async_computation.4 | async-start | bytes 2097152 | tf_op jit(solution)/shard_map/all_to_all | solution.py:78
  155.7 0.0 copy-start
  155.7 14.4 %multiply_convert_fusion = bf16[8,512,512]{1,2,0:T(8,128)(2,1)} fusion(f32[8,512,512]{1,2,0:T(8,128)} %fusion.18, f32[8,512,512]{1,2,0:T(8,128)} %get-tuple-element.21, f32[8,512]{1,0:T(8,128)S(1)} %get-tuple-element.20), kind=kOutput, calls=%fused_computation.6 | output fusion | flops 16781824 | bytes 20987904 | tf_op jit(solution)/shard_map/while/body/eval_jaxpr/sub | solution.py:41
  170.0 1.3 copy.40
  171.3 3.2 %fusion.42 = bf16[8,512,512]{1,2,0:T(8,128)(2,1)} fusion(f32[8,512,512]{1,2,0:T(8,128)S(1)} %copy-done, f32[8,512]{1,0:T(8,128)S(1)} %get-tuple-element.20), kind=kLoop, calls=%fused_computation.35 | loop fusion | flops 4194304 | bytes 12599296 | tf_op jit(solution)/shard_map/while/body/eval_jaxpr/convert_element_type | solution.py:36
  174.5 6.3 %all-to-all-done.4 = bf16[128,4,8,128]{3,0,2,1:T(8,128)(2,1)S(1)} async-done(((bf16[128,4,8,128]{3,0,2,1:T(8,128)(2,1)}), bf16[128,4,8,128]{3,0,2,1:T(8,128)(2,1)S(1)}, u32[]{:S(2)}, u32[]{:S(2)}) %all-to-all-start.4) | async-done | bytes 1048608 | tf_op jit(solution)/shard_map/all_to_all | solution.py:78
  180.8 0.1 copy.46
  180.9 4.9 %fusion.31 = bf16[512,1,8,128]{0,3,2,1:T(8,128)(2,1)S(1)} fusion(bf16[8,512,512]{1,2,0:T(8,128)(2,1)} %fusion.42, bf16[8,512,512]{1,2,0:T(8,128)(2,1)} %multiply_convert_fusion, bf16[512,8,128]{2,0,1:T(8,128)(2,1)S(1)} %bitcast.78, bf16[512,8,128]{2,0,1:T(8,128)(2,1)S(1)} %bitcast.76), kind=kOutput, calls=%fused_computation.29 | convolution fusion | flops 1095237632 | bytes 11534336 | tf_op jit(solution)/shard_map/while/body/eval_jaxpr/hqk,khd->qhd/dot_general | solution.py:43
  185.9 1.5 copy.55
  187.3 3.7 %all-to-all-start.7 = ((bf16[512,1,8,128]{3,2,1,0:T(8,128)(2,1)}), bf16[512,1,8,128]{3,2,1,0:T(8,128)(2,1)S(1)}, u32[]{:S(2)}, u32[]{:S(2)}) async-start(bf16[512,1,8,128]{3,2,1,0:T(8,128)(2,1)} %copy.55), calls=%async_computation.7 | async-start | bytes 2097152 | tf_op jit(solution)/shard_map/all_to_all | solution.py:83
  191.0 3.6 %fusion.30 = bf16[512,1,8,128]{3,0,2,1:T(8,128)(2,1)S(1)} fusion(bf16[8,512,512]{1,2,0:T(8,128)(2,1)} %fusion.42, bf16[512,8,128]{2,0,1:T(8,128)(2,1)S(1)} %bitcast.77), kind=kOutput, calls=%fused_computation.28 | convolution fusion | flops 537395200 | bytes 6291456 | tf_op jit(solution)/shard_map/while/body/eval_jaxpr/hqk,khd->qhd/dot_general | solution.py:37
  194.7 1.6 copy.42
  196.3 19.7 %all-to-all-done.7 = bf16[512,1,8,128]{3,2,1,0:T(8,128)(2,1)S(1)} async-done(((bf16[512,1,8,128]{3,2,1,0:T(8,128)(2,1)}), bf16[512,1,8,128]{3,2,1,0:T(8,128)(2,1)S(1)}, u32[]{:S(2)}, u32[]{:S(2)}) %all-to-all-start.7) | async-done | bytes 1048608 | tf_op jit(solution)/shard_map/all_to_all | solution.py:83
  216.0 3.5 %all-to-all-start.3 = ((bf16[512,1,8,128]{3,2,1,0:T(8,128)(2,1)}), bf16[512,1,8,128]{3,2,1,0:T(8,128)(2,1)S(1)}, u32[]{:S(2)}, u32[]{:S(2)}) async-start(bf16[512,1,8,128]{3,2,1,0:T(8,128)(2,1)} %copy.42), calls=%async_computation.3 | async-start | bytes 2097152 | tf_op jit(solution)/shard_map/all_to_all | solution.py:82
  219.6 0.2 copy.56
  219.7 1.3 reshape.50
  221.0 23.7 %all-to-all-done.3 = bf16[512,1,8,128]{3,2,1,0:T(8,128)(2,1)S(1)} async-done(((bf16[512,1,8,128]{3,2,1,0:T(8,128)(2,1)}), bf16[512,1,8,128]{3,2,1,0:T(8,128)(2,1)S(1)}, u32[]{:S(2)}, u32[]{:S(2)}) %all-to-all-start.3) | async-done | bytes 1048608 | tf_op jit(solution)/shard_map/all_to_all | solution.py:82
  244.7 0.2 copy.43
  244.9 1.3 reshape.46
  (2 shorter events, 0.0 us)
Async XLA Ops:
  3.6 32.0 %all-to-all-start = ((bf16[128,4,8,128]{3,0,2,1:T(8,128)(2,1)}), bf16[128,4,8,128]{3,0,2,1:T(8,128)(2,1)S(1)}, u32[]{:S(2)}, u32[]{:S(2)}) async-start(bf16[128,4,8,128]{3,0,2,1:T(8,128)(2,1)} %copy.33), calls=%async_computation | async-start | bytes 2097152 | tf_op jit(solution)/shard_map/all_to_all | solution.py:73
  35.6 28.7 %all-to-all-start.1 = ((bf16[128,4,8,128]{3,0,2,1:T(8,128)(2,1)}), bf16[128,4,8,128]{3,0,2,1:T(8,128)(2,1)S(1)}, u32[]{:S(2)}, u32[]{:S(2)}) async-start(bf16[128,4,8,128]{3,0,2,1:T(8,128)(2,1)} %copy.36), calls=%async_computation.1 | async-start | bytes 2097152 | tf_op jit(solution)/shard_map/all_to_all | solution.py:74
  64.3 28.7 %all-to-all-start.5 = ((bf16[128,4,8,128]{3,0,2,1:T(8,128)(2,1)}), bf16[128,4,8,128]{3,0,2,1:T(8,128)(2,1)S(1)}, u32[]{:S(2)}, u32[]{:S(2)}) async-start(bf16[128,4,8,128]{3,0,2,1:T(8,128)(2,1)} %copy.48), calls=%async_computation.5 | async-start | bytes 2097152 | tf_op jit(solution)/shard_map/all_to_all | solution.py:76
  93.0 38.3 %copy-start.1 = (bf16[128,4,8,128]{3,0,2,1:T(8,128)(2,1)}, bf16[128,4,8,128]{3,0,2,1:T(8,128)(2,1)S(1)}, u32[]{:S(2)}) copy-start(bf16[128,4,8,128]{3,0,2,1:T(8,128)(2,1)S(1)} %all-to-all-done.5) | copy-start | bytes 3145732
  93.0 29.5 %all-to-all-start.6 = ((bf16[128,4,8,128]{3,0,2,1:T(8,128)(2,1)}), bf16[128,4,8,128]{3,0,2,1:T(8,128)(2,1)}, u32[]{:S(2)}, u32[]{:S(2)}) async-start(bf16[128,4,8,128]{3,0,2,1:T(8,128)(2,1)} %copy.51), calls=%async_computation.6 | async-start | bytes 2097152 | tf_op jit(solution)/shard_map/all_to_all | solution.py:77
  122.6 29.5 %all-to-all-start.2 = ((bf16[128,4,8,128]{3,0,2,1:T(8,128)(2,1)}), bf16[128,4,8,128]{3,0,2,1:T(8,128)(2,1)}, u32[]{:S(2)}, u32[]{:S(2)}) async-start(bf16[128,4,8,128]{3,0,2,1:T(8,128)(2,1)} %copy.39), calls=%async_computation.2 | async-start | bytes 2097152 | tf_op jit(solution)/shard_map/all_to_all | solution.py:75
  152.1 28.7 %all-to-all-start.4 = ((bf16[128,4,8,128]{3,0,2,1:T(8,128)(2,1)}), bf16[128,4,8,128]{3,0,2,1:T(8,128)(2,1)S(1)}, u32[]{:S(2)}, u32[]{:S(2)}) async-start(bf16[128,4,8,128]{3,0,2,1:T(8,128)(2,1)} %copy.45), calls=%async_computation.4 | async-start | bytes 2097152 | tf_op jit(solution)/shard_map/all_to_all | solution.py:78
  155.7 15.7 %copy-start = (f32[8,512,512]{1,2,0:T(8,128)S(1)}, f32[8,512,512]{1,2,0:T(8,128)}, u32[]{:S(2)}) copy-start(f32[8,512,512]{1,2,0:T(8,128)} %get-tuple-element.21) | copy-start | bytes 25165828
  187.3 28.7 %all-to-all-start.7 = ((bf16[512,1,8,128]{3,2,1,0:T(8,128)(2,1)}), bf16[512,1,8,128]{3,2,1,0:T(8,128)(2,1)S(1)}, u32[]{:S(2)}, u32[]{:S(2)}) async-start(bf16[512,1,8,128]{3,2,1,0:T(8,128)(2,1)} %copy.55), calls=%async_computation.7 | async-start | bytes 2097152 | tf_op jit(solution)/shard_map/all_to_all | solution.py:83
  216.0 28.7 %all-to-all-start.3 = ((bf16[512,1,8,128]{3,2,1,0:T(8,128)(2,1)}), bf16[512,1,8,128]{3,2,1,0:T(8,128)(2,1)S(1)}, u32[]{:S(2)}, u32[]{:S(2)}) async-start(bf16[512,1,8,128]{3,2,1,0:T(8,128)(2,1)} %copy.42), calls=%async_computation.3 | async-start | bytes 2097152 | tf_op jit(solution)/shard_map/all_to_all | solution.py:82
where the time goes:
time: 247 us; the launch traced here: 246 us
  waiting for transfers between devices  145 us (59%)
  local copies, waits for them, and re-layouts  32.6 us (13%)
  starting transfers between devices  32.6 us (13%)
  matrix products  18 us (7%)
  other arithmetic  17.5 us (7%)
    all_to_all x1, waiting for transfers between devices, on_device(): lax.all_to_all(head_output, 'seq', split_axis=0, concat_axis=1, tiled=True)  23.7 us
    all_to_all x1, waiting for transfers between devices, on_device(): lax.all_to_all(split_queries, 'seq', split_axis=1, concat_axis=0, tiled=T...  22.8 us
    all_to_all x1, waiting for transfers between devices, on_device(): lax.all_to_all(split_keys, 'seq', split_axis=1, concat_axis=0, tiled=True)  22.3 us
    all_to_all x1, waiting for transfers between devices, on_device(): lax.all_to_all(split_dkey, 'seq', split_axis=1, concat_axis=0, tiled=True)  20.7 us
    all_to_all x1, waiting for transfers between devices, on_device(): lax.all_to_all(split_dquery, 'seq', split_axis=1, concat_axis=0, tiled=True)  20.6 us
    all_to_all x1, waiting for transfers between devices, on_device(): lax.all_to_all(head_tangent, 'seq', split_axis=0, concat_axis=1, tiled=True)  19.7 us
    sub x1, other arithmetic, one_block(): score_tangent - mean_tangent  14.4 us
    unnamed x10, local copies, waits for them, and re-layouts  11.6 us
  transfers between devices with their start and end apart: 8, of which 8 were waited for; matrix products, arithmetic and copies ran while one was open for 23% of the time, Pallas kernels for 0%

commit v1 on v0

v1 whole, which is shorter than its diff:
```python
import functools
import math

import jax
import jax.numpy as jnp
from jax import lax
from jax.experimental import pallas as pl
from jax.experimental.pallas import tpu as pltpu
from jax.sharding import PartitionSpec as P

HEADS = 32
HEAD = 128
ANYWHERE = pl.BlockSpec(memory_space=pl.ANY)


def chunk_sizes(count):
    sizes = []
    while count > 2:
        sizes.append(count // 2)
        count -= count // 2
    return sizes + [count]


def rounds_of(count):
    if count & (count - 1) == 0:
        return [[i ^ step for i in range(count)] for step in range(count - 1, 0, -1)]
    return [[(i + step) % count for i in range(count)] for step in range(1, count)]


def columns(start, width):
    return pl.ds(pl.multiple_of(start, HEAD), width)


def pack_kernel(count, width, starts, *refs):
    arrays, messages, sems = refs[:6], refs[6:6 + count], refs[6 + count]
    copies = []
    for m in range(count):
        for i in range(6):
            copies.append(
                pltpu.make_async_copy(
                    arrays[i].at[:, columns(starts[m], width)], messages[m].at[i], sems.at[m, i]
                )
            )
    for copy in copies:
        copy.start()
    for copy in copies:
        copy.wait()


def pack(arrays, starts, width):
    count = len(starts)
    rows = arrays[0].shape[0]
    message = jax.ShapeDtypeStruct((6, rows, width), arrays[0].dtype)
    return pl.pallas_call(
        functools.partial(pack_kernel, count, width),
        out_shape=[message] * count,
        in_specs=[pl.BlockSpec(memory_space=pltpu.SMEM)] + [ANYWHERE] * 6,
        out_specs=[ANYWHERE] * count,
        scratch_shapes=[pltpu.SemaphoreType.DMA((count, 6))],
        cost_estimate=pl.CostEstimate(
            flops=0, bytes_accessed=count * 6 * rows * width * 4, transcendentals=0
        ),
        name="pack",
    )(jnp.stack(starts).astype(jnp.int32), *arrays)


def place_kernel(count, width, starts, *refs):
    messages = refs[:count]
    outs = refs[-3:-1]
    sems = refs[-1]
    copies = []
    for m in range(count):
        for i in range(2):
            copies.append(
                pltpu.make_async_copy(
                    messages[m].at[i], outs[i].at[:, columns(starts[m], width)], sems.at[m, i]
                )
            )
    for copy in copies:
        copy.start()
    for copy in copies:
        copy.wait()


def place(outs, messages, starts, shape):
    count = len(messages)
    _, rows, width = messages[0].shape
    out = jax.ShapeDtypeStruct(shape, messages[0].dtype)
    return pl.pallas_call(
        functools.partial(place_kernel, count, width),
        out_shape=[out, out],
        in_specs=[pl.BlockSpec(memory_space=pltpu.SMEM)] + [ANYWHERE] * (count + len(outs)),
        out_specs=[ANYWHERE, ANYWHERE],
        scratch_shapes=[pltpu.SemaphoreType.DMA((count, 2))],
        input_output_aliases={1 + count + i: i for i in range(len(outs))},
        cost_estimate=pl.CostEstimate(
            flops=0, bytes_accessed=count * rows * width * 8, transcendentals=0
        ),
        name="place",
    )(jnp.stack(starts).astype(jnp.int32), *messages, *outs)


def attend_kernel(groups, start, *refs):
    own, messages = refs[:6], refs[6:6 + groups - 1]
    results = refs[6 + groups - 1:]
    del start

    def piece(which, group):
        return own[which][...] if group == 0 else messages[group - 1][which]

    def joined(which):
        return jnp.concatenate([piece(which, g) for g in range(groups)], axis=0)

    keys = joined(1)
    values = joined(2)
    both_keys = jnp.concatenate([keys, joined(4)], axis=1)
    both_values = jnp.concatenate([values, joined(5)], axis=1)
    width = keys.shape[1]
    scale = width ** -0.5
    across = (((1,), (1,)), ((), ()))
    for g in range(groups):
        queries = piece(0, g)
        paired = jnp.concatenate([piece(3, g), queries], axis=1)
        scores = lax.dot_general(queries, keys, across, preferred_element_type=jnp.float32)
        tangent = lax.dot_general(paired, both_keys, across, preferred_element_type=jnp.float32)
        row_max = jnp.max(scores, axis=1, keepdims=True)
        raised = jnp.exp2((scores - row_max) * (scale * math.log2(math.e)))
        exact = raised * (1.0 / jnp.sum(raised, axis=1, keepdims=True))
        weights = exact.astype(jnp.bfloat16)
        mean = jnp.sum(exact * tangent, axis=1, keepdims=True)
        weight_tangent = (exact * ((tangent - mean) * scale)).astype(jnp.bfloat16)
        sums = jnp.dot(weights, both_values, preferred_element_type=jnp.float32)
        moved = jnp.dot(weight_tangent, values, preferred_element_type=jnp.float32)
        results[g][0] = sums[:, :width].astype(jnp.bfloat16)
        results[g][1] = (sums[:, width:] + moved).astype(jnp.bfloat16)


def attend(arrays, messages, start, heads):
    groups = len(messages) + 1
    rows = arrays[0].shape[0]
    tokens = rows * groups
    own = pl.BlockSpec((rows, HEAD), lambda h, s: (0, s[0] + h))
    message = pl.BlockSpec((6, rows, HEAD), lambda h, s: (0, 0, h))
    result = pl.BlockSpec((2, rows, HEAD), lambda h, s: (0, 0, h))
    return pl.pallas_call(
        functools.partial(attend_kernel, groups),
        out_shape=[jax.ShapeDtypeStruct((2, rows, heads * HEAD), jnp.bfloat16)] * groups,
        grid_spec=pltpu.PrefetchScalarGridSpec(
            num_scalar_prefetch=1,
            grid=(heads,),
            in_specs=[own] * 6 + [message] * (groups - 1),
            out_specs=[result] * groups,
        ),
        compiler_params=pltpu.CompilerParams(vmem_limit_bytes=48 * 2**20),
        cost_estimate=pl.CostEstimate(
            flops=heads * 12 * tokens * tokens * HEAD,
            bytes_accessed=heads * 16 * tokens * HEAD,
            transcendentals=heads * tokens * tokens,
        ),
        name="attend",
    )((start // HEAD).astype(jnp.int32)[None], *arrays, *messages)


def on_device(*arrays):
    groups = lax.axis_size("seq")
    me = lax.axis_index("seq")
    span = arrays[0].shape[1] // groups
    sizes = chunk_sizes(span // HEAD)
    rounds = rounds_of(groups)
    to = [jnp.asarray(r, jnp.int32)[me] for r in rounds]
    outs = []
    base = 0
    sent = []
    for heads in sizes:
        width = heads * HEAD
        packed = pack(arrays, [t * span + base for t in to], width)
        received = [
            lax.ppermute(message, "seq", list(enumerate(r))) for message, r in zip(packed, rounds)
        ]
        sent.append((received, base, heads))
        base += width
    for received, base, heads in sent:
        own, *results = attend(arrays, received, me * span + base, heads)
        back = [
            lax.ppermute(message, "seq", [(b, a) for a, b in enumerate(r)])
            for message, r in zip(results, rounds)
        ]
        outs = place(
            outs, [own] + back, [me * span + base] + [t * span + base for t in to], arrays[0].shape
        )
    return tuple(outs)


def solution(mesh):
    spec = P(("dp", "seq"), None)
    return jax.shard_map(
        on_device, mesh=mesh, in_specs=(spec,) * 6, out_specs=(spec, spec), check_vma=False
    )
```

time: 247 us -> 326 us (1.32)
  Pallas kernels: 0 us -> 240 us
  waiting for transfers between devices: 145 us -> 18.7 us
  local copies, waits for them, and re-layouts: 32.6 us -> 10.5 us
  matrix products: 18 us -> 0 us
  starting transfers between devices: 32.6 us -> 50.1 us
  other arithmetic: 17.5 us -> 3.79 us
    pallas_call x0 -> x9, Pallas kernels: none -> 240 us  [the longest x3 149 us: pack(): pl.pallas_call(functools.partial(pack_kernel, count, width), out_shape=[m...]
    all_to_all x8 -> x0, waiting for transfers between devices: 145 us -> none  [the longest x1 23.7 us: on_device(): lax.all_to_all(head_output, 'seq', split_axis=0, concat_axis=1, tiled=True)]
    ppermute x0 -> x18, starting transfers between devices: none -> 50.1 us  [the longest x9 27 us: on_device(): lax.ppermute(message, 'seq', list(enumerate(r)))]
    all_to_all x8 -> x0, starting transfers between devices: 32.6 us -> none  [the longest x1 6.32 us: on_device(): lax.all_to_all(split_queries, 'seq', split_axis=1, concat_axis=0, tiled=T...]
    ppermute x0 -> x18, waiting for transfers between devices: none -> 18.7 us  [the longest x9 14.4 us: on_device(): lax.ppermute(message, 'seq', list(enumerate(r)))]
    sub x1 -> x0, other arithmetic: 14.4 us -> none  [one_block(): score_tangent - mean_tangent]
    reshape x8 -> x0, local copies, waits for them, and re-layouts: 13.3 us -> none  [the longest x1 2.27 us: on_device(): split_dkey = key_tangent.reshape(local_rows, groups, per_group, HEAD)]
    dot_general x3 -> x0, matrix products: 13.1 us -> none  [the longest x1 4.91 us: one_block(): jnp.einsum('hqk,khd->qhd', stacked, values_joined, preferred_element_type...]
  transfers between devices with their start and end apart: 8 -> 18, of which waited for: 8 -> 3; matrix products, arithmetic and copies ran while one was open for 23% -> 1% of each run, Pallas kernels for 0% -> 46%
where the time goes in v1:
time: 326 us
  Pallas kernels  240 us (74%)
  starting transfers between devices  50.1 us (15%)
  waiting for transfers between devices  18.7 us (6%)
  local copies, waits for them, and re-layouts  10.5 us (3%)
  other arithmetic  3.79 us (1%)
    pallas_call x3, Pallas kernels, pack(): pl.pallas_call(functools.partial(pack_kernel, count, width), out_shape=[m...  149 us
    pallas_call x3, Pallas kernels, place(): pl.pallas_call(functools.partial(place_kernel, count, width), out_shape=[...  69 us
    ppermute x9, starting transfers between devices, on_device(): lax.ppermute(message, 'seq', list(enumerate(r)))  27 us
    ppermute x9, starting transfers between devices, on_device(): lax.ppermute(message, 'seq', [(b, a) for a, b in enumerate(r)])  23.2 us
    pallas_call x3, Pallas kernels, attend(): pl.pallas_call(functools.partial(attend_kernel, groups), out_shape=[jax.S...  22.2 us
    ppermute x9, waiting for transfers between devices, on_device(): lax.ppermute(message, 'seq', list(enumerate(r)))  14.4 us
    unnamed x40, local copies, waits for them, and re-layouts  8.73 us
  transfers between devices with their start and end apart: 18, of which 3 were waited for; matrix products, arithmetic and copies ran while one was open for 1% of the time, Pallas kernels for 46%

profile of v1, /device:TPU:0, one launch (start us, length us, event | category | flops | bytes accessed | tf_op | source)
XLA Modules:
  0.0 325.9 jit_solution(2111355977453388362)
XLA Ops:
  0.6 0.6 copy-done.19
  1.3 0.6 dynamic_slice.9
  1.9 0.1 copy-done.18
  1.9 0.6 dynamic_slice.10
  3.9 0.6 dynamic_slice.11
  5.1 0.7 pad_add_fusion.5.starts
  5.8 73.4 %pack.5 = (bf16[6,128,512]{2,1,0:T(8,128)(2,1)}, bf16[6,128,512]{2,1,0:T(8,128)(2,1)}, bf16[6,128,512]{2,1,0:T(8,128)(2,1)}) custom-call(s32[3]{0:T(128)} %pad_add_fusion.5.starts, bf16[128,4096]{1,0:T(8,128)(2,1)} %refs_0_.11, bf16[128,4096]{1,0:T(8,128)(2,1)} %refs_1_.11, bf16[128,4096]{1,0:T(8,128)(2,1)} %refs_2_.11, bf16[128,4096]{1,0:T(8,128)(2,1)} %refs_3_.11, ...), custom_call_target="tpu_custom_call" | custom-call | bytes 4718592 | tf_op jit(solution)/shard_map/pack/pallas_call | solution.py:54
  79.2 5.1 %collective-permute-start.12 = (bf16[6,128,512]{2,1,0:T(8,128)(2,1)}, bf16[6,128,512]{2,1,0:T(8,128)(2,1)S(1)}, u32[]{:S(2)}, u32[]{:S(2)}) collective-permute-start(bf16[6,128,512]{2,1,0:T(8,128)(2,1)} %get-tuple-element.41), channel_id=1, source_target_pairs={{0,3},{1,2},{2,1},{3,0},{4,7},{5,6},{6,5},{7,4},{8,11},{9,10},{10,... | collective-permute-start | bytes 2359304 | tf_op jit(solution)/shard_map/ppermute | solution.py:178
  84.3 0.6 collective-permute-start.14
  84.9 0.7 pad_add_fusion.3.starts
  85.6 37.7 %pack.4 = (bf16[6,128,256]{2,1,0:T(8,128)(2,1)}, bf16[6,128,256]{2,1,0:T(8,128)(2,1)}, bf16[6,128,256]{2,1,0:T(8,128)(2,1)}) custom-call(s32[3]{0:T(128)} %pad_add_fusion.3.starts, bf16[128,4096]{1,0:T(8,128)(2,1)} %refs_0_.11, bf16[128,4096]{1,0:T(8,128)(2,1)} %refs_1_.11, bf16[128,4096]{1,0:T(8,128)(2,1)} %refs_2_.11, bf16[128,4096]{1,0:T(8,128)(2,1)} %refs_3_.11, ...), custom_call_target="tpu_custom_call" | custom-call | bytes 2359296 | tf_op jit(solution)/shard_map/pack/pallas_call | solution.py:54
  123.3 3.8 %collective-permute-start.6 = (bf16[6,128,256]{2,1,0:T(8,128)(2,1)}, bf16[6,128,256]{2,1,0:T(8,128)(2,1)S(1)}, u32[]{:S(2)}, u32[]{:S(2)}) collective-permute-start(bf16[6,128,256]{2,1,0:T(8,128)(2,1)} %get-tuple-element.34), channel_id=1, source_target_pairs={{0,3},{1,2},{2,1},{3,0},{4,7},{5,6},{6,5},{7,4},{8,11},{9,10},{10,... | collective-permute-start | bytes 1179656 | tf_op jit(solution)/shard_map/ppermute | solution.py:178
  127.1 0.7 pad_add_fusion.1.starts
  127.7 37.8 %pack.3 = (bf16[6,128,256]{2,1,0:T(8,128)(2,1)}, bf16[6,128,256]{2,1,0:T(8,128)(2,1)}, bf16[6,128,256]{2,1,0:T(8,128)(2,1)}) custom-call(s32[3]{0:T(128)} %pad_add_fusion.1.starts, bf16[128,4096]{1,0:T(8,128)(2,1)} %refs_0_.11, bf16[128,4096]{1,0:T(8,128)(2,1)} %refs_1_.11, bf16[128,4096]{1,0:T(8,128)(2,1)} %refs_2_.11, bf16[128,4096]{1,0:T(8,128)(2,1)} %refs_3_.11, ...), custom_call_target="tpu_custom_call" | custom-call | bytes 2359296 | tf_op jit(solution)/shard_map/pack/pallas_call | solution.py:54
  165.6 0.8 copy-done.7
  166.3 13.0 %collective-permute-start.8 = (bf16[6,128,256]{2,1,0:T(8,128)(2,1)}, bf16[6,128,256]{2,1,0:T(8,128)(2,1)}, u32[]{:S(2)}, u32[]{:S(2)}) collective-permute-start(bf16[6,128,256]{2,1,0:T(8,128)(2,1)} %get-tuple-element.36), channel_id=1, source_target_pairs={{0,1},{1,0},{2,3},{3,2},{4,5},{5,4},{6,7},{7,6},{8,9},{9,8},{10,11... | collective-permute-start | bytes 1179656 | tf_op jit(solution)/shard_map/ppermute | solution.py:178
  179.3 0.9 copy-done.5
  180.2 2.7 collective-permute-start
  182.9 1.7 collective-permute-start.2
  184.6 1.1 copy-done.6
  185.7 10.4 %attend.5 = (bf16[2,128,512]{2,1,0:T(8,128)(2,1)S(1)}, bf16[2,128,512]{2,1,0:T(8,128)(2,1)}, bf16[2,128,512]{2,1,0:T(8,128)(2,1)}, bf16[2,128,512]{2,1,0:T(8,128)(2,1)}) custom-call(s32[1]{0:T(128)} %bitcast.5.start, bf16[128,4096]{1,0:T(8,128)(2,1)S(1)} %copy-done, bf16[128,4096]{1,0:T(8,128)(2,1)S(1)} %copy-done.1, bf16[128,4096]{1,0:T(8,128)(2,1)} %refs_2_.11, ...), custom_call_target="tpu_custom_call" | custom-call | flops 1610612736 | bytes 4194304 | tf_op jit(solution)/shard_map/attend/pallas_call | solution.py:145
  196.1 0.7 copy-done.9
  196.8 2.7 collective-permute-start.15
  199.5 3.0 collective-permute-done.8.refs_8_
  202.5 0.6 collective-permute-start.16
  203.1 9.9 %collective-permute-start.17 = (bf16[2,128,512]{2,1,0:T(8,128)(2,1)}, bf16[2,128,512]{2,1,0:T(8,128)(2,1)}, u32[]{:S(2)}, u32[]{:S(2)}) collective-permute-start(bf16[2,128,512]{2,1,0:T(8,128)(2,1)} %get-tuple-element.47), channel_id=1, source_target_pairs={{1,0},{0,1},{3,2},{2,3},{5,4},{4,5},{7,6},{6,7},{9,8},{8,9},{11,10... | collective-permute-start | bytes 786440 | tf_op jit(solution)/shard_map/ppermute | solution.py:185
  212.9 5.9 %attend.4 = (bf16[2,128,256]{2,1,0:T(8,128)(2,1)S(1)}, bf16[2,128,256]{2,1,0:T(8,128)(2,1)}, bf16[2,128,256]{2,1,0:T(8,128)(2,1)}, bf16[2,128,256]{2,1,0:T(8,128)(2,1)S(1)}) custom-call(s32[1]{0:T(128)} %bitcast.3.start, bf16[128,4096]{1,0:T(8,128)(2,1)S(1)} %copy-done, bf16[128,4096]{1,0:T(8,128)(2,1)S(1)} %copy-done.1, bf16[128,4096]{1,0:T(8,128)(2,1)S(1)} %copy-done.2, ...), custom_call_target="tpu_custom_call" | custom-call | flops 805306368 | bytes 2097152 | tf_op jit(solution)/shard_map/attend/pallas_call | solution.py:145
  218.8 0.6 copy-done.10
  219.5 0.6 copy-done.12
  220.1 11.4 %collective-permute-done.1.refs_7_ = bf16[6,128,256]{2,1,0:T(8,128)(2,1)} collective-permute-done((bf16[6,128,256]{2,1,0:T(8,128)(2,1)}, bf16[6,128,256]{2,1,0:T(8,128)(2,1)}, u32[]{:S(2)}, u32[]{:S(2)}) %collective-permute-start.1) | collective-permute-done | bytes 393248 | tf_op jit(solution)/shard_map/ppermute | solution.py:178
  231.5 0.7 pad_add_fusion.4.starts
  232.2 3.2 collective-permute-start.11
  235.4 1.2 copy-done.4
  236.6 5.9 %attend.3 = (bf16[2,128,256]{2,1,0:T(8,128)(2,1)S(1)}, bf16[2,128,256]{2,1,0:T(8,128)(2,1)}, bf16[2,128,256]{2,1,0:T(8,128)(2,1)}, bf16[2,128,256]{2,1,0:T(8,128)(2,1)}) custom-call(s32[1]{0:T(128)} %bitcast.1.start, bf16[128,4096]{1,0:T(8,128)(2,1)S(1)} %copy-done, bf16[128,4096]{1,0:T(8,128)(2,1)S(1)} %copy-done.1, bf16[128,4096]{1,0:T(8,128)(2,1)S(1)} %copy-done.2, ...), custom_call_target="tpu_custom_call" | custom-call | flops 805306368 | bytes 2097152 | tf_op jit(solution)/shard_map/attend/pallas_call | solution.py:145
  242.5 0.7 copy-done.11
  243.2 4.2 %collective-permute-done.10.refs_2_ = bf16[2,128,256]{2,1,0:T(8,128)(2,1)} collective-permute-done((bf16[2,128,256]{2,1,0:T(8,128)(2,1)}, bf16[2,128,256]{2,1,0:T(8,128)(2,1)}, u32[]{:S(2)}, u32[]{:S(2)}) %collective-permute-start.10) | collective-permute-done | bytes 131104 | tf_op jit(solution)/shard_map/ppermute | solution.py:185
  247.4 2.5 collective-permute-start.9
  249.9 1.3 collective-permute-start.3
  251.2 3.0 collective-permute-start.5
  254.3 0.6 pad_add_fusion.2.starts
  254.9 0.6 pad_add_fusion.starts
  255.4 33.6 %place.3 = (bf16[128,4096]{1,0:T(8,128)(2,1)}, bf16[128,4096]{1,0:T(8,128)(2,1)}) custom-call(s32[4]{0:T(128)} %pad_add_fusion.4.starts, bf16[2,128,512]{2,1,0:T(8,128)(2,1)} %copy-done.9, bf16[2,128,512]{2,1,0:T(8,128)(2,1)} %collective-permute-done.15.refs_1_, bf16[2,128,512]{2,1,0:T(8,128)(2,1)} %collective-permute-done.16.refs_2_, ...), custom_call_target="tpu_custom_call" | custom-call | bytes 2097152 | tf_op jit(solution)/shard_map/place/pallas_call | solution.py:89
  289.1 0.6 copy-done.15
  289.7 17.7 %place.4 = (bf16[128,4096]{1,0:T(8,128)(2,1)}, bf16[128,4096]{1,0:T(8,128)(2,1)}) custom-call(s32[4]{0:T(128)} %pad_add_fusion.2.starts, bf16[2,128,256]{2,1,0:T(8,128)(2,1)} %copy-done.10, bf16[2,128,256]{2,1,0:T(8,128)(2,1)} %copy-done.15, bf16[2,128,256]{2,1,0:T(8,128)(2,1)} %collective-permute-done.10.refs_2_, ...), custom_call_target="tpu_custom_call", output_to_operand_aliasing={{0}: (5, {}), {1}: (6, {})} | custom-call | bytes 1048576 | tf_op jit(solution)/shard_map/place/pallas_call | solution.py:89
  307.5 0.6 copy-done.13
  308.1 0.0 copy-done.14
  308.1 0.1 copy-done.16
  308.2 17.7 %place.5 = (bf16[128,4096]{1,0:T(8,128)(2,1)}, bf16[128,4096]{1,0:T(8,128)(2,1)}) custom-call(s32[4]{0:T(128)} %pad_add_fusion.starts, bf16[2,128,256]{2,1,0:T(8,128)(2,1)} %copy-done.11, bf16[2,128,256]{2,1,0:T(8,128)(2,1)} %copy-done.13, bf16[2,128,256]{2,1,0:T(8,128)(2,1)} %copy-done.14, ...), custom_call_target="tpu_custom_call", output_to_operand_aliasing={{0}: (5, {}), {1}: (6, {})} | custom-call | bytes 1048576 | tf_op jit(solution)/shard_map/place/pallas_call | solution.py:89
  (46 shorter events, 0.1 us)
Async XLA Ops:
  0.6 0.7 copy-start.19
  1.3 0.7 copy-start.18
  3.2 0.7 copy-start.17
  79.2 100.2 %collective-permute-start.12 = (bf16[6,128,512]{2,1,0:T(8,128)(2,1)}, bf16[6,128,512]{2,1,0:T(8,128)(2,1)S(1)}, u32[]{:S(2)}, u32[]{:S(2)}) collective-permute-start(bf16[6,128,512]{2,1,0:T(8,128)(2,1)} %get-tuple-element.41), channel_id=1, source_target_pairs={{0,3},{1,2},{2,1},{3,0},{4,7},{5,6},{6,5},{7,4},{8,11},{9,10},{10,... | collective-permute-start | bytes 2359304 | tf_op jit(solution)/shard_map/ppermute | solution.py:178
  84.3 98.6 %collective-permute-start.13 = (bf16[6,128,512]{2,1,0:T(8,128)(2,1)}, bf16[6,128,512]{2,1,0:T(8,128)(2,1)}, u32[]{:S(2)}, u32[]{:S(2)}) collective-permute-start(bf16[6,128,512]{2,1,0:T(8,128)(2,1)} %get-tuple-element.42), channel_id=1, source_target_pairs={{0,2},{1,3},{2,0},{3,1},{4,6},{5,7},{6,4},{7,5},{8,10},{9,11},{10,... | collective-permute-start | bytes 2359304 | tf_op jit(solution)/shard_map/ppermute | solution.py:178
  84.3 98.6 %collective-permute-start.14 = (bf16[6,128,512]{2,1,0:T(8,128)(2,1)}, bf16[6,128,512]{2,1,0:T(8,128)(2,1)}, u32[]{:S(2)}, u32[]{:S(2)}) collective-permute-start(bf16[6,128,512]{2,1,0:T(8,128)(2,1)} %get-tuple-element.43), channel_id=1, source_target_pairs={{0,1},{1,0},{2,3},{3,2},{4,5},{5,4},{6,7},{7,6},{8,9},{9,8},{10,11... | collective-permute-start | bytes 2359304 | tf_op jit(solution)/shard_map/ppermute | solution.py:178
  123.3 42.3 %collective-permute-start.6 = (bf16[6,128,256]{2,1,0:T(8,128)(2,1)}, bf16[6,128,256]{2,1,0:T(8,128)(2,1)S(1)}, u32[]{:S(2)}, u32[]{:S(2)}) collective-permute-start(bf16[6,128,256]{2,1,0:T(8,128)(2,1)} %get-tuple-element.34), channel_id=1, source_target_pairs={{0,3},{1,2},{2,1},{3,0},{4,7},{5,6},{6,5},{7,4},{8,11},{9,10},{10,... | collective-permute-start | bytes 1179656 | tf_op jit(solution)/shard_map/ppermute | solution.py:178
  127.1 69.7 %collective-permute-start.7 = (bf16[6,128,256]{2,1,0:T(8,128)(2,1)}, bf16[6,128,256]{2,1,0:T(8,128)(2,1)}, u32[]{:S(2)}, u32[]{:S(2)}) collective-permute-start(bf16[6,128,256]{2,1,0:T(8,128)(2,1)} %get-tuple-element.35), channel_id=1, source_target_pairs={{0,2},{1,3},{2,0},{3,1},{4,6},{5,7},{6,4},{7,5},{8,10},{9,11},{10,... | collective-permute-start | bytes 1179656 | tf_op jit(solution)/shard_map/ppermute | solution.py:178
  127.7 56.9 %copy-start = (bf16[128,4096]{1,0:T(8,128)(2,1)S(1)}, bf16[128,4096]{1,0:T(8,128)(2,1)}, u32[]{:S(2)}) copy-start(bf16[128,4096]{1,0:T(8,128)(2,1)} %refs_0_.11) | copy-start | bytes 3145732
  127.7 56.9 %copy-start.1 = (bf16[128,4096]{1,0:T(8,128)(2,1)S(1)}, bf16[128,4096]{1,0:T(8,128)(2,1)}, u32[]{:S(2)}) copy-start(bf16[128,4096]{1,0:T(8,128)(2,1)} %refs_1_.11) | copy-start | bytes 3145732
  165.5 0.8 copy-start.7
  166.3 36.2 %collective-permute-start.8 = (bf16[6,128,256]{2,1,0:T(8,128)(2,1)}, bf16[6,128,256]{2,1,0:T(8,128)(2,1)}, u32[]{:S(2)}, u32[]{:S(2)}) collective-permute-start(bf16[6,128,256]{2,1,0:T(8,128)(2,1)} %get-tuple-element.36), channel_id=1, source_target_pairs={{0,1},{1,0},{2,3},{3,2},{4,5},{5,4},{6,7},{7,6},{8,9},{9,8},{10,11... | collective-permute-start | bytes 1179656 | tf_op jit(solution)/shard_map/ppermute | solution.py:178
  179.3 0.9 copy-start.5
  180.2 22.9 %collective-permute-start = (bf16[6,128,256]{2,1,0:T(8,128)(2,1)}, bf16[6,128,256]{2,1,0:T(8,128)(2,1)S(1)}, u32[]{:S(2)}, u32[]{:S(2)}) collective-permute-start(bf16[6,128,256]{2,1,0:T(8,128)(2,1)} %get-tuple-element.27), channel_id=1, source_target_pairs={{0,3},{1,2},{2,1},{3,0},{4,7},{5,6},{6,5},{7,4},{8,11},{9,10},{10,... | collective-permute-start | bytes 1179656 | tf_op jit(solution)/shard_map/ppermute | solution.py:178
  182.9 48.6 %collective-permute-start.1 = (bf16[6,128,256]{2,1,0:T(8,128)(2,1)}, bf16[6,128,256]{2,1,0:T(8,128)(2,1)}, u32[]{:S(2)}, u32[]{:S(2)}) collective-permute-start(bf16[6,128,256]{2,1,0:T(8,128)(2,1)} %get-tuple-element.28), channel_id=1, source_target_pairs={{0,2},{1,3},{2,0},{3,1},{4,6},{5,7},{6,4},{7,5},{8,10},{9,11},{10,... | collective-permute-start | bytes 1179656 | tf_op jit(solution)/shard_map/ppermute | solution.py:178
  182.9 49.3 %collective-permute-start.2 = (bf16[6,128,256]{2,1,0:T(8,128)(2,1)}, bf16[6,128,256]{2,1,0:T(8,128)(2,1)}, u32[]{:S(2)}, u32[]{:S(2)}) collective-permute-start(bf16[6,128,256]{2,1,0:T(8,128)(2,1)} %get-tuple-element.29), channel_id=1, source_target_pairs={{0,1},{1,0},{2,3},{3,2},{4,5},{5,4},{6,7},{7,6},{8,9},{9,8},{10,11... | collective-permute-start | bytes 1179656 | tf_op jit(solution)/shard_map/ppermute | solution.py:178
  184.6 1.1 copy-start.6
  185.7 27.2 %copy-start.2 = (bf16[128,4096]{1,0:T(8,128)(2,1)S(1)}, bf16[128,4096]{1,0:T(8,128)(2,1)}, u32[]{:S(2)}) copy-start(bf16[128,4096]{1,0:T(8,128)(2,1)} %refs_2_.11) | copy-start | bytes 3145732
  185.7 27.2 %copy-start.3 = (bf16[128,4096]{1,0:T(8,128)(2,1)S(1)}, bf16[128,4096]{1,0:T(8,128)(2,1)}, u32[]{:S(2)}) copy-start(bf16[128,4096]{1,0:T(8,128)(2,1)} %refs_3_.11) | copy-start | bytes 3145732
  185.7 27.2 %copy-start.8 = (bf16[6,128,256]{2,1,0:T(8,128)(2,1)S(1)}, bf16[6,128,256]{2,1,0:T(8,128)(2,1)}, u32[]{:S(2)}) copy-start(bf16[6,128,256]{2,1,0:T(8,128)(2,1)} %copy-done.7) | copy-start | bytes 1179652
  196.1 0.7 copy-start.9
  196.8 53.1 %collective-permute-start.15 = (bf16[2,128,512]{2,1,0:T(8,128)(2,1)}, bf16[2,128,512]{2,1,0:T(8,128)(2,1)}, u32[]{:S(2)}, u32[]{:S(2)}) collective-permute-start(bf16[2,128,512]{2,1,0:T(8,128)(2,1)} %get-tuple-element.45), channel_id=1, source_target_pairs={{3,0},{2,1},{1,2},{0,3},{7,4},{6,5},{5,6},{4,7},{11,8},{10,9},{9,1... | collective-permute-start | bytes 786440 | tf_op jit(solution)/shard_map/ppermute | solution.py:185
  202.5 48.7 %collective-permute-start.16 = (bf16[2,128,512]{2,1,0:T(8,128)(2,1)}, bf16[2,128,512]{2,1,0:T(8,128)(2,1)}, u32[]{:S(2)}, u32[]{:S(2)}) collective-permute-start(bf16[2,128,512]{2,1,0:T(8,128)(2,1)} %get-tuple-element.46), channel_id=1, source_target_pairs={{2,0},{3,1},{0,2},{1,3},{6,4},{7,5},{4,6},{5,7},{10,8},{11,9},{8,1... | collective-permute-start | bytes 786440 | tf_op jit(solution)/shard_map/ppermute | solution.py:185
  203.1 48.2 %collective-permute-start.17 = (bf16[2,128,512]{2,1,0:T(8,128)(2,1)}, bf16[2,128,512]{2,1,0:T(8,128)(2,1)}, u32[]{:S(2)}, u32[]{:S(2)}) collective-permute-start(bf16[2,128,512]{2,1,0:T(8,128)(2,1)} %get-tuple-element.47), channel_id=1, source_target_pairs={{1,0},{0,1},{3,2},{2,3},{5,4},{4,5},{7,6},{6,7},{9,8},{8,9},{11,10... | collective-permute-start | bytes 786440 | tf_op jit(solution)/shard_map/ppermute | solution.py:185
  218.8 0.7 copy-start.10
  219.5 0.6 copy-start.12
  231.5 15.9 %collective-permute-start.10 = (bf16[2,128,256]{2,1,0:T(8,128)(2,1)}, bf16[2,128,256]{2,1,0:T(8,128)(2,1)}, u32[]{:S(2)}, u32[]{:S(2)}) collective-permute-start(bf16[2,128,256]{2,1,0:T(8,128)(2,1)} %get-tuple-element.39), channel_id=1, source_target_pairs={{2,0},{3,1},{0,2},{1,3},{6,4},{7,5},{4,6},{5,7},{10,8},{11,9},{8,1... | collective-permute-start | bytes 393224 | tf_op jit(solution)/shard_map/ppermute | solution.py:185
  232.2 56.9 %collective-permute-start.11 = (bf16[2,128,256]{2,1,0:T(8,128)(2,1)}, bf16[2,128,256]{2,1,0:T(8,128)(2,1)}, u32[]{:S(2)}, u32[]{:S(2)}) collective-permute-start(bf16[2,128,256]{2,1,0:T(8,128)(2,1)} %copy-done.12), channel_id=1, source_target_pairs={{1,0},{0,1},{3,2},{2,3},{5,4},{4,5},{7,6},{6,7},{9,8},{8,9},{11,10... | collective-permute-start | bytes 393224 | tf_op jit(solution)/shard_map/ppermute | solution.py:185
  235.4 1.2 copy-start.4
  242.5 0.7 copy-start.11
  247.4 41.7 %collective-permute-start.9 = (bf16[2,128,256]{2,1,0:T(8,128)(2,1)}, bf16[2,128,256]{2,1,0:T(8,128)(2,1)S(1)}, u32[]{:S(2)}, u32[]{:S(2)}) collective-permute-start(bf16[2,128,256]{2,1,0:T(8,128)(2,1)} %get-tuple-element.38), channel_id=1, source_target_pairs={{3,0},{2,1},{1,2},{0,3},{7,4},{6,5},{5,6},{4,7},{11,8},{10,9},{9,1... | collective-permute-start | bytes 393224 | tf_op jit(solution)/shard_map/ppermute | solution.py:185
  249.9 57.5 %collective-permute-start.3 = (bf16[2,128,256]{2,1,0:T(8,128)(2,1)}, bf16[2,128,256]{2,1,0:T(8,128)(2,1)S(1)}, u32[]{:S(2)}, u32[]{:S(2)}) collective-permute-start(bf16[2,128,256]{2,1,0:T(8,128)(2,1)} %get-tuple-element.31), channel_id=1, source_target_pairs={{3,0},{2,1},{1,2},{0,3},{7,4},{6,5},{5,6},{4,7},{11,8},{10,9},{9,1... | collective-permute-start | bytes 393224 | tf_op jit(solution)/shard_map/ppermute | solution.py:185
  251.2 56.2 %collective-permute-start.4 = (bf16[2,128,256]{2,1,0:T(8,128)(2,1)}, bf16[2,128,256]{2,1,0:T(8,128)(2,1)S(1)}, u32[]{:S(2)}, u32[]{:S(2)}) collective-permute-start(bf16[2,128,256]{2,1,0:T(8,128)(2,1)} %get-tuple-element.32), channel_id=1, source_target_pairs={{2,0},{3,1},{0,2},{1,3},{6,4},{7,5},{4,6},{5,7},{10,8},{11,9},{8,1... | collective-permute-start | bytes 393224 | tf_op jit(solution)/shard_map/ppermute | solution.py:185
  251.2 56.2 %collective-permute-start.5 = (bf16[2,128,256]{2,1,0:T(8,128)(2,1)}, bf16[2,128,256]{2,1,0:T(8,128)(2,1)S(1)}, u32[]{:S(2)}, u32[]{:S(2)}) collective-permute-start(bf16[2,128,256]{2,1,0:T(8,128)(2,1)} %get-tuple-element.33), channel_id=1, source_target_pairs={{1,0},{0,1},{3,2},{2,3},{5,4},{4,5},{7,6},{6,7},{9,8},{8,9},{11,10... | collective-permute-start | bytes 393224 | tf_op jit(solution)/shard_map/ppermute | solution.py:185
  289.0 0.6 copy-start.15
  307.4 0.6 copy-start.13
  307.4 0.7 copy-start.14
  307.5 0.7 copy-start.16

commit v2 on v1

v2 whole, which is shorter than its diff:
```python
import functools
import math

import jax
import jax.numpy as jnp
from jax import lax
from jax.experimental import pallas as pl
from jax.experimental.pallas import tpu as pltpu
from jax.sharding import PartitionSpec as P

HEAD = 128
ANYWHERE = pl.BlockSpec(memory_space=pl.ANY)
WHOLE = pl.BlockSpec(memory_space=pltpu.VMEM)


def chunk_sizes(count):
    last = max(1, count // 4)
    return [count - last, last] if count > 1 else [count]


def rounds_of(count):
    if count & (count - 1) == 0:
        return [
            (lambda me, step=step: me ^ step, [i ^ step for i in range(count)])
            for step in range(count - 1, 0, -1)
        ]
    return [
        (lambda me, step=step: lax.rem(me + step, count), [(i + step) % count for i in range(count)])
        for step in range(1, count)
    ]


def own_group(me):
    return me


def columns(group, span, base, width):
    start = group(lax.axis_index("seq")) * span + base
    return pl.ds(pl.multiple_of(start, HEAD), width)


def run(copies):
    for copy in copies:
        copy.start()
    for copy in copies:
        copy.wait()


def pack_kernel(groups, span, base, width, *refs):
    arrays, messages, sems = refs[:6], refs[-1 - len(groups):-1], refs[-1]
    run(
        [
            pltpu.make_async_copy(
                arrays[i].at[:, columns(group, span, base, width)],
                messages[m].at[i],
                sems.at[m, i],
            )
            for m, group in enumerate(groups)
            for i in range(6)
        ]
    )


def pack(arrays, groups, span, base, width, after=()):
    count = len(groups)
    rows = arrays[0].shape[0]
    message = jax.ShapeDtypeStruct((6, rows, width), arrays[0].dtype)
    return pl.pallas_call(
        functools.partial(pack_kernel, groups, span, base, width),
        out_shape=[message] * count,
        in_specs=[ANYWHERE] * (6 + len(after)),
        out_specs=[WHOLE] * count,
        scratch_shapes=[pltpu.SemaphoreType.DMA((count, 6))],
        cost_estimate=pl.CostEstimate(
            flops=0, bytes_accessed=count * 24 * rows * width, transcendentals=0
        ),
        name="pack",
    )(*arrays, *after)


def place_kernel(groups, span, base, width, *refs):
    count = len(groups)
    messages, outs, sems = refs[:count], refs[-3:-1], refs[-1]
    run(
        [
            pltpu.make_async_copy(
                messages[m].at[i],
                outs[i].at[:, columns(group, span, base, width)],
                sems.at[m, i],
            )
            for m, group in enumerate(groups)
            for i in range(2)
        ]
    )


def place(outs, messages, groups, span, base, shape):
    count = len(messages)
    _, rows, width = messages[0].shape
    out = jax.ShapeDtypeStruct(shape, messages[0].dtype)
    return pl.pallas_call(
        functools.partial(place_kernel, groups, span, base, width),
        out_shape=[out, out],
        in_specs=[WHOLE] * count + [ANYWHERE] * len(outs),
        out_specs=[ANYWHERE, ANYWHERE],
        scratch_shapes=[pltpu.SemaphoreType.DMA((count, 2))],
        input_output_aliases={count + i: i for i in range(len(outs))},
        cost_estimate=pl.CostEstimate(
            flops=0, bytes_accessed=count * rows * width * 8, transcendentals=0
        ),
        name="place",
    )(*messages, *outs)


def attend_kernel(groups, *refs):
    messages, results = refs[:groups], refs[groups:]

    def joined(which):
        return jnp.concatenate([message[which] for message in messages], axis=0)

    keys = joined(1)
    values = joined(2)
    both_keys = jnp.concatenate([keys, joined(4)], axis=1)
    both_values = jnp.concatenate([values, joined(5)], axis=1)
    width = keys.shape[1]
    scale = width ** -0.5
    across = (((1,), (1,)), ((), ()))
    for message, result in zip(messages, results):
        queries = message[0]
        paired = jnp.concatenate([message[3], queries], axis=1)
        scores = lax.dot_general(queries, keys, across, preferred_element_type=jnp.float32)
        tangent = lax.dot_general(paired, both_keys, across, preferred_element_type=jnp.float32)
        row_max = jnp.max(scores, axis=1, keepdims=True)
        raised = jnp.exp2((scores - row_max) * (scale * math.log2(math.e)))
        exact = raised * (1.0 / jnp.sum(raised, axis=1, keepdims=True))
        weights = exact.astype(jnp.bfloat16)
        mean = jnp.sum(exact * tangent, axis=1, keepdims=True)
        weight_tangent = (exact * ((tangent - mean) * scale)).astype(jnp.bfloat16)
        sums = jnp.dot(weights, both_values, preferred_element_type=jnp.float32)
        moved = jnp.dot(weight_tangent, values, preferred_element_type=jnp.float32)
        result[0] = sums[:, :width].astype(jnp.bfloat16)
        result[1] = (sums[:, width:] + moved).astype(jnp.bfloat16)


def attend(messages):
    groups = len(messages)
    _, rows, width = messages[0].shape
    heads = width // HEAD
    tokens = rows * groups
    return pl.pallas_call(
        functools.partial(attend_kernel, groups),
        out_shape=[jax.ShapeDtypeStruct((2, rows, width), jnp.bfloat16)] * groups,
        grid=(heads,),
        in_specs=[pl.BlockSpec((6, rows, HEAD), lambda h: (0, 0, h))] * groups,
        out_specs=[pl.BlockSpec((2, rows, HEAD), lambda h: (0, 0, h))] * groups,
        compiler_params=pltpu.CompilerParams(vmem_limit_bytes=48 * 2**20),
        cost_estimate=pl.CostEstimate(
            flops=heads * 12 * tokens * tokens * HEAD,
            bytes_accessed=heads * 16 * tokens * HEAD,
            transcendentals=heads * tokens * tokens,
        ),
        name="attend",
    )(*messages)


def on_device(*arrays):
    count = lax.axis_size("seq")
    shape = arrays[0].shape
    span = shape[1] // count
    rounds = rounds_of(count)
    groups = [group for group, _ in rounds]

    def there(message, r):
        return lax.ppermute(message, "seq", list(enumerate(rounds[r][1])))

    def back(message, r):
        return lax.ppermute(message, "seq", [(b, a) for a, b in enumerate(rounds[r][1])])

    chunks = []
    base = 0
    for heads in chunk_sizes(span // HEAD):
        chunks.append((base, heads * HEAD))
        base += heads * HEAD
    received = []
    for base, width in chunks:
        first = pack(arrays, groups[:1], span, base, width)
        rest = pack(arrays, groups[1:], span, base, width)
        own = pack(arrays, [own_group], span, base, width)
        received.append([*own, *(there(m, r) for r, m in enumerate([*first, *rest]))])
    outs = ()
    for (base, width), messages in zip(chunks, received):
        own, *results = attend(messages)
        returned = [back(m, r) for r, m in enumerate(results)]
        outs = place(outs, [own], [own_group], span, base, shape)
        outs = place(outs, returned, groups, span, base, shape)
    return tuple(outs)


def solution(mesh):
    spec = P(("dp", "seq"), None)
    return jax.shard_map(
        on_device, mesh=mesh, in_specs=(spec,) * 6, out_specs=(spec, spec), check_vma=False
    )
```

time: 326 us -> 194 us (0.60)
  Pallas kernels: 240 us -> 41.1 us
  waiting for transfers between devices: 18.7 us -> 87.6 us
  starting transfers between devices: 50.1 us -> 59.7 us
  local copies, waits for them, and re-layouts: 10.5 us -> 3.99 us
  other arithmetic: 3.79 us -> 0 us
    pallas_call x6 -> x10, Pallas kernels: 218 us -> 21.5 us  [the longest x6 14 us: pack(): pl.pallas_call(functools.partial(pack_kernel, groups, span, base, width),...]
    ppermute x18 -> x12, waiting for transfers between devices: 18.7 us -> 87.6 us  [the longest x6 60.9 us: there(): return lax.ppermute(message, 'seq', list(enumerate(rounds[r][1])))]
    ppermute x18 -> x12, starting transfers between devices: 50.1 us -> 59.7 us  [the longest x6 46.4 us: back(): lax.ppermute(message, 'seq', [(b, a) for a, b in enumerate(rounds[r][1])])]
    unnamed x40 -> x20, local copies, waits for them, and re-layouts: 8.73 us -> 3.99 us
    another operation x6 -> x0, other arithmetic: 3.79 us -> none  [the longest x3 1.98 us: pack(): jnp.stack(starts).astype(jnp.int32)]
    pallas_call x3 -> x2, Pallas kernels: 22.2 us -> 19.6 us  [attend(): pl.pallas_call(functools.partial(attend_kernel, groups), out_shape=[jax.S...]
  transfers between devices with their start and end apart: 18 -> 12, of which waited for: 3 -> 6; matrix products, arithmetic and copies ran while one was open for 1% -> 0% of each run, Pallas kernels for 46% -> 19%
where the time goes in v2:
time: 194 us; the launch traced here: 193 us
  waiting for transfers between devices  87.6 us (45%)
  starting transfers between devices  59.7 us (31%)
  Pallas kernels  41.1 us (21%)
  local copies, waits for them, and re-layouts  3.99 us (2%)
    ppermute x6, waiting for transfers between devices, there(): return lax.ppermute(message, 'seq', list(enumerate(rounds[r][1])))  60.9 us
    ppermute x6, starting transfers between devices, back(): lax.ppermute(message, 'seq', [(b, a) for a, b in enumerate(rounds[r][1])])  46.4 us
    ppermute x6, waiting for transfers between devices, back(): lax.ppermute(message, 'seq', [(b, a) for a, b in enumerate(rounds[r][1])])  26.7 us
    pallas_call x2, Pallas kernels, attend(): pl.pallas_call(functools.partial(attend_kernel, groups), out_shape=[jax.S...  19.6 us
    pallas_call x6, Pallas kernels, pack(): pl.pallas_call(functools.partial(pack_kernel, groups, span, base, width),...  14 us
    ppermute x6, starting transfers between devices, there(): return lax.ppermute(message, 'seq', list(enumerate(rounds[r][1])))  13.3 us
    pallas_call x4, Pallas kernels, place(): pl.pallas_call(functools.partial(place_kernel, groups, span, base, width)...  7.57 us
    unnamed x20, local copies, waits for them, and re-layouts  3.99 us
  transfers between devices with their start and end apart: 12, of which 6 were waited for; matrix products, arithmetic and copies ran while one was open for 0% of the time, Pallas kernels for 19%

profile of v2, /device:TPU:0, one launch (start us, length us, event | category | flops | bytes accessed | tf_op | source)
XLA Modules:
  0.0 193.2 jit_solution(6914816173795074837)
XLA Ops:
  0.6 3.3 %pack.11 = (bf16[6,128,768]{2,1,0:T(8,128)(2,1)}, bf16[6,128,768]{2,1,0:T(8,128)(2,1)}) custom-call(bf16[128,4096]{1,0:T(8,128)(2,1)} %refs_0_.11, bf16[128,4096]{1,0:T(8,128)(2,1)} %refs_1_.11, bf16[128,4096]{1,0:T(8,128)(2,1)} %refs_2_.11, bf16[128,4096]{1,0:T(8,128)(2,1)} %refs_3_.11, bf16[128,4096]{1,0:T(8,128)(2,1)} %refs_4_.11, bf16[128,4096]{1,0:T(8,128)(2,1)} %refs_5_.11), custom_call_target="tpu_custom_call" | custom-call | bytes 4718592 | tf_op jit(solution)/shard_map/pack/pallas_call | solution.py:68
  3.9 4.1 %collective-permute-start.7 = (bf16[6,128,768]{2,1,0:T(8,128)(2,1)}, bf16[6,128,768]{2,1,0:T(8,128)(2,1)S(1)}, u32[]{:S(2)}, u32[]{:S(2)}) collective-permute-start(bf16[6,128,768]{2,1,0:T(8,128)(2,1)} %get-tuple-element.26), channel_id=1, source_target_pairs={{0,2},{1,3},{2,0},{3,1},{4,6},{5,7},{6,4},{7,5},{8,10},{9,11},{10,... | collective-permute-start | bytes 3538952 | tf_op jit(solution)/shard_map/ppermute | solution.py:174
  8.0 1.6 collective-permute-start.8
  9.6 2.4 %pack.10 = bf16[6,128,768]{2,1,0:T(8,128)(2,1)} custom-call(bf16[128,4096]{1,0:T(8,128)(2,1)} %refs_0_.11, bf16[128,4096]{1,0:T(8,128)(2,1)} %refs_1_.11, bf16[128,4096]{1,0:T(8,128)(2,1)} %refs_2_.11, bf16[128,4096]{1,0:T(8,128)(2,1)} %refs_3_.11, bf16[128,4096]{1,0:T(8,128)(2,1)} %refs_4_.11, bf16[128,4096]{1,0:T(8,128)(2,1)} %refs_5_.11), custom_call_target="tpu_custom_call" | custom-call | bytes 2359296 | tf_op jit(solution)/shard_map/pack/pallas_call | solution.py:68
  12.0 0.1 collective-permute-start.6
  12.1 2.2 %pack.8 = (bf16[6,128,256]{2,1,0:T(8,128)(2,1)}, bf16[6,128,256]{2,1,0:T(8,128)(2,1)}) custom-call(bf16[128,4096]{1,0:T(8,128)(2,1)} %refs_0_.11, bf16[128,4096]{1,0:T(8,128)(2,1)} %refs_1_.11, bf16[128,4096]{1,0:T(8,128)(2,1)} %refs_2_.11, bf16[128,4096]{1,0:T(8,128)(2,1)} %refs_3_.11, bf16[128,4096]{1,0:T(8,128)(2,1)} %refs_4_.11, bf16[128,4096]{1,0:T(8,128)(2,1)} %refs_5_.11), custom_call_target="tpu_custom_call" | custom-call | bytes 1572864 | tf_op jit(solution)/shard_map/pack/pallas_call | solution.py:68
  14.2 1.9 %collective-permute-start.1 = (bf16[6,128,256]{2,1,0:T(8,128)(2,1)}, bf16[6,128,256]{2,1,0:T(8,128)(2,1)}, u32[]{:S(2)}, u32[]{:S(2)}) collective-permute-start(bf16[6,128,256]{2,1,0:T(8,128)(2,1)} %get-tuple-element.20), channel_id=1, source_target_pairs={{0,2},{1,3},{2,0},{3,1},{4,6},{5,7},{6,4},{7,5},{8,10},{9,11},{10,... | collective-permute-start | bytes 1179656 | tf_op jit(solution)/shard_map/ppermute | solution.py:174
  16.2 2.5 %collective-permute-start.2 = (bf16[6,128,256]{2,1,0:T(8,128)(2,1)}, bf16[6,128,256]{2,1,0:T(8,128)(2,1)}, u32[]{:S(2)}, u32[]{:S(2)}) collective-permute-start(bf16[6,128,256]{2,1,0:T(8,128)(2,1)} %get-tuple-element.21), channel_id=1, source_target_pairs={{0,1},{1,0},{2,3},{3,2},{4,5},{5,4},{6,7},{7,6},{8,9},{9,8},{10,11... | collective-permute-start | bytes 1179656 | tf_op jit(solution)/shard_map/ppermute | solution.py:174
  18.7 2.4 %pack.9.refs_0_ = bf16[6,128,768]{2,1,0:T(8,128)(2,1)} custom-call(bf16[128,4096]{1,0:T(8,128)(2,1)} %refs_0_.11, bf16[128,4096]{1,0:T(8,128)(2,1)} %refs_1_.11, bf16[128,4096]{1,0:T(8,128)(2,1)} %refs_2_.11, bf16[128,4096]{1,0:T(8,128)(2,1)} %refs_3_.11, bf16[128,4096]{1,0:T(8,128)(2,1)} %refs_4_.11, bf16[128,4096]{1,0:T(8,128)(2,1)} %refs_5_.11), custom_call_target="tpu_custom_call" | custom-call | bytes 2359296 | tf_op jit(solution)/shard_map/pack/pallas_call | solution.py:68
  21.1 0.0 copy-start
  21.1 1.9 pack.7
  23.0 38.2 %collective-permute-done.7.refs_2_ = bf16[6,128,768]{2,1,0:T(8,128)(2,1)S(1)} collective-permute-done((bf16[6,128,768]{2,1,0:T(8,128)(2,1)}, bf16[6,128,768]{2,1,0:T(8,128)(2,1)S(1)}, u32[]{:S(2)}, u32[]{:S(2)}) %collective-permute-start.7) | collective-permute-done | bytes 1179680 | tf_op jit(solution)/shard_map/ppermute | solution.py:174
  61.2 3.1 %collective-permute-start = (bf16[6,128,256]{2,1,0:T(8,128)(2,1)}, bf16[6,128,256]{2,1,0:T(8,128)(2,1)}, u32[]{:S(2)}, u32[]{:S(2)}) collective-permute-start(bf16[6,128,256]{2,1,0:T(8,128)(2,1)} %pack.7), channel_id=1, source_target_pairs={{0,3},{1,2},{2,1},{3,0},{4,7},{5,6},{6,5},{7,4},{8,11},{9,10},{10,... | collective-permute-start | bytes 1179656 | tf_op jit(solution)/shard_map/ppermute | solution.py:174
  64.3 21.8 %collective-permute-done.8.refs_3_ = bf16[6,128,768]{2,1,0:T(8,128)(2,1)} collective-permute-done((bf16[6,128,768]{2,1,0:T(8,128)(2,1)}, bf16[6,128,768]{2,1,0:T(8,128)(2,1)}, u32[]{:S(2)}, u32[]{:S(2)}) %collective-permute-start.8) | collective-permute-done | bytes 1179680 | tf_op jit(solution)/shard_map/ppermute | solution.py:174
  86.1 1.0 collective-permute-done.6.refs_1_
  87.1 0.0 copy-done
  87.1 14.3 %attend.3 = (bf16[2,128,768]{2,1,0:T(8,128)(2,1)S(1)}, bf16[2,128,768]{2,1,0:T(8,128)(2,1)}, bf16[2,128,768]{2,1,0:T(8,128)(2,1)}, bf16[2,128,768]{2,1,0:T(8,128)(2,1)}) custom-call(bf16[6,128,768]{2,1,0:T(8,128)(2,1)S(1)} %copy-done, bf16[6,128,768]{2,1,0:T(8,128)(2,1)S(1)} %collective-permute-done.6.refs_1_, ...), custom_call_target="tpu_custom_call" | custom-call | flops 2415919104 | bytes 6291456 | tf_op jit(solution)/shard_map/attend/pallas_call | solution.py:150
  101.4 0.8 copy-done.2
  102.1 42.6 %collective-permute-start.10 = (bf16[2,128,768]{2,1,0:T(8,128)(2,1)}, bf16[2,128,768]{2,1,0:T(8,128)(2,1)S(1)}, u32[]{:S(2)}, u32[]{:S(2)}) collective-permute-start(bf16[2,128,768]{2,1,0:T(8,128)(2,1)} %get-tuple-element.29), channel_id=1, source_target_pairs={{2,0},{3,1},{0,2},{1,3},{6,4},{7,5},{4,6},{5,7},{10,8},{11,9},{8,1... | collective-permute-start | bytes 1179656 | tf_op jit(solution)/shard_map/ppermute | solution.py:177
  144.7 0.0 collective-permute-start.11
  144.7 0.0 collective-permute-done.1.refs_2_
  144.7 1.5 collective-permute-start.9
  146.2 1.8 pack.6.refs_0_
  148.0 0.0 collective-permute-done.2.refs_3_
  148.0 0.0 collective-permute-done.refs_1_
  148.0 0.0 copy-start.1
  148.0 1.0 copy-done.1
  149.0 5.3 %attend.2 = (bf16[2,128,256]{2,1,0:T(8,128)(2,1)S(1)}, bf16[2,128,256]{2,1,0:T(8,128)(2,1)S(1)}, bf16[2,128,256]{2,1,0:T(8,128)(2,1)S(1)}, bf16[2,128,256]{2,1,0:T(8,128)(2,1)S(1)}) custom-call(bf16[6,128,256]{2,1,0:T(8,128)(2,1)S(1)} %copy-done.1, bf16[6,128,256]{2,1,0:T(8,128)(2,1)} %collective-permute-done.refs_1_, ...), custom_call_target="tpu_custom_call" | custom-call | flops 805306368 | bytes 2097152 | tf_op jit(solution)/shard_map/attend/pallas_call | solution.py:150
  154.3 0.0 copy-start.3
  154.3 0.6 copy-done.3
  154.9 2.4 %collective-permute-start.3 = (bf16[2,128,256]{2,1,0:T(8,128)(2,1)S(1)}, bf16[2,128,256]{2,1,0:T(8,128)(2,1)S(1)}, u32[]{:S(2)}, u32[]{:S(2)}) collective-permute-start(bf16[2,128,256]{2,1,0:T(8,128)(2,1)S(1)} %get-tuple-element.22), channel_id=1, source_target_pairs={{3,0},{2,1},{1,2},{0,3},{7,4},{6,5},{5,6},{4,7},{11,8},{10,9},{9,1... | collective-permute-start | bytes 393224 | tf_op jit(solution)/shard_map/ppermute | solution.py:177
  157.3 0.0 collective-permute-start.4
  157.3 7.2 %collective-permute-done.10.refs_1_ = bf16[2,128,768]{2,1,0:T(8,128)(2,1)S(1)} collective-permute-done((bf16[2,128,768]{2,1,0:T(8,128)(2,1)}, bf16[2,128,768]{2,1,0:T(8,128)(2,1)S(1)}, u32[]{:S(2)}, u32[]{:S(2)}) %collective-permute-start.10) | collective-permute-done | bytes 393248 | tf_op jit(solution)/shard_map/ppermute | solution.py:177
  164.5 0.0 collective-permute-start.5
  164.5 1.9 place.4
  166.4 8.8 %collective-permute-done.11.refs_2_ = bf16[2,128,768]{2,1,0:T(8,128)(2,1)S(1)} collective-permute-done((bf16[2,128,768]{2,1,0:T(8,128)(2,1)}, bf16[2,128,768]{2,1,0:T(8,128)(2,1)S(1)}, u32[]{:S(2)}, u32[]{:S(2)}) %collective-permute-start.11) | collective-permute-done | bytes 393248 | tf_op jit(solution)/shard_map/ppermute | solution.py:177
  175.1 0.0 collective-permute-done.9.refs_0_
  175.2 0.7 copy-done.5
  175.9 0.2 copy-done.6
  176.1 2.3 %place.5 = (bf16[128,4096]{1,0:T(8,128)(2,1)}, bf16[128,4096]{1,0:T(8,128)(2,1)}) custom-call(bf16[2,128,768]{2,1,0:T(8,128)(2,1)} %copy-done.6, bf16[2,128,768]{2,1,0:T(8,128)(2,1)} %copy-done.4, bf16[2,128,768]{2,1,0:T(8,128)(2,1)} %copy-done.5, bf16[128,4096]{1,0:T(8,128)(2,1)} %get-tuple-element.32.refs_3_, ...), custom_call_target="tpu_custom_call", output_to_operand_aliasing={{0}: (3, {}), {1}: (4, {})} | custom-call | bytes 2359296 | tf_op jit(solution)/shard_map/place/pallas_call | solution.py:101
  178.4 1.6 place.6
  179.9 0.0 collective-permute-done.3.refs_0_
  179.9 0.0 copy-start.7
  180.0 10.7 %collective-permute-done.4.refs_1_ = bf16[2,128,256]{2,1,0:T(8,128)(2,1)S(1)} collective-permute-done((bf16[2,128,256]{2,1,0:T(8,128)(2,1)S(1)}, bf16[2,128,256]{2,1,0:T(8,128)(2,1)S(1)}, u32[]{:S(2)}, u32[]{:S(2)}) %collective-permute-start.4) | collective-permute-done | bytes 131104 | tf_op jit(solution)/shard_map/ppermute | solution.py:177
  190.7 0.0 collective-permute-done.5.refs_2_
  190.7 0.6 copy-done.8
  191.3 0.0 copy-done.9
  191.4 1.8 place.7
  (8 shorter events, 0.0 us)
Async XLA Ops:
  3.9 57.3 %collective-permute-start.7 = (bf16[6,128,768]{2,1,0:T(8,128)(2,1)}, bf16[6,128,768]{2,1,0:T(8,128)(2,1)S(1)}, u32[]{:S(2)}, u32[]{:S(2)}) collective-permute-start(bf16[6,128,768]{2,1,0:T(8,128)(2,1)} %get-tuple-element.26), channel_id=1, source_target_pairs={{0,2},{1,3},{2,0},{3,1},{4,6},{5,7},{6,4},{7,5},{8,10},{9,11},{10,... | collective-permute-start | bytes 3538952 | tf_op jit(solution)/shard_map/ppermute | solution.py:174
  8.0 78.1 %collective-permute-start.8 = (bf16[6,128,768]{2,1,0:T(8,128)(2,1)}, bf16[6,128,768]{2,1,0:T(8,128)(2,1)}, u32[]{:S(2)}, u32[]{:S(2)}) collective-permute-start(bf16[6,128,768]{2,1,0:T(8,128)(2,1)} %get-tuple-element.27), channel_id=1, source_target_pairs={{0,1},{1,0},{2,3},{3,2},{4,5},{5,4},{6,7},{7,6},{8,9},{9,8},{10,11... | collective-permute-start | bytes 3538952 | tf_op jit(solution)/shard_map/ppermute | solution.py:174
  12.0 75.1 %collective-permute-start.6 = (bf16[6,128,768]{2,1,0:T(8,128)(2,1)}, bf16[6,128,768]{2,1,0:T(8,128)(2,1)S(1)}, u32[]{:S(2)}, u32[]{:S(2)}) collective-permute-start(bf16[6,128,768]{2,1,0:T(8,128)(2,1)} %pack.10), channel_id=1, source_target_pairs={{0,3},{1,2},{2,1},{3,0},{4,7},{5,6},{6,5},{7,4},{8,11},{9,10},{10,... | collective-permute-start | bytes 3538952 | tf_op jit(solution)/shard_map/ppermute | solution.py:174
  14.2 130.5 %collective-permute-start.1 = (bf16[6,128,256]{2,1,0:T(8,128)(2,1)}, bf16[6,128,256]{2,1,0:T(8,128)(2,1)}, u32[]{:S(2)}, u32[]{:S(2)}) collective-permute-start(bf16[6,128,256]{2,1,0:T(8,128)(2,1)} %get-tuple-element.20), channel_id=1, source_target_pairs={{0,2},{1,3},{2,0},{3,1},{4,6},{5,7},{6,4},{7,5},{8,10},{9,11},{10,... | collective-permute-start | bytes 1179656 | tf_op jit(solution)/shard_map/ppermute | solution.py:174
  16.2 131.8 %collective-permute-start.2 = (bf16[6,128,256]{2,1,0:T(8,128)(2,1)}, bf16[6,128,256]{2,1,0:T(8,128)(2,1)}, u32[]{:S(2)}, u32[]{:S(2)}) collective-permute-start(bf16[6,128,256]{2,1,0:T(8,128)(2,1)} %get-tuple-element.21), channel_id=1, source_target_pairs={{0,1},{1,0},{2,3},{3,2},{4,5},{5,4},{6,7},{7,6},{8,9},{9,8},{10,11... | collective-permute-start | bytes 1179656 | tf_op jit(solution)/shard_map/ppermute | solution.py:174
  21.1 65.9 %copy-start = (bf16[6,128,768]{2,1,0:T(8,128)(2,1)S(1)}, bf16[6,128,768]{2,1,0:T(8,128)(2,1)}, u32[]{:S(2)}) copy-start(bf16[6,128,768]{2,1,0:T(8,128)(2,1)} %pack.9.refs_0_) | copy-start | bytes 3538948
  61.2 86.8 %collective-permute-start = (bf16[6,128,256]{2,1,0:T(8,128)(2,1)}, bf16[6,128,256]{2,1,0:T(8,128)(2,1)}, u32[]{:S(2)}, u32[]{:S(2)}) collective-permute-start(bf16[6,128,256]{2,1,0:T(8,128)(2,1)} %pack.7), channel_id=1, source_target_pairs={{0,3},{1,2},{2,1},{3,0},{4,7},{5,6},{6,5},{7,4},{8,11},{9,10},{10,... | collective-permute-start | bytes 1179656 | tf_op jit(solution)/shard_map/ppermute | solution.py:174
  101.4 0.8 copy-start.2
  102.1 62.4 %collective-permute-start.10 = (bf16[2,128,768]{2,1,0:T(8,128)(2,1)}, bf16[2,128,768]{2,1,0:T(8,128)(2,1)S(1)}, u32[]{:S(2)}, u32[]{:S(2)}) collective-permute-start(bf16[2,128,768]{2,1,0:T(8,128)(2,1)} %get-tuple-element.29), channel_id=1, source_target_pairs={{2,0},{3,1},{0,2},{1,3},{6,4},{7,5},{4,6},{5,7},{10,8},{11,9},{8,1... | collective-permute-start | bytes 1179656 | tf_op jit(solution)/shard_map/ppermute | solution.py:177
  144.7 30.4 %collective-permute-start.11 = (bf16[2,128,768]{2,1,0:T(8,128)(2,1)}, bf16[2,128,768]{2,1,0:T(8,128)(2,1)S(1)}, u32[]{:S(2)}, u32[]{:S(2)}) collective-permute-start(bf16[2,128,768]{2,1,0:T(8,128)(2,1)} %get-tuple-element.30), channel_id=1, source_target_pairs={{1,0},{0,1},{3,2},{2,3},{5,4},{4,5},{7,6},{6,7},{9,8},{8,9},{11,10... | collective-permute-start | bytes 1179656 | tf_op jit(solution)/shard_map/ppermute | solution.py:177
  144.7 30.4 %collective-permute-start.9 = (bf16[2,128,768]{2,1,0:T(8,128)(2,1)}, bf16[2,128,768]{2,1,0:T(8,128)(2,1)S(1)}, u32[]{:S(2)}, u32[]{:S(2)}) collective-permute-start(bf16[2,128,768]{2,1,0:T(8,128)(2,1)} %get-tuple-element.28), channel_id=1, source_target_pairs={{3,0},{2,1},{1,2},{0,3},{7,4},{6,5},{5,6},{4,7},{11,8},{10,9},{9,1... | collective-permute-start | bytes 1179656 | tf_op jit(solution)/shard_map/ppermute | solution.py:177
  148.0 1.0 copy-start.1
  154.3 0.6 copy-start.3
  154.9 25.0 %collective-permute-start.3 = (bf16[2,128,256]{2,1,0:T(8,128)(2,1)S(1)}, bf16[2,128,256]{2,1,0:T(8,128)(2,1)S(1)}, u32[]{:S(2)}, u32[]{:S(2)}) collective-permute-start(bf16[2,128,256]{2,1,0:T(8,128)(2,1)S(1)} %get-tuple-element.22), channel_id=1, source_target_pairs={{3,0},{2,1},{1,2},{0,3},{7,4},{6,5},{5,6},{4,7},{11,8},{10,9},{9,1... | collective-permute-start | bytes 393224 | tf_op jit(solution)/shard_map/ppermute | solution.py:177
  157.3 33.4 %collective-permute-start.4 = (bf16[2,128,256]{2,1,0:T(8,128)(2,1)S(1)}, bf16[2,128,256]{2,1,0:T(8,128)(2,1)S(1)}, u32[]{:S(2)}, u32[]{:S(2)}) collective-permute-start(bf16[2,128,256]{2,1,0:T(8,128)(2,1)S(1)} %get-tuple-element.23), channel_id=1, source_target_pairs={{2,0},{3,1},{0,2},{1,3},{6,4},{7,5},{4,6},{5,7},{10,8},{11,9},{8,1... | collective-permute-start | bytes 393224 | tf_op jit(solution)/shard_map/ppermute | solution.py:177
  164.5 10.7 %copy-start.4 = (bf16[2,128,768]{2,1,0:T(8,128)(2,1)}, bf16[2,128,768]{2,1,0:T(8,128)(2,1)S(1)}, u32[]{:S(2)}) copy-start(bf16[2,128,768]{2,1,0:T(8,128)(2,1)S(1)} %collective-permute-done.10.refs_1_) | copy-start | bytes 1179652
  164.5 26.2 %collective-permute-start.5 = (bf16[2,128,256]{2,1,0:T(8,128)(2,1)S(1)}, bf16[2,128,256]{2,1,0:T(8,128)(2,1)S(1)}, u32[]{:S(2)}, u32[]{:S(2)}) collective-permute-start(bf16[2,128,256]{2,1,0:T(8,128)(2,1)S(1)} %get-tuple-element.24), channel_id=1, source_target_pairs={{1,0},{0,1},{3,2},{2,3},{5,4},{4,5},{7,6},{6,7},{9,8},{8,9},{11,10... | collective-permute-start | bytes 393224 | tf_op jit(solution)/shard_map/ppermute | solution.py:177
  175.1 0.8 copy-start.5
  175.1 0.9 copy-start.6
  179.9 10.7 %copy-start.7 = (bf16[2,128,256]{2,1,0:T(8,128)(2,1)}, bf16[2,128,256]{2,1,0:T(8,128)(2,1)S(1)}, u32[]{:S(2)}) copy-start(bf16[2,128,256]{2,1,0:T(8,128)(2,1)S(1)} %collective-permute-done.3.refs_0_) | copy-start | bytes 393220
  190.7 0.6 copy-start.8
  190.7 0.7 copy-start.9

commit v3 on v2

--- a/solution.py
+++ b/solution.py
@@ -10,7 +10,12 @@
 
 HEAD = 128
 ANYWHERE = pl.BlockSpec(memory_space=pl.ANY)
+FAR = pl.BlockSpec(memory_space=pltpu.HBM)
 WHOLE = pl.BlockSpec(memory_space=pltpu.VMEM)
+
+
+def limit(*sizes):
+    return pltpu.CompilerParams(vmem_limit_bytes=sum(sizes) + 2**20)
 
 
 def chunk_sizes(count):
@@ -22,7 +27,7 @@
     if count & (count - 1) == 0:
         return [
             (lambda me, step=step: me ^ step, [i ^ step for i in range(count)])
-            for step in range(count - 1, 0, -1)
+            for step in range(1, count)
         ]
     return [
         (lambda me, step=step: lax.rem(me + step, count), [(i + step) % count for i in range(count)])
@@ -46,8 +51,8 @@
         copy.wait()
 
 
-def pack_kernel(groups, span, base, width, *refs):
-    arrays, messages, sems = refs[:6], refs[-1 - len(groups):-1], refs[-1]
+def pack_kernel(groups, count, span, base, width, *refs):
+    arrays, messages, sems = refs[:count], refs[-1 - len(groups):-1], refs[-1]
     run(
         [
             pltpu.make_async_copy(
@@ -56,26 +61,26 @@
                 sems.at[m, i],
             )
             for m, group in enumerate(groups)
-            for i in range(6)
+            for i in range(count)
         ]
     )
 
 
 def pack(arrays, groups, span, base, width, after=()):
-    count = len(groups)
+    count = len(arrays)
     rows = arrays[0].shape[0]
-    message = jax.ShapeDtypeStruct((6, rows, width), arrays[0].dtype)
+    message = pltpu.VMEM((count, rows, width), arrays[0].dtype)
+    size = len(groups) * count * rows * width * 2
     return pl.pallas_call(
-        functools.partial(pack_kernel, groups, span, base, width),
-        out_shape=[message] * count,
-        in_specs=[ANYWHERE] * (6 + len(after)),
-        out_specs=[WHOLE] * count,
-        scratch_shapes=[pltpu.SemaphoreType.DMA((count, 6))],
-        cost_estimate=pl.CostEstimate(
-            flops=0, bytes_accessed=count * 24 * rows * width, transcendentals=0
-        ),
+        functools.partial(pack_kernel, groups, count, span, base, width),
+        out_shape=[message] * len(groups),
+        in_specs=[FAR] * count + [ANYWHERE] * len(after),
+        out_specs=[WHOLE] * len(groups),
+        scratch_shapes=[pltpu.SemaphoreType.DMA((len(groups), count))],
+        compiler_params=limit(size),
+        cost_estimate=pl.CostEstimate(flops=0, bytes_accessed=2 * size, transcendentals=0),
         name="pack",
-    )(*arrays, *after)
+    )(*(pltpu.with_memory_space_constraint(array, pltpu.HBM) for array in arrays), *after)
 
 
 def place_kernel(groups, span, base, width, *refs):
@@ -101,10 +106,11 @@
     return pl.pallas_call(
         functools.partial(place_kernel, groups, span, base, width),
         out_shape=[out, out],
-        in_specs=[WHOLE] * count + [ANYWHERE] * len(outs),
-        out_specs=[ANYWHERE, ANYWHERE],
+        in_specs=[WHOLE] * count + [FAR] * len(outs),
+        out_specs=[FAR, FAR],
         scratch_shapes=[pltpu.SemaphoreType.DMA((count, 2))],
         input_output_aliases={count + i: i for i in range(len(outs))},
+        compiler_params=limit(count * rows * width * 4),
         cost_estimate=pl.CostEstimate(
             flops=0, bytes_accessed=count * rows * width * 8, transcendentals=0
         ),
@@ -112,11 +118,15 @@
     )(*messages, *outs)
 
 
-def attend_kernel(groups, *refs):
-    messages, results = refs[:groups], refs[groups:]
+def attend_kernel(layout, *refs):
+    messages = []
+    for counts in layout:
+        parts, refs = refs[:len(counts)], refs[len(counts):]
+        messages.append([part.at[i] for part, count in zip(parts, counts) for i in range(count)])
+    results = refs
 
     def joined(which):
-        return jnp.concatenate([message[which] for message in messages], axis=0)
+        return jnp.concatenate([message[which][...] for message in messages], axis=0)
 
     keys = joined(1)
     values = joined(2)
@@ -126,8 +136,8 @@
     scale = width ** -0.5
     across = (((1,), (1,)), ((), ()))
     for message, result in zip(messages, results):
-        queries = message[0]
-        paired = jnp.concatenate([message[3], queries], axis=1)
+        queries = message[0][...]
+        paired = jnp.concatenate([message[3][...], queries], axis=1)
         scores = lax.dot_general(queries, keys, across, preferred_element_type=jnp.float32)
         tangent = lax.dot_general(paired, both_keys, across, preferred_element_type=jnp.float32)
         row_max = jnp.max(scores, axis=1, keepdims=True)
@@ -144,23 +154,27 @@
 
 def attend(messages):
     groups = len(messages)
-    _, rows, width = messages[0].shape
+    parts = [part for message in messages for part in message]
+    layout = [[part.shape[0] for part in message] for message in messages]
+    _, rows, width = parts[0].shape
     heads = width // HEAD
     tokens = rows * groups
     return pl.pallas_call(
-        functools.partial(attend_kernel, groups),
+        functools.partial(attend_kernel, layout),
         out_shape=[jax.ShapeDtypeStruct((2, rows, width), jnp.bfloat16)] * groups,
         grid=(heads,),
-        in_specs=[pl.BlockSpec((6, rows, HEAD), lambda h: (0, 0, h))] * groups,
+        in_specs=[
+            pl.BlockSpec((part.shape[0], rows, HEAD), lambda h: (0, 0, h)) for part in parts
+        ],
         out_specs=[pl.BlockSpec((2, rows, HEAD), lambda h: (0, 0, h))] * groups,
-        compiler_params=pltpu.CompilerParams(vmem_limit_bytes=48 * 2**20),
+        compiler_params=limit(32 * tokens * HEAD * 2, 32 * rows * tokens * 4),
         cost_estimate=pl.CostEstimate(
             flops=heads * 12 * tokens * tokens * HEAD,
             bytes_accessed=heads * 16 * tokens * HEAD,
             transcendentals=heads * tokens * tokens,
         ),
         name="attend",
-    )(*messages)
+    )(*parts)
 
 
 def on_device(*arrays):
@@ -183,10 +197,9 @@
         base += heads * HEAD
     received = []
     for base, width in chunks:
-        first = pack(arrays, groups[:1], span, base, width)
-        rest = pack(arrays, groups[1:], span, base, width)
-        own = pack(arrays, [own_group], span, base, width)
-        received.append([*own, *(there(m, r) for r, m in enumerate([*first, *rest]))])
+        sent = [pack(arrays, [group], span, base, width) for group in groups]
+        own = pack(arrays, [own_group], span, base, width, after=sent[-1])
+        received.append([own, *([there(part, r) for part in m] for r, m in enumerate(sent))])
     outs = ()
     for (base, width), messages in zip(chunks, received):
         own, *results = attend(messages)

time: 194 us -> 186 us (0.959)
  waiting for transfers between devices: 87.6 us -> 108 us
  starting transfers between devices: 59.7 us -> 46.4 us
  Pallas kernels: 41.1 us -> 30.6 us
  local copies, waits for them, and re-layouts: 3.99 us -> 0 us
    ppermute x6, starting transfers between devices: 46.4 us -> 10.1 us  [back(): lax.ppermute(message, 'seq', [(b, a) for a, b in enumerate(rounds[r][1])])]
    ppermute x6, waiting for transfers between devices: 60.9 us -> 95.6 us  [there(): return lax.ppermute(message, 'seq', list(enumerate(rounds[r][1])))]
    ppermute x6, starting transfers between devices: 13.3 us -> 36.3 us  [there(): return lax.ppermute(message, 'seq', list(enumerate(rounds[r][1])))]
    ppermute x6, waiting for transfers between devices: 26.7 us -> 12.3 us  [back(): lax.ppermute(message, 'seq', [(b, a) for a, b in enumerate(rounds[r][1])])]
    pallas_call x8 -> x10, Pallas kernels: 33.5 us -> 27.3 us  [the longest x2 17.5 us: attend(): pl.pallas_call(functools.partial(attend_kernel, layout), out_shape=[jax.S...]
    pallas_call x4, Pallas kernels: 7.57 us -> 3.29 us  [place(): pl.pallas_call(functools.partial(place_kernel, groups, span, base, width)...]
    unnamed x20 -> x0, local copies, waits for them, and re-layouts: 3.99 us -> none
  transfers between devices with their start and end apart: 12 -> 12, of which waited for: 6 -> 5; matrix products, arithmetic and copies ran while one was open for 0% -> 0% of each run, Pallas kernels for 19% -> 15%
where the time goes in v3:
time: 186 us
  waiting for transfers between devices  108 us (58%)
  starting transfers between devices  46.4 us (25%)
  Pallas kernels  30.6 us (16%)
    ppermute x6, waiting for transfers between devices, there(): return lax.ppermute(message, 'seq', list(enumerate(rounds[r][1])))  95.6 us
    ppermute x6, starting transfers between devices, there(): return lax.ppermute(message, 'seq', list(enumerate(rounds[r][1])))  36.3 us
    pallas_call x2, Pallas kernels, attend(): pl.pallas_call(functools.partial(attend_kernel, layout), out_shape=[jax.S...  17.5 us
    ppermute x6, waiting for transfers between devices, back(): lax.ppermute(message, 'seq', [(b, a) for a, b in enumerate(rounds[r][1])])  12.3 us
    ppermute x6, starting transfers between devices, back(): lax.ppermute(message, 'seq', [(b, a) for a, b in enumerate(rounds[r][1])])  10.1 us
    pallas_call x8, Pallas kernels, pack(): pl.pallas_call(functools.partial(pack_kernel, groups, count, span, base,...  9.83 us
  transfers between devices with their start and end apart: 12, of which 5 were waited for; matrix products, arithmetic and copies ran while one was open for 0% of the time, Pallas kernels for 15%

profile of v3, /device:TPU:0, one launch (start us, length us, event | category | flops | bytes accessed | tf_op | source)
XLA Modules:
  0.0 185.7 jit_solution(9838194287091717154)
XLA Ops:
  0.6 1.4 pack.12.refs_6_
  2.0 5.1 %collective-permute-start.8 = (bf16[6,128,768]{2,1,0:T(8,128)(2,1)S(1)}, bf16[6,128,768]{2,1,0:T(8,128)(2,1)S(1)}, u32[]{:S(2)}, u32[]{:S(2)}) collective-permute-start(bf16[6,128,768]{2,1,0:T(8,128)(2,1)S(1)} %pack.12.refs_6_), channel_id=1, source_target_pairs={{0,3},{1,2},{2,1},{3,0},{4,7},{5,6},{6,5},{7,4},{8,11},{9,10},{10,... | collective-permute-start | bytes 3538952 | tf_op jit(solution)/shard_map/ppermute | solution.py:188
  7.2 1.4 pack.14
  8.6 0.1 collective-permute-start.6
  8.6 1.4 pack.15
  10.0 0.6 collective-permute-start.7
  10.7 1.1 pack.8.refs_6_
  11.7 3.9 %collective-permute-start.2 = (bf16[6,128,256]{2,1,0:T(8,128)(2,1)S(1)}, bf16[6,128,256]{2,1,0:T(8,128)(2,1)S(1)}, u32[]{:S(2)}, u32[]{:S(2)}) collective-permute-start(bf16[6,128,256]{2,1,0:T(8,128)(2,1)S(1)} %pack.8.refs_6_), channel_id=1, source_target_pairs={{0,3},{1,2},{2,1},{3,0},{4,7},{5,6},{6,5},{7,4},{8,11},{9,10},{10,... | collective-permute-start | bytes 1179656 | tf_op jit(solution)/shard_map/ppermute | solution.py:188
  15.6 1.1 pack.10
  16.7 0.1 collective-permute-start
  16.7 1.4 pack.13.refs_0_
  18.2 1.1 pack.11
  19.2 14.8 %collective-permute-done.8.refs_3_ = bf16[6,128,768]{2,1,0:T(8,128)(2,1)S(1)} collective-permute-done((bf16[6,128,768]{2,1,0:T(8,128)(2,1)S(1)}, bf16[6,128,768]{2,1,0:T(8,128)(2,1)S(1)}, u32[]{:S(2)}, u32[]{:S(2)}) %collective-permute-start.8) | collective-permute-done | bytes 1179680 | tf_op jit(solution)/shard_map/ppermute | solution.py:188
  34.0 26.5 %collective-permute-start.1 = (bf16[6,128,256]{2,1,0:T(8,128)(2,1)S(1)}, bf16[6,128,256]{2,1,0:T(8,128)(2,1)S(1)}, u32[]{:S(2)}, u32[]{:S(2)}) collective-permute-start(bf16[6,128,256]{2,1,0:T(8,128)(2,1)S(1)} %pack.11), channel_id=1, source_target_pairs={{0,2},{1,3},{2,0},{3,1},{4,6},{5,7},{6,4},{7,5},{8,10},{9,11},{10,... | collective-permute-start | bytes 1179656 | tf_op jit(solution)/shard_map/ppermute | solution.py:188
  60.6 0.0 collective-permute-done.6.refs_1_
  60.6 65.4 %collective-permute-done.7.refs_2_ = bf16[6,128,768]{2,1,0:T(8,128)(2,1)S(1)} collective-permute-done((bf16[6,128,768]{2,1,0:T(8,128)(2,1)S(1)}, bf16[6,128,768]{2,1,0:T(8,128)(2,1)S(1)}, u32[]{:S(2)}, u32[]{:S(2)}) %collective-permute-start.7) | collective-permute-done | bytes 1179680 | tf_op jit(solution)/shard_map/ppermute | solution.py:188
  125.9 13.1 %attend.3 = (bf16[2,128,768]{2,1,0:T(8,128)(2,1)S(1)}, bf16[2,128,768]{2,1,0:T(8,128)(2,1)S(1)}, bf16[2,128,768]{2,1,0:T(8,128)(2,1)S(1)}, bf16[2,128,768]{2,1,0:T(8,128)(2,1)S(1)}) custom-call(bf16[6,128,768]{2,1,0:T(8,128)(2,1)S(1)} %pack.13.refs_0_, bf16[6,128,768]{2,1,0:T(8,128)(2,1)S(1)} %collective-permute-done.6.refs_1_, ...), custom_call_target="tpu_custom_call" | custom-call | flops 2415919104 | bytes 6291456 | tf_op jit(solution)/shard_map/attend/pallas_call | solution.py:162
  139.0 0.1 collective-permute-start.10
  139.1 2.7 %collective-permute-start.11 = (bf16[2,128,768]{2,1,0:T(8,128)(2,1)S(1)}, bf16[2,128,768]{2,1,0:T(8,128)(2,1)S(1)}, u32[]{:S(2)}, u32[]{:S(2)}) collective-permute-start(bf16[2,128,768]{2,1,0:T(8,128)(2,1)S(1)} %get-tuple-element.22), channel_id=1, source_target_pairs={{3,0},{2,1},{1,2},{0,3},{7,4},{6,5},{5,6},{4,7},{11,8},{10,9},{9,1... | collective-permute-start | bytes 1179656 | tf_op jit(solution)/shard_map/ppermute | solution.py:191
  141.9 0.0 collective-permute-done.2.refs_3_
  141.9 0.7 collective-permute-start.9
  142.6 1.1 pack.9.refs_0_
  143.7 0.0 collective-permute-done.refs_1_
  143.7 15.4 %collective-permute-done.1.refs_2_ = bf16[6,128,256]{2,1,0:T(8,128)(2,1)S(1)} collective-permute-done((bf16[6,128,256]{2,1,0:T(8,128)(2,1)S(1)}, bf16[6,128,256]{2,1,0:T(8,128)(2,1)S(1)}, u32[]{:S(2)}, u32[]{:S(2)}) %collective-permute-start.1) | collective-permute-done | bytes 393248 | tf_op jit(solution)/shard_map/ppermute | solution.py:188
  159.1 4.4 %attend.2 = (bf16[2,128,256]{2,1,0:T(8,128)(2,1)S(1)}, bf16[2,128,256]{2,1,0:T(8,128)(2,1)S(1)}, bf16[2,128,256]{2,1,0:T(8,128)(2,1)S(1)}, bf16[2,128,256]{2,1,0:T(8,128)(2,1)S(1)}) custom-call(bf16[6,128,256]{2,1,0:T(8,128)(2,1)S(1)} %pack.9.refs_0_, bf16[6,128,256]{2,1,0:T(8,128)(2,1)S(1)} %collective-permute-done.refs_1_, ...), custom_call_target="tpu_custom_call" | custom-call | flops 805306368 | bytes 2097152 | tf_op jit(solution)/shard_map/attend/pallas_call | solution.py:162
  163.5 0.5 collective-permute-start.3
  164.0 3.4 %collective-permute-start.4 = (bf16[2,128,256]{2,1,0:T(8,128)(2,1)S(1)}, bf16[2,128,256]{2,1,0:T(8,128)(2,1)S(1)}, u32[]{:S(2)}, u32[]{:S(2)}) collective-permute-start(bf16[2,128,256]{2,1,0:T(8,128)(2,1)S(1)} %get-tuple-element.17), channel_id=1, source_target_pairs={{2,0},{3,1},{0,2},{1,3},{6,4},{7,5},{4,6},{5,7},{10,8},{11,9},{8,1... | collective-permute-start | bytes 393224 | tf_op jit(solution)/shard_map/ppermute | solution.py:191
  167.4 2.1 %collective-permute-done.10.refs_1_ = bf16[2,128,768]{2,1,0:T(8,128)(2,1)S(1)} collective-permute-done((bf16[2,128,768]{2,1,0:T(8,128)(2,1)S(1)}, bf16[2,128,768]{2,1,0:T(8,128)(2,1)S(1)}, u32[]{:S(2)}, u32[]{:S(2)}) %collective-permute-start.10) | collective-permute-done | bytes 393248 | tf_op jit(solution)/shard_map/ppermute | solution.py:191
  169.5 2.7 %collective-permute-start.5 = (bf16[2,128,256]{2,1,0:T(8,128)(2,1)S(1)}, bf16[2,128,256]{2,1,0:T(8,128)(2,1)S(1)}, u32[]{:S(2)}, u32[]{:S(2)}) collective-permute-start(bf16[2,128,256]{2,1,0:T(8,128)(2,1)S(1)} %get-tuple-element.18), channel_id=1, source_target_pairs={{3,0},{2,1},{1,2},{0,3},{7,4},{6,5},{5,6},{4,7},{11,8},{10,9},{9,1... | collective-permute-start | bytes 393224 | tf_op jit(solution)/shard_map/ppermute | solution.py:191
  172.2 0.8 place.4
  172.9 0.0 collective-permute-done.11.refs_2_
  173.0 0.0 collective-permute-done.9.refs_0_
  173.0 1.1 place.5
  174.0 0.7 place.6
  174.7 0.0 collective-permute-done.3.refs_0_
  174.7 10.2 %collective-permute-done.4.refs_1_ = bf16[2,128,256]{2,1,0:T(8,128)(2,1)S(1)} collective-permute-done((bf16[2,128,256]{2,1,0:T(8,128)(2,1)S(1)}, bf16[2,128,256]{2,1,0:T(8,128)(2,1)S(1)}, u32[]{:S(2)}, u32[]{:S(2)}) %collective-permute-start.4) | collective-permute-done | bytes 131104 | tf_op jit(solution)/shard_map/ppermute | solution.py:191
  185.0 0.0 collective-permute-done.5.refs_2_
  185.0 0.8 place.7
Async XLA Ops:
  2.0 32.0 %collective-permute-start.8 = (bf16[6,128,768]{2,1,0:T(8,128)(2,1)S(1)}, bf16[6,128,768]{2,1,0:T(8,128)(2,1)S(1)}, u32[]{:S(2)}, u32[]{:S(2)}) collective-permute-start(bf16[6,128,768]{2,1,0:T(8,128)(2,1)S(1)} %pack.12.refs_6_), channel_id=1, source_target_pairs={{0,3},{1,2},{2,1},{3,0},{4,7},{5,6},{6,5},{7,4},{8,11},{9,10},{10,... | collective-permute-start | bytes 3538952 | tf_op jit(solution)/shard_map/ppermute | solution.py:188
  8.6 52.0 %collective-permute-start.6 = (bf16[6,128,768]{2,1,0:T(8,128)(2,1)S(1)}, bf16[6,128,768]{2,1,0:T(8,128)(2,1)S(1)}, u32[]{:S(2)}, u32[]{:S(2)}) collective-permute-start(bf16[6,128,768]{2,1,0:T(8,128)(2,1)S(1)} %pack.14), channel_id=1, source_target_pairs={{0,1},{1,0},{2,3},{3,2},{4,5},{5,4},{6,7},{7,6},{8,9},{9,8},{10,11... | collective-permute-start | bytes 3538952 | tf_op jit(solution)/shard_map/ppermute | solution.py:188
  10.0 115.9 %collective-permute-start.7 = (bf16[6,128,768]{2,1,0:T(8,128)(2,1)S(1)}, bf16[6,128,768]{2,1,0:T(8,128)(2,1)S(1)}, u32[]{:S(2)}, u32[]{:S(2)}) collective-permute-start(bf16[6,128,768]{2,1,0:T(8,128)(2,1)S(1)} %pack.15), channel_id=1, source_target_pairs={{0,2},{1,3},{2,0},{3,1},{4,6},{5,7},{6,4},{7,5},{8,10},{9,11},{10,... | collective-permute-start | bytes 3538952 | tf_op jit(solution)/shard_map/ppermute | solution.py:188
  11.7 130.1 %collective-permute-start.2 = (bf16[6,128,256]{2,1,0:T(8,128)(2,1)S(1)}, bf16[6,128,256]{2,1,0:T(8,128)(2,1)S(1)}, u32[]{:S(2)}, u32[]{:S(2)}) collective-permute-start(bf16[6,128,256]{2,1,0:T(8,128)(2,1)S(1)} %pack.8.refs_6_), channel_id=1, source_target_pairs={{0,3},{1,2},{2,1},{3,0},{4,7},{5,6},{6,5},{7,4},{8,11},{9,10},{10,... | collective-permute-start | bytes 1179656 | tf_op jit(solution)/shard_map/ppermute | solution.py:188
  16.7 127.0 %collective-permute-start = (bf16[6,128,256]{2,1,0:T(8,128)(2,1)S(1)}, bf16[6,128,256]{2,1,0:T(8,128)(2,1)S(1)}, u32[]{:S(2)}, u32[]{:S(2)}) collective-permute-start(bf16[6,128,256]{2,1,0:T(8,128)(2,1)S(1)} %pack.10), channel_id=1, source_target_pairs={{0,1},{1,0},{2,3},{3,2},{4,5},{5,4},{6,7},{7,6},{8,9},{9,8},{10,11... | collective-permute-start | bytes 1179656 | tf_op jit(solution)/shard_map/ppermute | solution.py:188
  34.0 125.1 %collective-permute-start.1 = (bf16[6,128,256]{2,1,0:T(8,128)(2,1)S(1)}, bf16[6,128,256]{2,1,0:T(8,128)(2,1)S(1)}, u32[]{:S(2)}, u32[]{:S(2)}) collective-permute-start(bf16[6,128,256]{2,1,0:T(8,128)(2,1)S(1)} %pack.11), channel_id=1, source_target_pairs={{0,2},{1,3},{2,0},{3,1},{4,6},{5,7},{6,4},{7,5},{8,10},{9,11},{10,... | collective-permute-start | bytes 1179656 | tf_op jit(solution)/shard_map/ppermute | solution.py:188
  139.0 30.5 %collective-permute-start.10 = (bf16[2,128,768]{2,1,0:T(8,128)(2,1)S(1)}, bf16[2,128,768]{2,1,0:T(8,128)(2,1)S(1)}, u32[]{:S(2)}, u32[]{:S(2)}) collective-permute-start(bf16[2,128,768]{2,1,0:T(8,128)(2,1)S(1)} %get-tuple-element.21), channel_id=1, source_target_pairs={{2,0},{3,1},{0,2},{1,3},{6,4},{7,5},{4,6},{5,7},{10,8},{11,9},{8,1... | collective-permute-start | bytes 1179656 | tf_op jit(solution)/shard_map/ppermute | solution.py:191
  139.1 33.8 %collective-permute-start.11 = (bf16[2,128,768]{2,1,0:T(8,128)(2,1)S(1)}, bf16[2,128,768]{2,1,0:T(8,128)(2,1)S(1)}, u32[]{:S(2)}, u32[]{:S(2)}) collective-permute-start(bf16[2,128,768]{2,1,0:T(8,128)(2,1)S(1)} %get-tuple-element.22), channel_id=1, source_target_pairs={{3,0},{2,1},{1,2},{0,3},{7,4},{6,5},{5,6},{4,7},{11,8},{10,9},{9,1... | collective-permute-start | bytes 1179656 | tf_op jit(solution)/shard_map/ppermute | solution.py:191
  141.9 31.1 %collective-permute-start.9 = (bf16[2,128,768]{2,1,0:T(8,128)(2,1)S(1)}, bf16[2,128,768]{2,1,0:T(8,128)(2,1)S(1)}, u32[]{:S(2)}, u32[]{:S(2)}) collective-permute-start(bf16[2,128,768]{2,1,0:T(8,128)(2,1)S(1)} %get-tuple-element.20), channel_id=1, source_target_pairs={{1,0},{0,1},{3,2},{2,3},{5,4},{4,5},{7,6},{6,7},{9,8},{8,9},{11,10... | collective-permute-start | bytes 1179656 | tf_op jit(solution)/shard_map/ppermute | solution.py:191
  163.5 11.2 %collective-permute-start.3 = (bf16[2,128,256]{2,1,0:T(8,128)(2,1)S(1)}, bf16[2,128,256]{2,1,0:T(8,128)(2,1)S(1)}, u32[]{:S(2)}, u32[]{:S(2)}) collective-permute-start(bf16[2,128,256]{2,1,0:T(8,128)(2,1)S(1)} %get-tuple-element.16), channel_id=1, source_target_pairs={{1,0},{0,1},{3,2},{2,3},{5,4},{4,5},{7,6},{6,7},{9,8},{8,9},{11,10... | collective-permute-start | bytes 393224 | tf_op jit(solution)/shard_map/ppermute | solution.py:191
  164.0 21.0 %collective-permute-start.4 = (bf16[2,128,256]{2,1,0:T(8,128)(2,1)S(1)}, bf16[2,128,256]{2,1,0:T(8,128)(2,1)S(1)}, u32[]{:S(2)}, u32[]{:S(2)}) collective-permute-start(bf16[2,128,256]{2,1,0:T(8,128)(2,1)S(1)} %get-tuple-element.17), channel_id=1, source_target_pairs={{2,0},{3,1},{0,2},{1,3},{6,4},{7,5},{4,6},{5,7},{10,8},{11,9},{8,1... | collective-permute-start | bytes 393224 | tf_op jit(solution)/shard_map/ppermute | solution.py:191
  169.5 15.5 %collective-permute-start.5 = (bf16[2,128,256]{2,1,0:T(8,128)(2,1)S(1)}, bf16[2,128,256]{2,1,0:T(8,128)(2,1)S(1)}, u32[]{:S(2)}, u32[]{:S(2)}) collective-permute-start(bf16[2,128,256]{2,1,0:T(8,128)(2,1)S(1)} %get-tuple-element.18), channel_id=1, source_target_pairs={{3,0},{2,1},{1,2},{0,3},{7,4},{6,5},{5,6},{4,7},{11,8},{10,9},{9,1... | collective-permute-start | bytes 393224 | tf_op jit(solution)/shard_map/ppermute | solution.py:191

commit v4 on v3

--- a/solution.py
+++ b/solution.py
@@ -19,7 +19,7 @@
 
 
 def chunk_sizes(count):
-    last = max(1, count // 4)
+    last = max(1, 3 * count // 8)
     return [count - last, last] if count > 1 else [count]
 
 
@@ -205,7 +205,8 @@
         own, *results = attend(messages)
         returned = [back(m, r) for r, m in enumerate(results)]
         outs = place(outs, [own], [own_group], span, base, shape)
-        outs = place(outs, returned, groups, span, base, shape)
+        for group, message in zip(groups, returned):
+            outs = place(outs, [message], [group], span, base, shape)
     return tuple(outs)
 
 

time: 186 us -> 185 us (level)
  starting transfers between devices: 46.4 us -> 41 us
  Pallas kernels: 30.6 us -> 33.4 us
  waiting for transfers between devices: 108 us -> 110 us
    ppermute x6, starting transfers between devices: 36.3 us -> 32.1 us  [there(): return lax.ppermute(message, 'seq', list(enumerate(rounds[r][1])))]
    ppermute x6, waiting for transfers between devices: 95.6 us -> 98.5 us  [there(): return lax.ppermute(message, 'seq', list(enumerate(rounds[r][1])))]
    pallas_call x4 -> x8, Pallas kernels: 3.29 us -> 5.78 us  [place(): pl.pallas_call(functools.partial(place_kernel, groups, span, base, width)...]
  transfers between devices with their start and end apart: 12 -> 12, of which waited for: 5 -> 4; matrix products, arithmetic and copies ran while one was open for 0% -> 0% of each run, Pallas kernels for 15% -> 17%
where the time goes in v4:
time: 185 us
  waiting for transfers between devices  110 us (59%)
  starting transfers between devices  41 us (22%)
  Pallas kernels  33.4 us (18%)
    ppermute x6, waiting for transfers between devices, there(): return lax.ppermute(message, 'seq', list(enumerate(rounds[r][1])))  98.5 us
    ppermute x6, starting transfers between devices, there(): return lax.ppermute(message, 'seq', list(enumerate(rounds[r][1])))  32.1 us
    pallas_call x2, Pallas kernels, attend(): pl.pallas_call(functools.partial(attend_kernel, layout), out_shape=[jax.S...  17.5 us
    ppermute x6, waiting for transfers between devices, back(): lax.ppermute(message, 'seq', [(b, a) for a, b in enumerate(rounds[r][1])])  11.2 us
    pallas_call x8, Pallas kernels, pack(): pl.pallas_call(functools.partial(pack_kernel, groups, count, span, base,...  10.1 us
    ppermute x6, starting transfers between devices, back(): lax.ppermute(message, 'seq', [(b, a) for a, b in enumerate(rounds[r][1])])  8.89 us
    pallas_call x8, Pallas kernels, place(): pl.pallas_call(functools.partial(place_kernel, groups, span, base, width)...  5.78 us
  transfers between devices with their start and end apart: 12, of which 4 were waited for; matrix products, arithmetic and copies ran while one was open for 0% of the time, Pallas kernels for 17%

profile of v4, /device:TPU:0, one launch (start us, length us, event | category | flops | bytes accessed | tf_op | source)
XLA Modules:
  0.0 184.9 jit_solution(4817568799742770966)
XLA Ops:
  0.6 1.4 pack.12.refs_6_
  2.0 5.1 %collective-permute-start.8 = (bf16[6,128,640]{2,1,0:T(8,128)(2,1)S(1)}, bf16[6,128,640]{2,1,0:T(8,128)(2,1)S(1)}, u32[]{:S(2)}, u32[]{:S(2)}) collective-permute-start(bf16[6,128,640]{2,1,0:T(8,128)(2,1)S(1)} %pack.12.refs_6_), channel_id=1, source_target_pairs={{0,3},{1,2},{2,1},{3,0},{4,7},{5,6},{6,5},{7,4},{8,11},{9,10},{10,... | collective-permute-start | bytes 2949128 | tf_op jit(solution)/shard_map/ppermute | solution.py:188
  7.1 1.3 pack.14
  8.5 0.1 collective-permute-start.6
  8.5 1.4 pack.15
  9.9 0.6 collective-permute-start.7
  10.5 1.2 pack.8.refs_6_
  11.7 3.9 %collective-permute-start.2 = (bf16[6,128,384]{2,1,0:T(8,128)(2,1)S(1)}, bf16[6,128,384]{2,1,0:T(8,128)(2,1)S(1)}, u32[]{:S(2)}, u32[]{:S(2)}) collective-permute-start(bf16[6,128,384]{2,1,0:T(8,128)(2,1)S(1)} %pack.8.refs_6_), channel_id=1, source_target_pairs={{0,3},{1,2},{2,1},{3,0},{4,7},{5,6},{6,5},{7,4},{8,11},{9,10},{10,... | collective-permute-start | bytes 1769480 | tf_op jit(solution)/shard_map/ppermute | solution.py:188
  15.6 1.2 pack.10
  16.8 0.1 collective-permute-start
  16.9 1.2 pack.11
  18.1 11.7 %collective-permute-done.8.refs_3_ = bf16[6,128,640]{2,1,0:T(8,128)(2,1)S(1)} collective-permute-done((bf16[6,128,640]{2,1,0:T(8,128)(2,1)S(1)}, bf16[6,128,640]{2,1,0:T(8,128)(2,1)S(1)}, u32[]{:S(2)}, u32[]{:S(2)}) %collective-permute-start.8) | collective-permute-done | bytes 983072 | tf_op jit(solution)/shard_map/ppermute | solution.py:188
  29.8 22.3 %collective-permute-start.1 = (bf16[6,128,384]{2,1,0:T(8,128)(2,1)S(1)}, bf16[6,128,384]{2,1,0:T(8,128)(2,1)S(1)}, u32[]{:S(2)}, u32[]{:S(2)}) collective-permute-start(bf16[6,128,384]{2,1,0:T(8,128)(2,1)S(1)} %pack.11), channel_id=1, source_target_pairs={{0,2},{1,3},{2,0},{3,1},{4,6},{5,7},{6,4},{7,5},{8,10},{9,11},{10,... | collective-permute-start | bytes 1769480 | tf_op jit(solution)/shard_map/ppermute | solution.py:188
  52.1 1.3 pack.13.refs_0_
  53.4 0.0 collective-permute-done.6.refs_1_
  53.5 64.0 %collective-permute-done.7.refs_2_ = bf16[6,128,640]{2,1,0:T(8,128)(2,1)S(1)} collective-permute-done((bf16[6,128,640]{2,1,0:T(8,128)(2,1)S(1)}, bf16[6,128,640]{2,1,0:T(8,128)(2,1)S(1)}, u32[]{:S(2)}, u32[]{:S(2)}) %collective-permute-start.7) | collective-permute-done | bytes 983072 | tf_op jit(solution)/shard_map/ppermute | solution.py:188
  117.5 10.9 %attend.3 = (bf16[2,128,640]{2,1,0:T(8,128)(2,1)S(1)}, bf16[2,128,640]{2,1,0:T(8,128)(2,1)S(1)}, bf16[2,128,640]{2,1,0:T(8,128)(2,1)S(1)}, bf16[2,128,640]{2,1,0:T(8,128)(2,1)S(1)}) custom-call(bf16[6,128,640]{2,1,0:T(8,128)(2,1)S(1)} %pack.13.refs_0_, bf16[6,128,640]{2,1,0:T(8,128)(2,1)S(1)} %collective-permute-done.6.refs_1_, ...), custom_call_target="tpu_custom_call" | custom-call | flops 2013265920 | bytes 5242880 | tf_op jit(solution)/shard_map/attend/pallas_call | solution.py:162
  128.4 0.1 collective-permute-start.11
  128.5 3.2 %collective-permute-start.10 = (bf16[2,128,640]{2,1,0:T(8,128)(2,1)S(1)}, bf16[2,128,640]{2,1,0:T(8,128)(2,1)S(1)}, u32[]{:S(2)}, u32[]{:S(2)}) collective-permute-start(bf16[2,128,640]{2,1,0:T(8,128)(2,1)S(1)} %get-tuple-element.29), channel_id=1, source_target_pairs={{2,0},{3,1},{0,2},{1,3},{6,4},{7,5},{4,6},{5,7},{10,8},{11,9},{8,1... | collective-permute-start | bytes 983048 | tf_op jit(solution)/shard_map/ppermute | solution.py:191
  131.7 0.0 collective-permute-done.2.refs_3_
  131.7 1.2 collective-permute-start.9
  132.8 1.2 pack.9.refs_0_
  134.0 0.0 collective-permute-done.refs_1_
  134.1 22.8 %collective-permute-done.1.refs_2_ = bf16[6,128,384]{2,1,0:T(8,128)(2,1)S(1)} collective-permute-done((bf16[6,128,384]{2,1,0:T(8,128)(2,1)S(1)}, bf16[6,128,384]{2,1,0:T(8,128)(2,1)S(1)}, u32[]{:S(2)}, u32[]{:S(2)}) %collective-permute-start.1) | collective-permute-done | bytes 589856 | tf_op jit(solution)/shard_map/ppermute | solution.py:188
  156.8 6.6 %attend.2 = (bf16[2,128,384]{2,1,0:T(8,128)(2,1)S(1)}, bf16[2,128,384]{2,1,0:T(8,128)(2,1)S(1)}, bf16[2,128,384]{2,1,0:T(8,128)(2,1)S(1)}, bf16[2,128,384]{2,1,0:T(8,128)(2,1)S(1)}) custom-call(bf16[6,128,384]{2,1,0:T(8,128)(2,1)S(1)} %pack.9.refs_0_, bf16[6,128,384]{2,1,0:T(8,128)(2,1)S(1)} %collective-permute-done.refs_1_, ...), custom_call_target="tpu_custom_call" | custom-call | flops 1207959552 | bytes 3145728 | tf_op jit(solution)/shard_map/attend/pallas_call | solution.py:162
  163.4 0.1 collective-permute-start.5
  163.5 3.2 %collective-permute-start.4 = (bf16[2,128,384]{2,1,0:T(8,128)(2,1)S(1)}, bf16[2,128,384]{2,1,0:T(8,128)(2,1)S(1)}, u32[]{:S(2)}, u32[]{:S(2)}) collective-permute-start(bf16[2,128,384]{2,1,0:T(8,128)(2,1)S(1)} %get-tuple-element.25), channel_id=1, source_target_pairs={{2,0},{3,1},{0,2},{1,3},{6,4},{7,5},{4,6},{5,7},{10,8},{11,9},{8,1... | collective-permute-start | bytes 589832 | tf_op jit(solution)/shard_map/ppermute | solution.py:191
  166.7 0.0 collective-permute-done.11.refs_0_
  166.7 1.2 collective-permute-start.3
  167.8 0.7 place.8
  168.6 0.8 place.9
  169.4 0.0 collective-permute-done.10.refs_0_
  169.4 0.8 place.10
  170.1 0.0 collective-permute-done.9.refs_0_
  170.1 0.8 place.11
  170.9 0.7 place.12
  171.6 0.0 collective-permute-done.5.refs_0_
  171.6 0.7 place.13
  172.3 11.2 %collective-permute-done.4.refs_0_ = bf16[2,128,384]{2,1,0:T(8,128)(2,1)S(1)} collective-permute-done((bf16[2,128,384]{2,1,0:T(8,128)(2,1)S(1)}, bf16[2,128,384]{2,1,0:T(8,128)(2,1)S(1)}, u32[]{:S(2)}, u32[]{:S(2)}) %collective-permute-start.4) | collective-permute-done | bytes 196640 | tf_op jit(solution)/shard_map/ppermute | solution.py:191
  183.5 0.7 place.14
  184.2 0.0 collective-permute-done.3.refs_0_
  184.2 0.7 place.15
Async XLA Ops:
  2.0 27.8 %collective-permute-start.8 = (bf16[6,128,640]{2,1,0:T(8,128)(2,1)S(1)}, bf16[6,128,640]{2,1,0:T(8,128)(2,1)S(1)}, u32[]{:S(2)}, u32[]{:S(2)}) collective-permute-start(bf16[6,128,640]{2,1,0:T(8,128)(2,1)S(1)} %pack.12.refs_6_), channel_id=1, source_target_pairs={{0,3},{1,2},{2,1},{3,0},{4,7},{5,6},{6,5},{7,4},{8,11},{9,10},{10,... | collective-permute-start | bytes 2949128 | tf_op jit(solution)/shard_map/ppermute | solution.py:188
  8.5 45.0 %collective-permute-start.6 = (bf16[6,128,640]{2,1,0:T(8,128)(2,1)S(1)}, bf16[6,128,640]{2,1,0:T(8,128)(2,1)S(1)}, u32[]{:S(2)}, u32[]{:S(2)}) collective-permute-start(bf16[6,128,640]{2,1,0:T(8,128)(2,1)S(1)} %pack.14), channel_id=1, source_target_pairs={{0,1},{1,0},{2,3},{3,2},{4,5},{5,4},{6,7},{7,6},{8,9},{9,8},{10,11... | collective-permute-start | bytes 2949128 | tf_op jit(solution)/shard_map/ppermute | solution.py:188
  9.9 107.6 %collective-permute-start.7 = (bf16[6,128,640]{2,1,0:T(8,128)(2,1)S(1)}, bf16[6,128,640]{2,1,0:T(8,128)(2,1)S(1)}, u32[]{:S(2)}, u32[]{:S(2)}) collective-permute-start(bf16[6,128,640]{2,1,0:T(8,128)(2,1)S(1)} %pack.15), channel_id=1, source_target_pairs={{0,2},{1,3},{2,0},{3,1},{4,6},{5,7},{6,4},{7,5},{8,10},{9,11},{10,... | collective-permute-start | bytes 2949128 | tf_op jit(solution)/shard_map/ppermute | solution.py:188
  11.7 120.0 %collective-permute-start.2 = (bf16[6,128,384]{2,1,0:T(8,128)(2,1)S(1)}, bf16[6,128,384]{2,1,0:T(8,128)(2,1)S(1)}, u32[]{:S(2)}, u32[]{:S(2)}) collective-permute-start(bf16[6,128,384]{2,1,0:T(8,128)(2,1)S(1)} %pack.8.refs_6_), channel_id=1, source_target_pairs={{0,3},{1,2},{2,1},{3,0},{4,7},{5,6},{6,5},{7,4},{8,11},{9,10},{10,... | collective-permute-start | bytes 1769480 | tf_op jit(solution)/shard_map/ppermute | solution.py:188
  16.8 117.3 %collective-permute-start = (bf16[6,128,384]{2,1,0:T(8,128)(2,1)S(1)}, bf16[6,128,384]{2,1,0:T(8,128)(2,1)S(1)}, u32[]{:S(2)}, u32[]{:S(2)}) collective-permute-start(bf16[6,128,384]{2,1,0:T(8,128)(2,1)S(1)} %pack.10), channel_id=1, source_target_pairs={{0,1},{1,0},{2,3},{3,2},{4,5},{5,4},{6,7},{7,6},{8,9},{9,8},{10,11... | collective-permute-start | bytes 1769480 | tf_op jit(solution)/shard_map/ppermute | solution.py:188
  29.8 127.0 %collective-permute-start.1 = (bf16[6,128,384]{2,1,0:T(8,128)(2,1)S(1)}, bf16[6,128,384]{2,1,0:T(8,128)(2,1)S(1)}, u32[]{:S(2)}, u32[]{:S(2)}) collective-permute-start(bf16[6,128,384]{2,1,0:T(8,128)(2,1)S(1)} %pack.11), channel_id=1, source_target_pairs={{0,2},{1,3},{2,0},{3,1},{4,6},{5,7},{6,4},{7,5},{8,10},{9,11},{10,... | collective-permute-start | bytes 1769480 | tf_op jit(solution)/shard_map/ppermute | solution.py:188
  128.4 38.3 %collective-permute-start.11 = (bf16[2,128,640]{2,1,0:T(8,128)(2,1)S(1)}, bf16[2,128,640]{2,1,0:T(8,128)(2,1)S(1)}, u32[]{:S(2)}, u32[]{:S(2)}) collective-permute-start(bf16[2,128,640]{2,1,0:T(8,128)(2,1)S(1)} %get-tuple-element.30), channel_id=1, source_target_pairs={{1,0},{0,1},{3,2},{2,3},{5,4},{4,5},{7,6},{6,7},{9,8},{8,9},{11,10... | collective-permute-start | bytes 983048 | tf_op jit(solution)/shard_map/ppermute | solution.py:191
  128.5 40.9 %collective-permute-start.10 = (bf16[2,128,640]{2,1,0:T(8,128)(2,1)S(1)}, bf16[2,128,640]{2,1,0:T(8,128)(2,1)S(1)}, u32[]{:S(2)}, u32[]{:S(2)}) collective-permute-start(bf16[2,128,640]{2,1,0:T(8,128)(2,1)S(1)} %get-tuple-element.29), channel_id=1, source_target_pairs={{2,0},{3,1},{0,2},{1,3},{6,4},{7,5},{4,6},{5,7},{10,8},{11,9},{8,1... | collective-permute-start | bytes 983048 | tf_op jit(solution)/shard_map/ppermute | solution.py:191
  131.7 38.4 %collective-permute-start.9 = (bf16[2,128,640]{2,1,0:T(8,128)(2,1)S(1)}, bf16[2,128,640]{2,1,0:T(8,128)(2,1)S(1)}, u32[]{:S(2)}, u32[]{:S(2)}) collective-permute-start(bf16[2,128,640]{2,1,0:T(8,128)(2,1)S(1)} %get-tuple-element.28), channel_id=1, source_target_pairs={{3,0},{2,1},{1,2},{0,3},{7,4},{6,5},{5,6},{4,7},{11,8},{10,9},{9,1... | collective-permute-start | bytes 983048 | tf_op jit(solution)/shard_map/ppermute | solution.py:191
  163.4 8.2 %collective-permute-start.5 = (bf16[2,128,384]{2,1,0:T(8,128)(2,1)S(1)}, bf16[2,128,384]{2,1,0:T(8,128)(2,1)S(1)}, u32[]{:S(2)}, u32[]{:S(2)}) collective-permute-start(bf16[2,128,384]{2,1,0:T(8,128)(2,1)S(1)} %get-tuple-element.26), channel_id=1, source_target_pairs={{1,0},{0,1},{3,2},{2,3},{5,4},{4,5},{7,6},{6,7},{9,8},{8,9},{11,10... | collective-permute-start | bytes 589832 | tf_op jit(solution)/shard_map/ppermute | solution.py:191
  163.5 20.0 %collective-permute-start.4 = (bf16[2,128,384]{2,1,0:T(8,128)(2,1)S(1)}, bf16[2,128,384]{2,1,0:T(8,128)(2,1)S(1)}, u32[]{:S(2)}, u32[]{:S(2)}) collective-permute-start(bf16[2,128,384]{2,1,0:T(8,128)(2,1)S(1)} %get-tuple-element.25), channel_id=1, source_target_pairs={{2,0},{3,1},{0,2},{1,3},{6,4},{7,5},{4,6},{5,7},{10,8},{11,9},{8,1... | collective-permute-start | bytes 589832 | tf_op jit(solution)/shard_map/ppermute | solution.py:191
  166.7 17.5 %collective-permute-start.3 = (bf16[2,128,384]{2,1,0:T(8,128)(2,1)S(1)}, bf16[2,128,384]{2,1,0:T(8,128)(2,1)S(1)}, u32[]{:S(2)}, u32[]{:S(2)}) collective-permute-start(bf16[2,128,384]{2,1,0:T(8,128)(2,1)S(1)} %get-tuple-element.24), channel_id=1, source_target_pairs={{3,0},{2,1},{1,2},{0,3},{7,4},{6,5},{5,6},{4,7},{11,8},{10,9},{9,1... | collective-permute-start | bytes 589832 | tf_op jit(solution)/shard_map/ppermute | solution.py:191

commit v5 on v4

--- a/solution.py
+++ b/solution.py
@@ -24,9 +24,17 @@
 
 
 def rounds_of(count):
-    if count & (count - 1) == 0:
+    if count & (count - 1) == 0 and count > 2:
+        half = count // 2
+
+        def partner(step, me):
+            return me ^ step if step < half else me ^ step ^ lax.div(me, half)
+
+        def static(step, i):
+            return i ^ step if step < half else i ^ step ^ (i // half)
+
         return [
-            (lambda me, step=step: me ^ step, [i ^ step for i in range(count)])
+            (functools.partial(partner, step), [static(step, i) for i in range(count)])
             for step in range(1, count)
         ]
     return [

time: 185 us -> 185 us (level)
  waiting for transfers between devices: 110 us -> 65.8 us
  starting transfers between devices: 41 us -> 84.6 us
    ppermute x6, starting transfers between devices: 8.89 us -> 73.8 us  [back(): lax.ppermute(message, 'seq', [(b, a) for a, b in enumerate(rounds[r][1])])]
    ppermute x6, waiting for transfers between devices: 98.5 us -> 53.7 us  [there(): return lax.ppermute(message, 'seq', list(enumerate(rounds[r][1])))]
    ppermute x6, starting transfers between devices: 32.1 us -> 10.8 us  [there(): return lax.ppermute(message, 'seq', list(enumerate(rounds[r][1])))]
  transfers between devices with their start and end apart: 12 -> 12, of which waited for: 4 -> 3; matrix products, arithmetic and copies ran while one was open for 0% -> 0% of each run, Pallas kernels for 17% -> 17%
where the time goes in v5:
time: 185 us
  starting transfers between devices  84.6 us (46%)
  waiting for transfers between devices  65.8 us (36%)
  Pallas kernels  33.4 us (18%)
    ppermute x6, starting transfers between devices, back(): lax.ppermute(message, 'seq', [(b, a) for a, b in enumerate(rounds[r][1])])  73.8 us
    ppermute x6, waiting for transfers between devices, there(): return lax.ppermute(message, 'seq', list(enumerate(rounds[r][1])))  53.7 us
    pallas_call x2, Pallas kernels, attend(): pl.pallas_call(functools.partial(attend_kernel, layout), out_shape=[jax.S...  17.5 us
    ppermute x6, waiting for transfers between devices, back(): lax.ppermute(message, 'seq', [(b, a) for a, b in enumerate(rounds[r][1])])  12.1 us
    ppermute x6, starting transfers between devices, there(): return lax.ppermute(message, 'seq', list(enumerate(rounds[r][1])))  10.8 us
    pallas_call x8, Pallas kernels, pack(): pl.pallas_call(functools.partial(pack_kernel, groups, count, span, base,...  10.1 us
    pallas_call x8, Pallas kernels, place(): pl.pallas_call(functools.partial(place_kernel, groups, span, base, width)...  5.79 us
  transfers between devices with their start and end apart: 12, of which 3 were waited for; matrix products, arithmetic and copies ran while one was open for 0% of the time, Pallas kernels for 17%

profile of v5, /device:TPU:0, one launch (start us, length us, event | category | flops | bytes accessed | tf_op | source)
XLA Modules:
  0.0 184.6 jit_solution(8825302148363424965)
XLA Ops:
  0.6 1.4 pack.12.refs_6_
  2.0 5.1 %collective-permute-start.8 = (bf16[6,128,640]{2,1,0:T(8,128)(2,1)S(1)}, bf16[6,128,640]{2,1,0:T(8,128)(2,1)S(1)}, u32[]{:S(2)}, u32[]{:S(2)}) collective-permute-start(bf16[6,128,640]{2,1,0:T(8,128)(2,1)S(1)} %pack.12.refs_6_), channel_id=1, source_target_pairs={{0,3},{1,2},{2,0},{3,1},{4,7},{5,6},{6,4},{7,5},{8,11},{9,10},{10,... | collective-permute-start | bytes 2949128 | tf_op jit(solution)/shard_map/ppermute | solution.py:196
  7.1 1.3 pack.14
  8.4 0.1 collective-permute-start.6
  8.5 1.4 pack.15
  9.9 0.9 collective-permute-start.7
  10.8 1.2 pack.8.refs_6_
  12.0 3.0 %collective-permute-start.2 = (bf16[6,128,384]{2,1,0:T(8,128)(2,1)S(1)}, bf16[6,128,384]{2,1,0:T(8,128)(2,1)S(1)}, u32[]{:S(2)}, u32[]{:S(2)}) collective-permute-start(bf16[6,128,384]{2,1,0:T(8,128)(2,1)S(1)} %pack.8.refs_6_), channel_id=1, source_target_pairs={{0,3},{1,2},{2,0},{3,1},{4,7},{5,6},{6,4},{7,5},{8,11},{9,10},{10,... | collective-permute-start | bytes 1769480 | tf_op jit(solution)/shard_map/ppermute | solution.py:196
  15.0 1.2 pack.10
  16.2 0.3 collective-permute-start
  16.5 1.2 pack.11
  17.7 33.0 %collective-permute-done.8.refs_3_ = bf16[6,128,640]{2,1,0:T(8,128)(2,1)S(1)} collective-permute-done((bf16[6,128,640]{2,1,0:T(8,128)(2,1)S(1)}, bf16[6,128,640]{2,1,0:T(8,128)(2,1)S(1)}, u32[]{:S(2)}, u32[]{:S(2)}) %collective-permute-start.8) | collective-permute-done | bytes 983072 | tf_op jit(solution)/shard_map/ppermute | solution.py:196
  50.6 1.4 collective-permute-start.1
  52.1 1.3 pack.13.refs_0_
  53.4 20.7 %collective-permute-done.6.refs_1_ = bf16[6,128,640]{2,1,0:T(8,128)(2,1)S(1)} collective-permute-done((bf16[6,128,640]{2,1,0:T(8,128)(2,1)S(1)}, bf16[6,128,640]{2,1,0:T(8,128)(2,1)S(1)}, u32[]{:S(2)}, u32[]{:S(2)}) %collective-permute-start.6) | collective-permute-done | bytes 983072 | tf_op jit(solution)/shard_map/ppermute | solution.py:196
  74.2 0.0 collective-permute-done.7.refs_2_
  74.2 10.9 %attend.3 = (bf16[2,128,640]{2,1,0:T(8,128)(2,1)S(1)}, bf16[2,128,640]{2,1,0:T(8,128)(2,1)S(1)}, bf16[2,128,640]{2,1,0:T(8,128)(2,1)S(1)}, bf16[2,128,640]{2,1,0:T(8,128)(2,1)S(1)}) custom-call(bf16[6,128,640]{2,1,0:T(8,128)(2,1)S(1)} %pack.13.refs_0_, bf16[6,128,640]{2,1,0:T(8,128)(2,1)S(1)} %collective-permute-done.6.refs_1_, ...), custom_call_target="tpu_custom_call" | custom-call | flops 2013265920 | bytes 5242880 | tf_op jit(solution)/shard_map/attend/pallas_call | solution.py:170
  85.1 43.7 %collective-permute-start.11 = (bf16[2,128,640]{2,1,0:T(8,128)(2,1)S(1)}, bf16[2,128,640]{2,1,0:T(8,128)(2,1)S(1)}, u32[]{:S(2)}, u32[]{:S(2)}) collective-permute-start(bf16[2,128,640]{2,1,0:T(8,128)(2,1)S(1)} %get-tuple-element.30), channel_id=1, source_target_pairs={{1,0},{0,1},{3,2},{2,3},{5,4},{4,5},{7,6},{6,7},{9,8},{8,9},{11,10... | collective-permute-start | bytes 983048 | tf_op jit(solution)/shard_map/ppermute | solution.py:199
  128.8 2.4 %collective-permute-start.10 = (bf16[2,128,640]{2,1,0:T(8,128)(2,1)S(1)}, bf16[2,128,640]{2,1,0:T(8,128)(2,1)S(1)}, u32[]{:S(2)}, u32[]{:S(2)}) collective-permute-start(bf16[2,128,640]{2,1,0:T(8,128)(2,1)S(1)} %get-tuple-element.29), channel_id=1, source_target_pairs={{2,0},{3,1},{1,2},{0,3},{6,4},{7,5},{5,6},{4,7},{10,8},{11,9},{9,1... | collective-permute-start | bytes 983048 | tf_op jit(solution)/shard_map/ppermute | solution.py:199
  131.2 0.0 collective-permute-done.2.refs_3_
  131.2 0.7 collective-permute-start.9
  131.8 1.2 pack.9.refs_0_
  133.0 0.0 collective-permute-done.refs_1_
  133.0 0.0 collective-permute-done.1.refs_2_
  133.1 6.6 %attend.2 = (bf16[2,128,384]{2,1,0:T(8,128)(2,1)S(1)}, bf16[2,128,384]{2,1,0:T(8,128)(2,1)S(1)}, bf16[2,128,384]{2,1,0:T(8,128)(2,1)S(1)}, bf16[2,128,384]{2,1,0:T(8,128)(2,1)S(1)}) custom-call(bf16[6,128,384]{2,1,0:T(8,128)(2,1)S(1)} %pack.9.refs_0_, bf16[6,128,384]{2,1,0:T(8,128)(2,1)S(1)} %collective-permute-done.refs_1_, ...), custom_call_target="tpu_custom_call" | custom-call | flops 1207959552 | bytes 3145728 | tf_op jit(solution)/shard_map/attend/pallas_call | solution.py:170
  139.7 24.1 %collective-permute-start.5 = (bf16[2,128,384]{2,1,0:T(8,128)(2,1)S(1)}, bf16[2,128,384]{2,1,0:T(8,128)(2,1)S(1)}, u32[]{:S(2)}, u32[]{:S(2)}) collective-permute-start(bf16[2,128,384]{2,1,0:T(8,128)(2,1)S(1)} %get-tuple-element.26), channel_id=1, source_target_pairs={{1,0},{0,1},{3,2},{2,3},{5,4},{4,5},{7,6},{6,7},{9,8},{8,9},{11,10... | collective-permute-start | bytes 589832 | tf_op jit(solution)/shard_map/ppermute | solution.py:199
  163.7 2.5 %collective-permute-start.4 = (bf16[2,128,384]{2,1,0:T(8,128)(2,1)S(1)}, bf16[2,128,384]{2,1,0:T(8,128)(2,1)S(1)}, u32[]{:S(2)}, u32[]{:S(2)}) collective-permute-start(bf16[2,128,384]{2,1,0:T(8,128)(2,1)S(1)} %get-tuple-element.25), channel_id=1, source_target_pairs={{2,0},{3,1},{1,2},{0,3},{6,4},{7,5},{5,6},{4,7},{10,8},{11,9},{9,1... | collective-permute-start | bytes 589832 | tf_op jit(solution)/shard_map/ppermute | solution.py:199
  166.2 0.0 collective-permute-done.11.refs_0_
  166.2 0.5 collective-permute-start.3
  166.7 0.7 place.8
  167.4 0.8 place.9
  168.2 0.0 collective-permute-done.10.refs_0_
  168.2 0.8 place.10
  169.0 0.0 collective-permute-done.9.refs_0_
  169.0 0.8 place.11
  169.7 0.7 place.12
  170.4 0.0 collective-permute-done.5.refs_0_
  170.4 0.7 place.13
  171.2 12.0 %collective-permute-done.4.refs_0_ = bf16[2,128,384]{2,1,0:T(8,128)(2,1)S(1)} collective-permute-done((bf16[2,128,384]{2,1,0:T(8,128)(2,1)S(1)}, bf16[2,128,384]{2,1,0:T(8,128)(2,1)S(1)}, u32[]{:S(2)}, u32[]{:S(2)}) %collective-permute-start.4) | collective-permute-done | bytes 196640 | tf_op jit(solution)/shard_map/ppermute | solution.py:199
  183.2 0.7 place.14
  183.9 0.0 collective-permute-done.3.refs_0_
  183.9 0.7 place.15
Async XLA Ops:
  2.0 48.7 %collective-permute-start.8 = (bf16[6,128,640]{2,1,0:T(8,128)(2,1)S(1)}, bf16[6,128,640]{2,1,0:T(8,128)(2,1)S(1)}, u32[]{:S(2)}, u32[]{:S(2)}) collective-permute-start(bf16[6,128,640]{2,1,0:T(8,128)(2,1)S(1)} %pack.12.refs_6_), channel_id=1, source_target_pairs={{0,3},{1,2},{2,0},{3,1},{4,7},{5,6},{6,4},{7,5},{8,11},{9,10},{10,... | collective-permute-start | bytes 2949128 | tf_op jit(solution)/shard_map/ppermute | solution.py:196
  8.4 65.7 %collective-permute-start.6 = (bf16[6,128,640]{2,1,0:T(8,128)(2,1)S(1)}, bf16[6,128,640]{2,1,0:T(8,128)(2,1)S(1)}, u32[]{:S(2)}, u32[]{:S(2)}) collective-permute-start(bf16[6,128,640]{2,1,0:T(8,128)(2,1)S(1)} %pack.14), channel_id=1, source_target_pairs={{0,1},{1,0},{2,3},{3,2},{4,5},{5,4},{6,7},{7,6},{8,9},{9,8},{10,11... | collective-permute-start | bytes 2949128 | tf_op jit(solution)/shard_map/ppermute | solution.py:196
  9.9 64.3 %collective-permute-start.7 = (bf16[6,128,640]{2,1,0:T(8,128)(2,1)S(1)}, bf16[6,128,640]{2,1,0:T(8,128)(2,1)S(1)}, u32[]{:S(2)}, u32[]{:S(2)}) collective-permute-start(bf16[6,128,640]{2,1,0:T(8,128)(2,1)S(1)} %pack.15), channel_id=1, source_target_pairs={{0,2},{1,3},{2,1},{3,0},{4,6},{5,7},{6,5},{7,4},{8,10},{9,11},{10,... | collective-permute-start | bytes 2949128 | tf_op jit(solution)/shard_map/ppermute | solution.py:196
  12.0 119.2 %collective-permute-start.2 = (bf16[6,128,384]{2,1,0:T(8,128)(2,1)S(1)}, bf16[6,128,384]{2,1,0:T(8,128)(2,1)S(1)}, u32[]{:S(2)}, u32[]{:S(2)}) collective-permute-start(bf16[6,128,384]{2,1,0:T(8,128)(2,1)S(1)} %pack.8.refs_6_), channel_id=1, source_target_pairs={{0,3},{1,2},{2,0},{3,1},{4,7},{5,6},{6,4},{7,5},{8,11},{9,10},{10,... | collective-permute-start | bytes 1769480 | tf_op jit(solution)/shard_map/ppermute | solution.py:196
  16.2 116.8 %collective-permute-start = (bf16[6,128,384]{2,1,0:T(8,128)(2,1)S(1)}, bf16[6,128,384]{2,1,0:T(8,128)(2,1)S(1)}, u32[]{:S(2)}, u32[]{:S(2)}) collective-permute-start(bf16[6,128,384]{2,1,0:T(8,128)(2,1)S(1)} %pack.10), channel_id=1, source_target_pairs={{0,1},{1,0},{2,3},{3,2},{4,5},{5,4},{6,7},{7,6},{8,9},{9,8},{10,11... | collective-permute-start | bytes 1769480 | tf_op jit(solution)/shard_map/ppermute | solution.py:196
  50.6 82.4 %collective-permute-start.1 = (bf16[6,128,384]{2,1,0:T(8,128)(2,1)S(1)}, bf16[6,128,384]{2,1,0:T(8,128)(2,1)S(1)}, u32[]{:S(2)}, u32[]{:S(2)}) collective-permute-start(bf16[6,128,384]{2,1,0:T(8,128)(2,1)S(1)} %pack.11), channel_id=1, source_target_pairs={{0,2},{1,3},{2,1},{3,0},{4,6},{5,7},{6,5},{7,4},{8,10},{9,11},{10,... | collective-permute-start | bytes 1769480 | tf_op jit(solution)/shard_map/ppermute | solution.py:196
  85.1 81.1 %collective-permute-start.11 = (bf16[2,128,640]{2,1,0:T(8,128)(2,1)S(1)}, bf16[2,128,640]{2,1,0:T(8,128)(2,1)S(1)}, u32[]{:S(2)}, u32[]{:S(2)}) collective-permute-start(bf16[2,128,640]{2,1,0:T(8,128)(2,1)S(1)} %get-tuple-element.30), channel_id=1, source_target_pairs={{1,0},{0,1},{3,2},{2,3},{5,4},{4,5},{7,6},{6,7},{9,8},{8,9},{11,10... | collective-permute-start | bytes 983048 | tf_op jit(solution)/shard_map/ppermute | solution.py:199
  128.8 39.4 %collective-permute-start.10 = (bf16[2,128,640]{2,1,0:T(8,128)(2,1)S(1)}, bf16[2,128,640]{2,1,0:T(8,128)(2,1)S(1)}, u32[]{:S(2)}, u32[]{:S(2)}) collective-permute-start(bf16[2,128,640]{2,1,0:T(8,128)(2,1)S(1)} %get-tuple-element.29), channel_id=1, source_target_pairs={{2,0},{3,1},{1,2},{0,3},{6,4},{7,5},{5,6},{4,7},{10,8},{11,9},{9,1... | collective-permute-start | bytes 983048 | tf_op jit(solution)/shard_map/ppermute | solution.py:199
  131.2 37.8 %collective-permute-start.9 = (bf16[2,128,640]{2,1,0:T(8,128)(2,1)S(1)}, bf16[2,128,640]{2,1,0:T(8,128)(2,1)S(1)}, u32[]{:S(2)}, u32[]{:S(2)}) collective-permute-start(bf16[2,128,640]{2,1,0:T(8,128)(2,1)S(1)} %get-tuple-element.28), channel_id=1, source_target_pairs={{3,0},{2,1},{0,2},{1,3},{7,4},{6,5},{4,6},{5,7},{11,8},{10,9},{8,1... | collective-permute-start | bytes 983048 | tf_op jit(solution)/shard_map/ppermute | solution.py:199
  139.7 30.8 %collective-permute-start.5 = (bf16[2,128,384]{2,1,0:T(8,128)(2,1)S(1)}, bf16[2,128,384]{2,1,0:T(8,128)(2,1)S(1)}, u32[]{:S(2)}, u32[]{:S(2)}) collective-permute-start(bf16[2,128,384]{2,1,0:T(8,128)(2,1)S(1)} %get-tuple-element.26), channel_id=1, source_target_pairs={{1,0},{0,1},{3,2},{2,3},{5,4},{4,5},{7,6},{6,7},{9,8},{8,9},{11,10... | collective-permute-start | bytes 589832 | tf_op jit(solution)/shard_map/ppermute | solution.py:199
  163.7 19.5 %collective-permute-start.4 = (bf16[2,128,384]{2,1,0:T(8,128)(2,1)S(1)}, bf16[2,128,384]{2,1,0:T(8,128)(2,1)S(1)}, u32[]{:S(2)}, u32[]{:S(2)}) collective-permute-start(bf16[2,128,384]{2,1,0:T(8,128)(2,1)S(1)} %get-tuple-element.25), channel_id=1, source_target_pairs={{2,0},{3,1},{1,2},{0,3},{6,4},{7,5},{5,6},{4,7},{10,8},{11,9},{9,1... | collective-permute-start | bytes 589832 | tf_op jit(solution)/shard_map/ppermute | solution.py:199
  166.2 17.7 %collective-permute-start.3 = (bf16[2,128,384]{2,1,0:T(8,128)(2,1)S(1)}, bf16[2,128,384]{2,1,0:T(8,128)(2,1)S(1)}, u32[]{:S(2)}, u32[]{:S(2)}) collective-permute-start(bf16[2,128,384]{2,1,0:T(8,128)(2,1)S(1)} %get-tuple-element.24), channel_id=1, source_target_pairs={{3,0},{2,1},{0,2},{1,3},{7,4},{6,5},{4,6},{5,7},{11,8},{10,9},{8,1... | collective-permute-start | bytes 589832 | tf_op jit(solution)/shard_map/ppermute | solution.py:199

commit v6 on v5

--- a/solution.py
+++ b/solution.py
@@ -60,18 +60,20 @@
 
 
 def pack_kernel(groups, count, span, base, width, *refs):
-    arrays, messages, sems = refs[:count], refs[-1 - len(groups):-1], refs[-1]
-    run(
-        [
-            pltpu.make_async_copy(
-                arrays[i].at[:, columns(group, span, base, width)],
-                messages[m].at[i],
-                sems.at[m, i],
-            )
-            for m, group in enumerate(groups)
-            for i in range(count)
-        ]
-    )
+    arrays, messages, sem = refs[:count], refs[-1 - len(groups):-1], refs[-1]
+    rows = arrays[0].shape[0]
+    slabs = math.gcd(rows // 16, 4) if rows % 16 == 0 else 1
+    for m, group in enumerate(groups):
+        for i in range(count):
+            for j in range(slabs):
+                slab = pl.ds(j * (rows // slabs), rows // slabs)
+                pltpu.make_async_copy(
+                    arrays[i].at[slab, columns(group, span, base, width)],
+                    messages[m].at[i, slab],
+                    sem.at[m],
+                ).start()
+    for m in range(len(groups)):
+        pltpu.make_async_copy(messages[m], messages[m], sem.at[m]).wait()
 
 
 def pack(arrays, groups, span, base, width, after=()):
@@ -84,7 +86,7 @@
         out_shape=[message] * len(groups),
         in_specs=[FAR] * count + [ANYWHERE] * len(after),
         out_specs=[WHOLE] * len(groups),
-        scratch_shapes=[pltpu.SemaphoreType.DMA((len(groups), count))],
+        scratch_shapes=[pltpu.SemaphoreType.DMA((len(groups),))],
         compiler_params=limit(size),
         cost_estimate=pl.CostEstimate(flops=0, bytes_accessed=2 * size, transcendentals=0),
         name="pack",

time: 185 us -> 186 us (level)
  transfers between devices with their start and end apart: 12 -> 12, of which waited for: 3 -> 3; matrix products, arithmetic and copies ran while one was open for 0% -> 0% of each run, Pallas kernels for 17% -> 16%
where the time goes in v6:
time: 186 us; the launch traced here: 184 us
  starting transfers between devices  84.9 us (46%)
  waiting for transfers between devices  66.6 us (36%)
  Pallas kernels  32.2 us (17%)
    ppermute x6, starting transfers between devices, back(): lax.ppermute(message, 'seq', [(b, a) for a, b in enumerate(rounds[r][1])])  74.1 us
    ppermute x6, waiting for transfers between devices, there(): return lax.ppermute(message, 'seq', list(enumerate(rounds[r][1])))  54.5 us
    pallas_call x2, Pallas kernels, attend(): pl.pallas_call(functools.partial(attend_kernel, layout), out_shape=[jax.S...  17.5 us
    ppermute x6, waiting for transfers between devices, back(): lax.ppermute(message, 'seq', [(b, a) for a, b in enumerate(rounds[r][1])])  12.1 us
    ppermute x6, starting transfers between devices, there(): return lax.ppermute(message, 'seq', list(enumerate(rounds[r][1])))  10.8 us
    pallas_call x8, Pallas kernels, pack(): pl.pallas_call(functools.partial(pack_kernel, groups, count, span, base,...  8.85 us
    pallas_call x8, Pallas kernels, place(): pl.pallas_call(functools.partial(place_kernel, groups, span, base, width)...  5.79 us
  transfers between devices with their start and end apart: 12, of which 3 were waited for; matrix products, arithmetic and copies ran while one was open for 0% of the time, Pallas kernels for 16%

profile of v6, /device:TPU:0, one launch (start us, length us, event | category | flops | bytes accessed | tf_op | source)
XLA Modules:
  0.0 184.5 jit_solution(1322914456973597152)
XLA Ops:
  0.6 1.2 pack.12.refs_6_
  1.8 5.1 %collective-permute-start.8 = (bf16[6,128,640]{2,1,0:T(8,128)(2,1)S(1)}, bf16[6,128,640]{2,1,0:T(8,128)(2,1)S(1)}, u32[]{:S(2)}, u32[]{:S(2)}) collective-permute-start(bf16[6,128,640]{2,1,0:T(8,128)(2,1)S(1)} %pack.12.refs_6_), channel_id=1, source_target_pairs={{0,3},{1,2},{2,0},{3,1},{4,7},{5,6},{6,4},{7,5},{8,11},{9,10},{10,... | collective-permute-start | bytes 2949128 | tf_op jit(solution)/shard_map/ppermute | solution.py:198
  6.9 1.2 pack.14
  8.1 0.1 collective-permute-start.6
  8.2 1.2 pack.15
  9.4 0.9 collective-permute-start.7
  10.3 1.0 pack.8.refs_6_
  11.4 3.0 %collective-permute-start.2 = (bf16[6,128,384]{2,1,0:T(8,128)(2,1)S(1)}, bf16[6,128,384]{2,1,0:T(8,128)(2,1)S(1)}, u32[]{:S(2)}, u32[]{:S(2)}) collective-permute-start(bf16[6,128,384]{2,1,0:T(8,128)(2,1)S(1)} %pack.8.refs_6_), channel_id=1, source_target_pairs={{0,3},{1,2},{2,0},{3,1},{4,7},{5,6},{6,4},{7,5},{8,11},{9,10},{10,... | collective-permute-start | bytes 1769480 | tf_op jit(solution)/shard_map/ppermute | solution.py:198
  14.4 1.0 pack.10
  15.4 0.3 collective-permute-start
  15.7 1.0 pack.11
  16.7 33.8 %collective-permute-done.8.refs_3_ = bf16[6,128,640]{2,1,0:T(8,128)(2,1)S(1)} collective-permute-done((bf16[6,128,640]{2,1,0:T(8,128)(2,1)S(1)}, bf16[6,128,640]{2,1,0:T(8,128)(2,1)S(1)}, u32[]{:S(2)}, u32[]{:S(2)}) %collective-permute-start.8) | collective-permute-done | bytes 983072 | tf_op jit(solution)/shard_map/ppermute | solution.py:198
  50.5 1.4 collective-permute-start.1
  51.9 1.2 pack.13.refs_0_
  53.1 20.7 %collective-permute-done.6.refs_1_ = bf16[6,128,640]{2,1,0:T(8,128)(2,1)S(1)} collective-permute-done((bf16[6,128,640]{2,1,0:T(8,128)(2,1)S(1)}, bf16[6,128,640]{2,1,0:T(8,128)(2,1)S(1)}, u32[]{:S(2)}, u32[]{:S(2)}) %collective-permute-start.6) | collective-permute-done | bytes 983072 | tf_op jit(solution)/shard_map/ppermute | solution.py:198
  73.8 0.0 collective-permute-done.7.refs_2_
  73.8 10.9 %attend.3 = (bf16[2,128,640]{2,1,0:T(8,128)(2,1)S(1)}, bf16[2,128,640]{2,1,0:T(8,128)(2,1)S(1)}, bf16[2,128,640]{2,1,0:T(8,128)(2,1)S(1)}, bf16[2,128,640]{2,1,0:T(8,128)(2,1)S(1)}) custom-call(bf16[6,128,640]{2,1,0:T(8,128)(2,1)S(1)} %pack.13.refs_0_, bf16[6,128,640]{2,1,0:T(8,128)(2,1)S(1)} %collective-permute-done.6.refs_1_, ...), custom_call_target="tpu_custom_call" | custom-call | flops 2013265920 | bytes 5242880 | tf_op jit(solution)/shard_map/attend/pallas_call | solution.py:172
  84.8 43.8 %collective-permute-start.11 = (bf16[2,128,640]{2,1,0:T(8,128)(2,1)S(1)}, bf16[2,128,640]{2,1,0:T(8,128)(2,1)S(1)}, u32[]{:S(2)}, u32[]{:S(2)}) collective-permute-start(bf16[2,128,640]{2,1,0:T(8,128)(2,1)S(1)} %get-tuple-element.30), channel_id=1, source_target_pairs={{1,0},{0,1},{3,2},{2,3},{5,4},{4,5},{7,6},{6,7},{9,8},{8,9},{11,10... | collective-permute-start | bytes 983048 | tf_op jit(solution)/shard_map/ppermute | solution.py:201
  128.6 2.4 %collective-permute-start.10 = (bf16[2,128,640]{2,1,0:T(8,128)(2,1)S(1)}, bf16[2,128,640]{2,1,0:T(8,128)(2,1)S(1)}, u32[]{:S(2)}, u32[]{:S(2)}) collective-permute-start(bf16[2,128,640]{2,1,0:T(8,128)(2,1)S(1)} %get-tuple-element.29), channel_id=1, source_target_pairs={{2,0},{3,1},{1,2},{0,3},{6,4},{7,5},{5,6},{4,7},{10,8},{11,9},{9,1... | collective-permute-start | bytes 983048 | tf_op jit(solution)/shard_map/ppermute | solution.py:201
  131.0 0.0 collective-permute-done.2.refs_3_
  131.0 0.7 collective-permute-start.9
  131.7 1.0 pack.9.refs_0_
  132.7 0.0 collective-permute-done.refs_1_
  132.7 0.0 collective-permute-done.1.refs_2_
  132.7 6.6 %attend.2 = (bf16[2,128,384]{2,1,0:T(8,128)(2,1)S(1)}, bf16[2,128,384]{2,1,0:T(8,128)(2,1)S(1)}, bf16[2,128,384]{2,1,0:T(8,128)(2,1)S(1)}, bf16[2,128,384]{2,1,0:T(8,128)(2,1)S(1)}) custom-call(bf16[6,128,384]{2,1,0:T(8,128)(2,1)S(1)} %pack.9.refs_0_, bf16[6,128,384]{2,1,0:T(8,128)(2,1)S(1)} %collective-permute-done.refs_1_, ...), custom_call_target="tpu_custom_call" | custom-call | flops 1207959552 | bytes 3145728 | tf_op jit(solution)/shard_map/attend/pallas_call | solution.py:172
  139.3 24.2 %collective-permute-start.5 = (bf16[2,128,384]{2,1,0:T(8,128)(2,1)S(1)}, bf16[2,128,384]{2,1,0:T(8,128)(2,1)S(1)}, u32[]{:S(2)}, u32[]{:S(2)}) collective-permute-start(bf16[2,128,384]{2,1,0:T(8,128)(2,1)S(1)} %get-tuple-element.26), channel_id=1, source_target_pairs={{1,0},{0,1},{3,2},{2,3},{5,4},{4,5},{7,6},{6,7},{9,8},{8,9},{11,10... | collective-permute-start | bytes 589832 | tf_op jit(solution)/shard_map/ppermute | solution.py:201
  163.6 2.5 %collective-permute-start.4 = (bf16[2,128,384]{2,1,0:T(8,128)(2,1)S(1)}, bf16[2,128,384]{2,1,0:T(8,128)(2,1)S(1)}, u32[]{:S(2)}, u32[]{:S(2)}) collective-permute-start(bf16[2,128,384]{2,1,0:T(8,128)(2,1)S(1)} %get-tuple-element.25), channel_id=1, source_target_pairs={{2,0},{3,1},{1,2},{0,3},{6,4},{7,5},{5,6},{4,7},{10,8},{11,9},{9,1... | collective-permute-start | bytes 589832 | tf_op jit(solution)/shard_map/ppermute | solution.py:201
  166.0 0.0 collective-permute-done.11.refs_0_
  166.0 0.5 collective-permute-start.3
  166.5 0.7 place.8
  167.3 0.8 place.9
  168.0 0.0 collective-permute-done.10.refs_0_
  168.0 0.8 place.10
  168.8 0.0 collective-permute-done.9.refs_0_
  168.8 0.8 place.11
  169.6 0.7 place.12
  170.3 0.0 collective-permute-done.5.refs_0_
  170.3 0.7 place.13
  171.0 12.0 %collective-permute-done.4.refs_0_ = bf16[2,128,384]{2,1,0:T(8,128)(2,1)S(1)} collective-permute-done((bf16[2,128,384]{2,1,0:T(8,128)(2,1)S(1)}, bf16[2,128,384]{2,1,0:T(8,128)(2,1)S(1)}, u32[]{:S(2)}, u32[]{:S(2)}) %collective-permute-start.4) | collective-permute-done | bytes 196640 | tf_op jit(solution)/shard_map/ppermute | solution.py:201
  183.0 0.7 place.14
  183.7 0.0 collective-permute-done.3.refs_0_
  183.7 0.7 place.15
Async XLA Ops:
  1.8 48.7 %collective-permute-start.8 = (bf16[6,128,640]{2,1,0:T(8,128)(2,1)S(1)}, bf16[6,128,640]{2,1,0:T(8,128)(2,1)S(1)}, u32[]{:S(2)}, u32[]{:S(2)}) collective-permute-start(bf16[6,128,640]{2,1,0:T(8,128)(2,1)S(1)} %pack.12.refs_6_), channel_id=1, source_target_pairs={{0,3},{1,2},{2,0},{3,1},{4,7},{5,6},{6,4},{7,5},{8,11},{9,10},{10,... | collective-permute-start | bytes 2949128 | tf_op jit(solution)/shard_map/ppermute | solution.py:198
  8.1 65.7 %collective-permute-start.6 = (bf16[6,128,640]{2,1,0:T(8,128)(2,1)S(1)}, bf16[6,128,640]{2,1,0:T(8,128)(2,1)S(1)}, u32[]{:S(2)}, u32[]{:S(2)}) collective-permute-start(bf16[6,128,640]{2,1,0:T(8,128)(2,1)S(1)} %pack.14), channel_id=1, source_target_pairs={{0,1},{1,0},{2,3},{3,2},{4,5},{5,4},{6,7},{7,6},{8,9},{9,8},{10,11... | collective-permute-start | bytes 2949128 | tf_op jit(solution)/shard_map/ppermute | solution.py:198
  9.4 64.4 %collective-permute-start.7 = (bf16[6,128,640]{2,1,0:T(8,128)(2,1)S(1)}, bf16[6,128,640]{2,1,0:T(8,128)(2,1)S(1)}, u32[]{:S(2)}, u32[]{:S(2)}) collective-permute-start(bf16[6,128,640]{2,1,0:T(8,128)(2,1)S(1)} %pack.15), channel_id=1, source_target_pairs={{0,2},{1,3},{2,1},{3,0},{4,6},{5,7},{6,5},{7,4},{8,10},{9,11},{10,... | collective-permute-start | bytes 2949128 | tf_op jit(solution)/shard_map/ppermute | solution.py:198
  11.4 119.7 %collective-permute-start.2 = (bf16[6,128,384]{2,1,0:T(8,128)(2,1)S(1)}, bf16[6,128,384]{2,1,0:T(8,128)(2,1)S(1)}, u32[]{:S(2)}, u32[]{:S(2)}) collective-permute-start(bf16[6,128,384]{2,1,0:T(8,128)(2,1)S(1)} %pack.8.refs_6_), channel_id=1, source_target_pairs={{0,3},{1,2},{2,0},{3,1},{4,7},{5,6},{6,4},{7,5},{8,11},{9,10},{10,... | collective-permute-start | bytes 1769480 | tf_op jit(solution)/shard_map/ppermute | solution.py:198
  15.4 117.3 %collective-permute-start = (bf16[6,128,384]{2,1,0:T(8,128)(2,1)S(1)}, bf16[6,128,384]{2,1,0:T(8,128)(2,1)S(1)}, u32[]{:S(2)}, u32[]{:S(2)}) collective-permute-start(bf16[6,128,384]{2,1,0:T(8,128)(2,1)S(1)} %pack.10), channel_id=1, source_target_pairs={{0,1},{1,0},{2,3},{3,2},{4,5},{5,4},{6,7},{7,6},{8,9},{9,8},{10,11... | collective-permute-start | bytes 1769480 | tf_op jit(solution)/shard_map/ppermute | solution.py:198
  50.5 82.2 %collective-permute-start.1 = (bf16[6,128,384]{2,1,0:T(8,128)(2,1)S(1)}, bf16[6,128,384]{2,1,0:T(8,128)(2,1)S(1)}, u32[]{:S(2)}, u32[]{:S(2)}) collective-permute-start(bf16[6,128,384]{2,1,0:T(8,128)(2,1)S(1)} %pack.11), channel_id=1, source_target_pairs={{0,2},{1,3},{2,1},{3,0},{4,6},{5,7},{6,5},{7,4},{8,10},{9,11},{10,... | collective-permute-start | bytes 1769480 | tf_op jit(solution)/shard_map/ppermute | solution.py:198
  84.8 81.2 %collective-permute-start.11 = (bf16[2,128,640]{2,1,0:T(8,128)(2,1)S(1)}, bf16[2,128,640]{2,1,0:T(8,128)(2,1)S(1)}, u32[]{:S(2)}, u32[]{:S(2)}) collective-permute-start(bf16[2,128,640]{2,1,0:T(8,128)(2,1)S(1)} %get-tuple-element.30), channel_id=1, source_target_pairs={{1,0},{0,1},{3,2},{2,3},{5,4},{4,5},{7,6},{6,7},{9,8},{8,9},{11,10... | collective-permute-start | bytes 983048 | tf_op jit(solution)/shard_map/ppermute | solution.py:201
  128.6 39.4 %collective-permute-start.10 = (bf16[2,128,640]{2,1,0:T(8,128)(2,1)S(1)}, bf16[2,128,640]{2,1,0:T(8,128)(2,1)S(1)}, u32[]{:S(2)}, u32[]{:S(2)}) collective-permute-start(bf16[2,128,640]{2,1,0:T(8,128)(2,1)S(1)} %get-tuple-element.29), channel_id=1, source_target_pairs={{2,0},{3,1},{1,2},{0,3},{6,4},{7,5},{5,6},{4,7},{10,8},{11,9},{9,1... | collective-permute-start | bytes 983048 | tf_op jit(solution)/shard_map/ppermute | solution.py:201
  131.0 37.8 %collective-permute-start.9 = (bf16[2,128,640]{2,1,0:T(8,128)(2,1)S(1)}, bf16[2,128,640]{2,1,0:T(8,128)(2,1)S(1)}, u32[]{:S(2)}, u32[]{:S(2)}) collective-permute-start(bf16[2,128,640]{2,1,0:T(8,128)(2,1)S(1)} %get-tuple-element.28), channel_id=1, source_target_pairs={{3,0},{2,1},{0,2},{1,3},{7,4},{6,5},{4,6},{5,7},{11,8},{10,9},{8,1... | collective-permute-start | bytes 983048 | tf_op jit(solution)/shard_map/ppermute | solution.py:201
  139.3 31.0 %collective-permute-start.5 = (bf16[2,128,384]{2,1,0:T(8,128)(2,1)S(1)}, bf16[2,128,384]{2,1,0:T(8,128)(2,1)S(1)}, u32[]{:S(2)}, u32[]{:S(2)}) collective-permute-start(bf16[2,128,384]{2,1,0:T(8,128)(2,1)S(1)} %get-tuple-element.26), channel_id=1, source_target_pairs={{1,0},{0,1},{3,2},{2,3},{5,4},{4,5},{7,6},{6,7},{9,8},{8,9},{11,10... | collective-permute-start | bytes 589832 | tf_op jit(solution)/shard_map/ppermute | solution.py:201
  163.6 19.5 %collective-permute-start.4 = (bf16[2,128,384]{2,1,0:T(8,128)(2,1)S(1)}, bf16[2,128,384]{2,1,0:T(8,128)(2,1)S(1)}, u32[]{:S(2)}, u32[]{:S(2)}) collective-permute-start(bf16[2,128,384]{2,1,0:T(8,128)(2,1)S(1)} %get-tuple-element.25), channel_id=1, source_target_pairs={{2,0},{3,1},{1,2},{0,3},{6,4},{7,5},{5,6},{4,7},{10,8},{11,9},{9,1... | collective-permute-start | bytes 589832 | tf_op jit(solution)/shard_map/ppermute | solution.py:201
  166.0 17.7 %collective-permute-start.3 = (bf16[2,128,384]{2,1,0:T(8,128)(2,1)S(1)}, bf16[2,128,384]{2,1,0:T(8,128)(2,1)S(1)}, u32[]{:S(2)}, u32[]{:S(2)}) collective-permute-start(bf16[2,128,384]{2,1,0:T(8,128)(2,1)S(1)} %get-tuple-element.24), channel_id=1, source_target_pairs={{3,0},{2,1},{0,2},{1,3},{7,4},{6,5},{4,6},{5,7},{11,8},{10,9},{8,1... | collective-permute-start | bytes 589832 | tf_op jit(solution)/shard_map/ppermute | solution.py:201

commit v7 on v6

--- a/solution.py
+++ b/solution.py
@@ -207,7 +207,8 @@
         base += heads * HEAD
     received = []
     for base, width in chunks:
-        sent = [pack(arrays, [group], span, base, width) for group in groups]
+        parts = [arrays[:4], arrays[4:]] if base == 0 else [arrays]
+        sent = [[*(pack(part, [group], span, base, width)[0] for part in parts)] for group in groups]
         own = pack(arrays, [own_group], span, base, width, after=sent[-1])
         received.append([own, *([there(part, r) for part in m] for r, m in enumerate(sent))])
     outs = ()

time: 186 us -> 186 us (level)
  starting transfers between devices: 84.9 us -> 66 us
  waiting for transfers between devices: 66.6 us -> 82.8 us
  Pallas kernels: 32.2 us -> 34.7 us
    ppermute x6, starting transfers between devices: 74.1 us -> 21.4 us  [back(): lax.ppermute(message, 'seq', [(b, a) for a, b in enumerate(rounds[r][1])])]
    ppermute x6 -> x9, starting transfers between devices: 10.8 us -> 44.5 us  [there(): return lax.ppermute(message, 'seq', list(enumerate(rounds[r][1])))]
    ppermute x6 -> x9, waiting for transfers between devices: 54.5 us -> 70.7 us  [there(): return lax.ppermute(message, 'seq', list(enumerate(rounds[r][1])))]
    pallas_call x8 -> x11, Pallas kernels: 8.85 us -> 11.3 us  [pack(): pl.pallas_call(functools.partial(pack_kernel, groups, count, span, base,...]
  transfers between devices with their start and end apart: 12 -> 15, of which waited for: 3 -> 4; matrix products, arithmetic and copies ran while one was open for 0% -> 0% of each run, Pallas kernels for 16% -> 18%
where the time goes in v7:
time: 186 us; the launch traced here: 184 us
  waiting for transfers between devices  82.8 us (45%)
  starting transfers between devices  66 us (35%)
  Pallas kernels  34.7 us (19%)
    ppermute x9, waiting for transfers between devices, there(): return lax.ppermute(message, 'seq', list(enumerate(rounds[r][1])))  70.7 us
    ppermute x9, starting transfers between devices, there(): return lax.ppermute(message, 'seq', list(enumerate(rounds[r][1])))  44.5 us
    ppermute x6, starting transfers between devices, back(): lax.ppermute(message, 'seq', [(b, a) for a, b in enumerate(rounds[r][1])])  21.4 us
    pallas_call x2, Pallas kernels, attend(): pl.pallas_call(functools.partial(attend_kernel, layout), out_shape=[jax.S...  17.5 us
    ppermute x6, waiting for transfers between devices, back(): lax.ppermute(message, 'seq', [(b, a) for a, b in enumerate(rounds[r][1])])  12.1 us
    pallas_call x11, Pallas kernels, pack(): pl.pallas_call(functools.partial(pack_kernel, groups, count, span, base,...  11.3 us
    pallas_call x8, Pallas kernels, place(): pl.pallas_call(functools.partial(place_kernel, groups, span, base, width)...  5.79 us
  transfers between devices with their start and end apart: 15, of which 4 were waited for; matrix products, arithmetic and copies ran while one was open for 0% of the time, Pallas kernels for 18%

profile of v7, /device:TPU:0, one launch (start us, length us, event | category | flops | bytes accessed | tf_op | source)
XLA Modules:
  0.0 184.2 jit_solution(12663142637746181349)
XLA Ops:
  0.6 0.9 pack.16.refs_7_
  1.6 5.1 %collective-permute-start.11 = (bf16[2,128,640]{2,1,0:T(8,128)(2,1)S(1)}, bf16[2,128,640]{2,1,0:T(8,128)(2,1)S(1)}, u32[]{:S(2)}, u32[]{:S(2)}) collective-permute-start(bf16[2,128,640]{2,1,0:T(8,128)(2,1)S(1)} %pack.16.refs_7_), channel_id=1, source_target_pairs={{0,3},{1,2},{2,0},{3,1},{4,7},{5,6},{6,4},{7,5},{8,11},{9,10},{10,... | collective-permute-start | bytes 983048 | tf_op jit(solution)/shard_map/ppermute | solution.py:198
  6.7 1.1 pack.15.refs_6_
  7.8 0.4 collective-permute-start.10
  8.2 1.1 pack.18
  9.2 0.1 collective-permute-start.6
  9.3 1.1 pack.20
  10.4 2.6 %collective-permute-start.8 = (bf16[4,128,640]{2,1,0:T(8,128)(2,1)S(1)}, bf16[4,128,640]{2,1,0:T(8,128)(2,1)S(1)}, u32[]{:S(2)}, u32[]{:S(2)}) collective-permute-start(bf16[4,128,640]{2,1,0:T(8,128)(2,1)S(1)} %pack.20), channel_id=1, source_target_pairs={{0,2},{1,3},{2,1},{3,0},{4,6},{5,7},{6,5},{7,4},{8,10},{9,11},{10,... | collective-permute-start | bytes 1966088 | tf_op jit(solution)/shard_map/ppermute | solution.py:198
  13.1 0.9 pack.19
  14.0 2.1 %collective-permute-start.7 = (bf16[2,128,640]{2,1,0:T(8,128)(2,1)S(1)}, bf16[2,128,640]{2,1,0:T(8,128)(2,1)S(1)}, u32[]{:S(2)}, u32[]{:S(2)}) collective-permute-start(bf16[2,128,640]{2,1,0:T(8,128)(2,1)S(1)} %pack.19), channel_id=1, source_target_pairs={{0,1},{1,0},{2,3},{3,2},{4,5},{5,4},{6,7},{7,6},{8,9},{9,8},{10,11... | collective-permute-start | bytes 983048 | tf_op jit(solution)/shard_map/ppermute | solution.py:198
  16.0 0.9 pack.21
  17.0 18.4 %collective-permute-done.11.refs_6_ = bf16[2,128,640]{2,1,0:T(8,128)(2,1)S(1)} collective-permute-done((bf16[2,128,640]{2,1,0:T(8,128)(2,1)S(1)}, bf16[2,128,640]{2,1,0:T(8,128)(2,1)S(1)}, u32[]{:S(2)}, u32[]{:S(2)}) %collective-permute-start.11) | collective-permute-done | bytes 327712 | tf_op jit(solution)/shard_map/ppermute | solution.py:198
  35.4 2.0 %collective-permute-start.9 = (bf16[2,128,640]{2,1,0:T(8,128)(2,1)S(1)}, bf16[2,128,640]{2,1,0:T(8,128)(2,1)S(1)}, u32[]{:S(2)}, u32[]{:S(2)}) collective-permute-start(bf16[2,128,640]{2,1,0:T(8,128)(2,1)S(1)} %pack.21), channel_id=1, source_target_pairs={{0,2},{1,3},{2,1},{3,0},{4,6},{5,7},{6,5},{7,4},{8,10},{9,11},{10,... | collective-permute-start | bytes 983048 | tf_op jit(solution)/shard_map/ppermute | solution.py:198
  37.3 1.0 pack.11.refs_6_
  38.4 34.8 %collective-permute-done.7.refs_2_ = bf16[2,128,640]{2,1,0:T(8,128)(2,1)S(1)} collective-permute-done((bf16[2,128,640]{2,1,0:T(8,128)(2,1)S(1)}, bf16[2,128,640]{2,1,0:T(8,128)(2,1)S(1)}, u32[]{:S(2)}, u32[]{:S(2)}) %collective-permute-start.7) | collective-permute-done | bytes 327712 | tf_op jit(solution)/shard_map/ppermute | solution.py:198
  73.2 0.0 collective-permute-start.2
  73.2 1.0 pack.13
  74.2 1.0 pack.14
  75.3 0.0 collective-permute-done.9.refs_4_
  75.3 29.4 %collective-permute-start = (bf16[6,128,384]{2,1,0:T(8,128)(2,1)S(1)}, bf16[6,128,384]{2,1,0:T(8,128)(2,1)S(1)}, u32[]{:S(2)}, u32[]{:S(2)}) collective-permute-start(bf16[6,128,384]{2,1,0:T(8,128)(2,1)S(1)} %pack.13), channel_id=1, source_target_pairs={{0,1},{1,0},{2,3},{3,2},{4,5},{5,4},{6,7},{7,6},{8,9},{9,8},{10,11... | collective-permute-start | bytes 1769480 | tf_op jit(solution)/shard_map/ppermute | solution.py:198
  104.7 2.9 %collective-permute-start.1 = (bf16[6,128,384]{2,1,0:T(8,128)(2,1)S(1)}, bf16[6,128,384]{2,1,0:T(8,128)(2,1)S(1)}, u32[]{:S(2)}, u32[]{:S(2)}) collective-permute-start(bf16[6,128,384]{2,1,0:T(8,128)(2,1)S(1)} %pack.14), channel_id=1, source_target_pairs={{0,2},{1,3},{2,1},{3,0},{4,6},{5,7},{6,5},{7,4},{8,10},{9,11},{10,... | collective-permute-start | bytes 1769480 | tf_op jit(solution)/shard_map/ppermute | solution.py:198
  107.6 1.2 pack.17.refs_0_
  108.8 0.0 collective-permute-done.6.refs_1_
  108.8 0.0 collective-permute-done.8.refs_3_
  108.8 11.0 %attend.3 = (bf16[2,128,640]{2,1,0:T(8,128)(2,1)S(1)}, bf16[2,128,640]{2,1,0:T(8,128)(2,1)S(1)}, bf16[2,128,640]{2,1,0:T(8,128)(2,1)S(1)}, bf16[2,128,640]{2,1,0:T(8,128)(2,1)S(1)}) custom-call(bf16[6,128,640]{2,1,0:T(8,128)(2,1)S(1)} %pack.17.refs_0_, bf16[4,128,640]{2,1,0:T(8,128)(2,1)S(1)} %collective-permute-done.6.refs_1_, ...), custom_call_target="tpu_custom_call" | custom-call | flops 2013265920 | bytes 5242880 | tf_op jit(solution)/shard_map/attend/pallas_call | solution.py:172
  119.8 0.1 collective-permute-start.14
  119.9 1.5 collective-permute-start.13
  121.3 1.5 collective-permute-start.12
  122.9 1.0 pack.12.refs_0_
  123.9 17.4 %collective-permute-done.refs_1_ = bf16[6,128,384]{2,1,0:T(8,128)(2,1)S(1)} collective-permute-done((bf16[6,128,384]{2,1,0:T(8,128)(2,1)S(1)}, bf16[6,128,384]{2,1,0:T(8,128)(2,1)S(1)}, u32[]{:S(2)}, u32[]{:S(2)}) %collective-permute-start) | collective-permute-done | bytes 589856 | tf_op jit(solution)/shard_map/ppermute | solution.py:198
  141.3 0.0 collective-permute-done.1.refs_2_
  141.3 6.6 %attend.2 = (bf16[2,128,384]{2,1,0:T(8,128)(2,1)S(1)}, bf16[2,128,384]{2,1,0:T(8,128)(2,1)S(1)}, bf16[2,128,384]{2,1,0:T(8,128)(2,1)S(1)}, bf16[2,128,384]{2,1,0:T(8,128)(2,1)S(1)}) custom-call(bf16[6,128,384]{2,1,0:T(8,128)(2,1)S(1)} %pack.12.refs_0_, bf16[6,128,384]{2,1,0:T(8,128)(2,1)S(1)} %collective-permute-done.refs_1_, ...), custom_call_target="tpu_custom_call" | custom-call | flops 1207959552 | bytes 3145728 | tf_op jit(solution)/shard_map/attend/pallas_call | solution.py:172
  147.9 15.4 %collective-permute-start.5 = (bf16[2,128,384]{2,1,0:T(8,128)(2,1)S(1)}, bf16[2,128,384]{2,1,0:T(8,128)(2,1)S(1)}, u32[]{:S(2)}, u32[]{:S(2)}) collective-permute-start(bf16[2,128,384]{2,1,0:T(8,128)(2,1)S(1)} %get-tuple-element.26), channel_id=1, source_target_pairs={{1,0},{0,1},{3,2},{2,3},{5,4},{4,5},{7,6},{6,7},{9,8},{8,9},{11,10... | collective-permute-start | bytes 589832 | tf_op jit(solution)/shard_map/ppermute | solution.py:201
  163.4 2.4 %collective-permute-start.4 = (bf16[2,128,384]{2,1,0:T(8,128)(2,1)S(1)}, bf16[2,128,384]{2,1,0:T(8,128)(2,1)S(1)}, u32[]{:S(2)}, u32[]{:S(2)}) collective-permute-start(bf16[2,128,384]{2,1,0:T(8,128)(2,1)S(1)} %get-tuple-element.25), channel_id=1, source_target_pairs={{2,0},{3,1},{1,2},{0,3},{6,4},{7,5},{5,6},{4,7},{10,8},{11,9},{9,1... | collective-permute-start | bytes 589832 | tf_op jit(solution)/shard_map/ppermute | solution.py:201
  165.7 0.0 collective-permute-done.14.refs_0_
  165.7 0.6 collective-permute-start.3
  166.3 0.7 place.8
  167.0 0.8 place.9
  167.8 0.8 place.10
  168.6 0.0 collective-permute-done.12.refs_0_
  168.6 0.8 place.11
  169.3 0.7 place.12
  170.0 0.0 collective-permute-done.5.refs_0_
  170.0 0.7 place.13
  170.8 12.1 %collective-permute-done.4.refs_0_ = bf16[2,128,384]{2,1,0:T(8,128)(2,1)S(1)} collective-permute-done((bf16[2,128,384]{2,1,0:T(8,128)(2,1)S(1)}, bf16[2,128,384]{2,1,0:T(8,128)(2,1)S(1)}, u32[]{:S(2)}, u32[]{:S(2)}) %collective-permute-start.4) | collective-permute-done | bytes 196640 | tf_op jit(solution)/shard_map/ppermute | solution.py:201
  182.8 0.7 place.14
  183.5 0.0 collective-permute-done.3.refs_0_
  183.5 0.7 place.15
  (3 shorter events, 0.0 us)
Async XLA Ops:
  1.6 33.8 %collective-permute-start.11 = (bf16[2,128,640]{2,1,0:T(8,128)(2,1)S(1)}, bf16[2,128,640]{2,1,0:T(8,128)(2,1)S(1)}, u32[]{:S(2)}, u32[]{:S(2)}) collective-permute-start(bf16[2,128,640]{2,1,0:T(8,128)(2,1)S(1)} %pack.16.refs_7_), channel_id=1, source_target_pairs={{0,3},{1,2},{2,0},{3,1},{4,7},{5,6},{6,4},{7,5},{8,11},{9,10},{10,... | collective-permute-start | bytes 983048 | tf_op jit(solution)/shard_map/ppermute | solution.py:198
  7.8 96.9 %collective-permute-start.10 = (bf16[4,128,640]{2,1,0:T(8,128)(2,1)S(1)}, bf16[4,128,640]{2,1,0:T(8,128)(2,1)S(1)}, u32[]{:S(2)}, u32[]{:S(2)}) collective-permute-start(bf16[4,128,640]{2,1,0:T(8,128)(2,1)S(1)} %pack.15.refs_6_), channel_id=1, source_target_pairs={{0,3},{1,2},{2,0},{3,1},{4,7},{5,6},{6,4},{7,5},{8,11},{9,10},{10,... | collective-permute-start | bytes 1966088 | tf_op jit(solution)/shard_map/ppermute | solution.py:198
  9.2 99.6 %collective-permute-start.6 = (bf16[4,128,640]{2,1,0:T(8,128)(2,1)S(1)}, bf16[4,128,640]{2,1,0:T(8,128)(2,1)S(1)}, u32[]{:S(2)}, u32[]{:S(2)}) collective-permute-start(bf16[4,128,640]{2,1,0:T(8,128)(2,1)S(1)} %pack.18), channel_id=1, source_target_pairs={{0,1},{1,0},{2,3},{3,2},{4,5},{5,4},{6,7},{7,6},{8,9},{9,8},{10,11... | collective-permute-start | bytes 1966088 | tf_op jit(solution)/shard_map/ppermute | solution.py:198
  10.4 98.4 %collective-permute-start.8 = (bf16[4,128,640]{2,1,0:T(8,128)(2,1)S(1)}, bf16[4,128,640]{2,1,0:T(8,128)(2,1)S(1)}, u32[]{:S(2)}, u32[]{:S(2)}) collective-permute-start(bf16[4,128,640]{2,1,0:T(8,128)(2,1)S(1)} %pack.20), channel_id=1, source_target_pairs={{0,2},{1,3},{2,1},{3,0},{4,6},{5,7},{6,5},{7,4},{8,10},{9,11},{10,... | collective-permute-start | bytes 1966088 | tf_op jit(solution)/shard_map/ppermute | solution.py:198
  14.0 59.2 %collective-permute-start.7 = (bf16[2,128,640]{2,1,0:T(8,128)(2,1)S(1)}, bf16[2,128,640]{2,1,0:T(8,128)(2,1)S(1)}, u32[]{:S(2)}, u32[]{:S(2)}) collective-permute-start(bf16[2,128,640]{2,1,0:T(8,128)(2,1)S(1)} %pack.19), channel_id=1, source_target_pairs={{0,1},{1,0},{2,3},{3,2},{4,5},{5,4},{6,7},{7,6},{8,9},{9,8},{10,11... | collective-permute-start | bytes 983048 | tf_op jit(solution)/shard_map/ppermute | solution.py:198
  35.4 39.9 %collective-permute-start.9 = (bf16[2,128,640]{2,1,0:T(8,128)(2,1)S(1)}, bf16[2,128,640]{2,1,0:T(8,128)(2,1)S(1)}, u32[]{:S(2)}, u32[]{:S(2)}) collective-permute-start(bf16[2,128,640]{2,1,0:T(8,128)(2,1)S(1)} %pack.21), channel_id=1, source_target_pairs={{0,2},{1,3},{2,1},{3,0},{4,6},{5,7},{6,5},{7,4},{8,10},{9,11},{10,... | collective-permute-start | bytes 983048 | tf_op jit(solution)/shard_map/ppermute | solution.py:198
  73.2 48.1 %collective-permute-start.2 = (bf16[6,128,384]{2,1,0:T(8,128)(2,1)S(1)}, bf16[6,128,384]{2,1,0:T(8,128)(2,1)S(1)}, u32[]{:S(2)}, u32[]{:S(2)}) collective-permute-start(bf16[6,128,384]{2,1,0:T(8,128)(2,1)S(1)} %pack.11.refs_6_), channel_id=1, source_target_pairs={{0,3},{1,2},{2,0},{3,1},{4,7},{5,6},{6,4},{7,5},{8,11},{9,10},{10,... | collective-permute-start | bytes 1769480 | tf_op jit(solution)/shard_map/ppermute | solution.py:198
  75.3 66.0 %collective-permute-start = (bf16[6,128,384]{2,1,0:T(8,128)(2,1)S(1)}, bf16[6,128,384]{2,1,0:T(8,128)(2,1)S(1)}, u32[]{:S(2)}, u32[]{:S(2)}) collective-permute-start(bf16[6,128,384]{2,1,0:T(8,128)(2,1)S(1)} %pack.13), channel_id=1, source_target_pairs={{0,1},{1,0},{2,3},{3,2},{4,5},{5,4},{6,7},{7,6},{8,9},{9,8},{10,11... | collective-permute-start | bytes 1769480 | tf_op jit(solution)/shard_map/ppermute | solution.py:198
  104.7 36.6 %collective-permute-start.1 = (bf16[6,128,384]{2,1,0:T(8,128)(2,1)S(1)}, bf16[6,128,384]{2,1,0:T(8,128)(2,1)S(1)}, u32[]{:S(2)}, u32[]{:S(2)}) collective-permute-start(bf16[6,128,384]{2,1,0:T(8,128)(2,1)S(1)} %pack.14), channel_id=1, source_target_pairs={{0,2},{1,3},{2,1},{3,0},{4,6},{5,7},{6,5},{7,4},{8,10},{9,11},{10,... | collective-permute-start | bytes 1769480 | tf_op jit(solution)/shard_map/ppermute | solution.py:198
  119.8 45.9 %collective-permute-start.14 = (bf16[2,128,640]{2,1,0:T(8,128)(2,1)S(1)}, bf16[2,128,640]{2,1,0:T(8,128)(2,1)S(1)}, u32[]{:S(2)}, u32[]{:S(2)}) collective-permute-start(bf16[2,128,640]{2,1,0:T(8,128)(2,1)S(1)} %get-tuple-element.30), channel_id=1, source_target_pairs={{1,0},{0,1},{3,2},{2,3},{5,4},{4,5},{7,6},{6,7},{9,8},{8,9},{11,10... | collective-permute-start | bytes 983048 | tf_op jit(solution)/shard_map/ppermute | solution.py:201
  119.9 47.9 %collective-permute-start.13 = (bf16[2,128,640]{2,1,0:T(8,128)(2,1)S(1)}, bf16[2,128,640]{2,1,0:T(8,128)(2,1)S(1)}, u32[]{:S(2)}, u32[]{:S(2)}) collective-permute-start(bf16[2,128,640]{2,1,0:T(8,128)(2,1)S(1)} %get-tuple-element.29), channel_id=1, source_target_pairs={{2,0},{3,1},{1,2},{0,3},{6,4},{7,5},{5,6},{4,7},{10,8},{11,9},{9,1... | collective-permute-start | bytes 983048 | tf_op jit(solution)/shard_map/ppermute | solution.py:201
  121.3 47.2 %collective-permute-start.12 = (bf16[2,128,640]{2,1,0:T(8,128)(2,1)S(1)}, bf16[2,128,640]{2,1,0:T(8,128)(2,1)S(1)}, u32[]{:S(2)}, u32[]{:S(2)}) collective-permute-start(bf16[2,128,640]{2,1,0:T(8,128)(2,1)S(1)} %get-tuple-element.28), channel_id=1, source_target_pairs={{3,0},{2,1},{0,2},{1,3},{7,4},{6,5},{4,6},{5,7},{11,8},{10,9},{8,1... | collective-permute-start | bytes 983048 | tf_op jit(solution)/shard_map/ppermute | solution.py:201
  147.9 22.1 %collective-permute-start.5 = (bf16[2,128,384]{2,1,0:T(8,128)(2,1)S(1)}, bf16[2,128,384]{2,1,0:T(8,128)(2,1)S(1)}, u32[]{:S(2)}, u32[]{:S(2)}) collective-permute-start(bf16[2,128,384]{2,1,0:T(8,128)(2,1)S(1)} %get-tuple-element.26), channel_id=1, source_target_pairs={{1,0},{0,1},{3,2},{2,3},{5,4},{4,5},{7,6},{6,7},{9,8},{8,9},{11,10... | collective-permute-start | bytes 589832 | tf_op jit(solution)/shard_map/ppermute | solution.py:201
  163.4 19.5 %collective-permute-start.4 = (bf16[2,128,384]{2,1,0:T(8,128)(2,1)S(1)}, bf16[2,128,384]{2,1,0:T(8,128)(2,1)S(1)}, u32[]{:S(2)}, u32[]{:S(2)}) collective-permute-start(bf16[2,128,384]{2,1,0:T(8,128)(2,1)S(1)} %get-tuple-element.25), channel_id=1, source_target_pairs={{2,0},{3,1},{1,2},{0,3},{6,4},{7,5},{5,6},{4,7},{10,8},{11,9},{9,1... | collective-permute-start | bytes 589832 | tf_op jit(solution)/shard_map/ppermute | solution.py:201
  165.7 17.8 %collective-permute-start.3 = (bf16[2,128,384]{2,1,0:T(8,128)(2,1)S(1)}, bf16[2,128,384]{2,1,0:T(8,128)(2,1)S(1)}, u32[]{:S(2)}, u32[]{:S(2)}) collective-permute-start(bf16[2,128,384]{2,1,0:T(8,128)(2,1)S(1)} %get-tuple-element.24), channel_id=1, source_target_pairs={{3,0},{2,1},{0,2},{1,3},{7,4},{6,5},{4,6},{5,7},{11,8},{10,9},{8,1... | collective-permute-start | bytes 589832 | tf_op jit(solution)/shard_map/ppermute | solution.py:201

commit v8 on v7

--- a/solution.py
+++ b/solution.py
@@ -207,7 +207,7 @@
         base += heads * HEAD
     received = []
     for base, width in chunks:
-        parts = [arrays[:4], arrays[4:]] if base == 0 else [arrays]
+        parts = [arrays[:2], arrays[2:4], arrays[4:]] if base == 0 else [arrays]
         sent = [[*(pack(part, [group], span, base, width)[0] for part in parts)] for group in groups]
         own = pack(arrays, [own_group], span, base, width, after=sent[-1])
         received.append([own, *([there(part, r) for part in m] for r, m in enumerate(sent))])

time: 186 us -> 186 us (level)
  waiting for transfers between devices: 82.8 us -> 67.7 us
  starting transfers between devices: 66 us -> 78.5 us
  Pallas kernels: 34.7 us -> 37.1 us
    ppermute x6, starting transfers between devices: 21.4 us -> 44.4 us  [back(): lax.ppermute(message, 'seq', [(b, a) for a, b in enumerate(rounds[r][1])])]
    ppermute x9 -> x12, waiting for transfers between devices: 70.7 us -> 55.7 us  [there(): return lax.ppermute(message, 'seq', list(enumerate(rounds[r][1])))]
    ppermute x9 -> x12, starting transfers between devices: 44.5 us -> 34.1 us  [there(): return lax.ppermute(message, 'seq', list(enumerate(rounds[r][1])))]
    pallas_call x11 -> x14, Pallas kernels: 11.3 us -> 13.7 us  [pack(): pl.pallas_call(functools.partial(pack_kernel, groups, count, span, base,...]
  transfers between devices with their start and end apart: 15 -> 18, of which waited for: 4 -> 5; matrix products, arithmetic and copies ran while one was open for 0% -> 0% of each run, Pallas kernels for 18% -> 19%
where the time goes in v8:
time: 186 us; the launch traced here: 184 us
  starting transfers between devices  78.5 us (42%)
  waiting for transfers between devices  67.7 us (36%)
  Pallas kernels  37.1 us (20%)
    ppermute x12, waiting for transfers between devices, there(): return lax.ppermute(message, 'seq', list(enumerate(rounds[r][1])))  55.7 us
    ppermute x6, starting transfers between devices, back(): lax.ppermute(message, 'seq', [(b, a) for a, b in enumerate(rounds[r][1])])  44.4 us
    ppermute x12, starting transfers between devices, there(): return lax.ppermute(message, 'seq', list(enumerate(rounds[r][1])))  34.1 us
    pallas_call x2, Pallas kernels, attend(): pl.pallas_call(functools.partial(attend_kernel, layout), out_shape=[jax.S...  17.6 us
    pallas_call x14, Pallas kernels, pack(): pl.pallas_call(functools.partial(pack_kernel, groups, count, span, base,...  13.7 us
    ppermute x6, waiting for transfers between devices, back(): lax.ppermute(message, 'seq', [(b, a) for a, b in enumerate(rounds[r][1])])  12 us
    pallas_call x8, Pallas kernels, place(): pl.pallas_call(functools.partial(place_kernel, groups, span, base, width)...  5.79 us
  transfers between devices with their start and end apart: 18, of which 5 were waited for; matrix products, arithmetic and copies ran while one was open for 0% of the time, Pallas kernels for 19%

profile of v8, /device:TPU:0, one launch (start us, length us, event | category | flops | bytes accessed | tf_op | source)
XLA Modules:
  0.0 184.2 jit_solution(11711998306899538163)
XLA Ops:
  0.6 0.9 pack.18.refs_6_
  1.6 5.1 %collective-permute-start.12 = (bf16[2,128,640]{2,1,0:T(8,128)(2,1)S(1)}, bf16[2,128,640]{2,1,0:T(8,128)(2,1)S(1)}, u32[]{:S(2)}, u32[]{:S(2)}) collective-permute-start(bf16[2,128,640]{2,1,0:T(8,128)(2,1)S(1)} %pack.18.refs_6_), channel_id=1, source_target_pairs={{0,3},{1,2},{2,0},{3,1},{4,7},{5,6},{6,4},{7,5},{8,11},{9,10},{10,... | collective-permute-start | bytes 983048 | tf_op jit(solution)/shard_map/ppermute | solution.py:198
  6.7 0.9 pack.19.refs_7_
  7.6 0.4 collective-permute-start.13
  8.0 0.9 pack.20.refs_8_
  8.9 1.6 collective-permute-start.14
  10.6 0.9 pack.26
  11.5 1.4 collective-permute-start.10
  12.9 0.9 pack.27
  13.8 1.7 collective-permute-start.11
  15.6 0.9 pack.22
  16.5 0.9 pack.23
  17.5 31.9 %collective-permute-done.12.refs_7_ = bf16[2,128,640]{2,1,0:T(8,128)(2,1)S(1)} collective-permute-done((bf16[2,128,640]{2,1,0:T(8,128)(2,1)S(1)}, bf16[2,128,640]{2,1,0:T(8,128)(2,1)S(1)}, u32[]{:S(2)}, u32[]{:S(2)}) %collective-permute-start.12) | collective-permute-done | bytes 327712 | tf_op jit(solution)/shard_map/ppermute | solution.py:198
  49.3 0.1 collective-permute-start.6
  49.5 7.0 %collective-permute-done.13.refs_8_ = bf16[2,128,640]{2,1,0:T(8,128)(2,1)S(1)} collective-permute-done((bf16[2,128,640]{2,1,0:T(8,128)(2,1)S(1)}, bf16[2,128,640]{2,1,0:T(8,128)(2,1)S(1)}, u32[]{:S(2)}, u32[]{:S(2)}) %collective-permute-start.13) | collective-permute-done | bytes 327712 | tf_op jit(solution)/shard_map/ppermute | solution.py:198
  56.4 0.0 collective-permute-start.7
  56.5 0.9 pack.24
  57.4 0.9 pack.25
  58.4 5.0 %collective-permute-done.14.refs_9_ = bf16[2,128,640]{2,1,0:T(8,128)(2,1)S(1)} collective-permute-done((bf16[2,128,640]{2,1,0:T(8,128)(2,1)S(1)}, bf16[2,128,640]{2,1,0:T(8,128)(2,1)S(1)}, u32[]{:S(2)}, u32[]{:S(2)}) %collective-permute-start.14) | collective-permute-done | bytes 327712 | tf_op jit(solution)/shard_map/ppermute | solution.py:198
  63.4 0.1 collective-permute-start.8
  63.5 6.5 %collective-permute-start.9 = (bf16[2,128,640]{2,1,0:T(8,128)(2,1)S(1)}, bf16[2,128,640]{2,1,0:T(8,128)(2,1)S(1)}, u32[]{:S(2)}, u32[]{:S(2)}) collective-permute-start(bf16[2,128,640]{2,1,0:T(8,128)(2,1)S(1)} %pack.25), channel_id=1, source_target_pairs={{0,2},{1,3},{2,1},{3,0},{4,6},{5,7},{6,5},{7,4},{8,10},{9,11},{10,... | collective-permute-start | bytes 983048 | tf_op jit(solution)/shard_map/ppermute | solution.py:198
  70.0 1.0 pack.14.refs_6_
  71.0 0.0 collective-permute-done.11.refs_6_
  71.0 16.5 %collective-permute-start.2 = (bf16[6,128,384]{2,1,0:T(8,128)(2,1)S(1)}, bf16[6,128,384]{2,1,0:T(8,128)(2,1)S(1)}, u32[]{:S(2)}, u32[]{:S(2)}) collective-permute-start(bf16[6,128,384]{2,1,0:T(8,128)(2,1)S(1)} %pack.14.refs_6_), channel_id=1, source_target_pairs={{0,3},{1,2},{2,0},{3,1},{4,7},{5,6},{6,4},{7,5},{8,11},{9,10},{10,... | collective-permute-start | bytes 1769480 | tf_op jit(solution)/shard_map/ppermute | solution.py:198
  87.5 1.0 pack.16
  88.6 1.0 pack.17
  89.6 0.1 collective-permute-start
  89.7 0.5 collective-permute-start.1
  90.3 1.2 pack.21.refs_0_
  91.5 11.0 %attend.3 = (bf16[2,128,640]{2,1,0:T(8,128)(2,1)S(1)}, bf16[2,128,640]{2,1,0:T(8,128)(2,1)S(1)}, bf16[2,128,640]{2,1,0:T(8,128)(2,1)S(1)}, bf16[2,128,640]{2,1,0:T(8,128)(2,1)S(1)}) custom-call(bf16[6,128,640]{2,1,0:T(8,128)(2,1)S(1)} %pack.21.refs_0_, bf16[2,128,640]{2,1,0:T(8,128)(2,1)S(1)} %collective-permute-done.6.refs_1_, ...), custom_call_target="tpu_custom_call" | custom-call | flops 2013265920 | bytes 5242880 | tf_op jit(solution)/shard_map/attend/pallas_call | solution.py:172
  102.5 13.3 %collective-permute-start.17 = (bf16[2,128,640]{2,1,0:T(8,128)(2,1)S(1)}, bf16[2,128,640]{2,1,0:T(8,128)(2,1)S(1)}, u32[]{:S(2)}, u32[]{:S(2)}) collective-permute-start(bf16[2,128,640]{2,1,0:T(8,128)(2,1)S(1)} %get-tuple-element.30), channel_id=1, source_target_pairs={{1,0},{0,1},{3,2},{2,3},{5,4},{4,5},{7,6},{6,7},{9,8},{8,9},{11,10... | collective-permute-start | bytes 983048 | tf_op jit(solution)/shard_map/ppermute | solution.py:201
  115.8 2.5 %collective-permute-start.16 = (bf16[2,128,640]{2,1,0:T(8,128)(2,1)S(1)}, bf16[2,128,640]{2,1,0:T(8,128)(2,1)S(1)}, u32[]{:S(2)}, u32[]{:S(2)}) collective-permute-start(bf16[2,128,640]{2,1,0:T(8,128)(2,1)S(1)} %get-tuple-element.29), channel_id=1, source_target_pairs={{2,0},{3,1},{1,2},{0,3},{6,4},{7,5},{5,6},{4,7},{10,8},{11,9},{9,1... | collective-permute-start | bytes 983048 | tf_op jit(solution)/shard_map/ppermute | solution.py:201
  118.3 11.8 %collective-permute-done.2.refs_3_ = bf16[6,128,384]{2,1,0:T(8,128)(2,1)S(1)} collective-permute-done((bf16[6,128,384]{2,1,0:T(8,128)(2,1)S(1)}, bf16[6,128,384]{2,1,0:T(8,128)(2,1)S(1)}, u32[]{:S(2)}, u32[]{:S(2)}) %collective-permute-start.2) | collective-permute-done | bytes 589856 | tf_op jit(solution)/shard_map/ppermute | solution.py:198
  130.1 2.3 %collective-permute-start.15 = (bf16[2,128,640]{2,1,0:T(8,128)(2,1)S(1)}, bf16[2,128,640]{2,1,0:T(8,128)(2,1)S(1)}, u32[]{:S(2)}, u32[]{:S(2)}) collective-permute-start(bf16[2,128,640]{2,1,0:T(8,128)(2,1)S(1)} %get-tuple-element.28), channel_id=1, source_target_pairs={{3,0},{2,1},{0,2},{1,3},{7,4},{6,5},{4,6},{5,7},{11,8},{10,9},{8,1... | collective-permute-start | bytes 983048 | tf_op jit(solution)/shard_map/ppermute | solution.py:201
  132.4 1.0 pack.15.refs_0_
  133.5 6.6 %attend.2 = (bf16[2,128,384]{2,1,0:T(8,128)(2,1)S(1)}, bf16[2,128,384]{2,1,0:T(8,128)(2,1)S(1)}, bf16[2,128,384]{2,1,0:T(8,128)(2,1)S(1)}, bf16[2,128,384]{2,1,0:T(8,128)(2,1)S(1)}) custom-call(bf16[6,128,384]{2,1,0:T(8,128)(2,1)S(1)} %pack.15.refs_0_, bf16[6,128,384]{2,1,0:T(8,128)(2,1)S(1)} %collective-permute-done.refs_1_, ...), custom_call_target="tpu_custom_call" | custom-call | flops 1207959552 | bytes 3145728 | tf_op jit(solution)/shard_map/attend/pallas_call | solution.py:172
  140.1 23.3 %collective-permute-start.5 = (bf16[2,128,384]{2,1,0:T(8,128)(2,1)S(1)}, bf16[2,128,384]{2,1,0:T(8,128)(2,1)S(1)}, u32[]{:S(2)}, u32[]{:S(2)}) collective-permute-start(bf16[2,128,384]{2,1,0:T(8,128)(2,1)S(1)} %get-tuple-element.26), channel_id=1, source_target_pairs={{1,0},{0,1},{3,2},{2,3},{5,4},{4,5},{7,6},{6,7},{9,8},{8,9},{11,10... | collective-permute-start | bytes 589832 | tf_op jit(solution)/shard_map/ppermute | solution.py:201
  163.3 2.5 %collective-permute-start.4 = (bf16[2,128,384]{2,1,0:T(8,128)(2,1)S(1)}, bf16[2,128,384]{2,1,0:T(8,128)(2,1)S(1)}, u32[]{:S(2)}, u32[]{:S(2)}) collective-permute-start(bf16[2,128,384]{2,1,0:T(8,128)(2,1)S(1)} %get-tuple-element.25), channel_id=1, source_target_pairs={{2,0},{3,1},{1,2},{0,3},{6,4},{7,5},{5,6},{4,7},{10,8},{11,9},{9,1... | collective-permute-start | bytes 589832 | tf_op jit(solution)/shard_map/ppermute | solution.py:201
  165.8 0.5 collective-permute-start.3
  166.3 0.7 place.8
  167.1 0.8 place.9
  167.8 0.8 place.10
  168.6 0.8 place.11
  169.4 0.7 place.12
  170.1 0.7 place.13
  170.8 12.0 %collective-permute-done.4.refs_0_ = bf16[2,128,384]{2,1,0:T(8,128)(2,1)S(1)} collective-permute-done((bf16[2,128,384]{2,1,0:T(8,128)(2,1)S(1)}, bf16[2,128,384]{2,1,0:T(8,128)(2,1)S(1)}, u32[]{:S(2)}, u32[]{:S(2)}) %collective-permute-start.4) | collective-permute-done | bytes 196640 | tf_op jit(solution)/shard_map/ppermute | solution.py:201
  182.8 0.7 place.14
  183.5 0.7 place.15
  (12 shorter events, 0.0 us)
Async XLA Ops:
  1.6 47.7 %collective-permute-start.12 = (bf16[2,128,640]{2,1,0:T(8,128)(2,1)S(1)}, bf16[2,128,640]{2,1,0:T(8,128)(2,1)S(1)}, u32[]{:S(2)}, u32[]{:S(2)}) collective-permute-start(bf16[2,128,640]{2,1,0:T(8,128)(2,1)S(1)} %pack.18.refs_6_), channel_id=1, source_target_pairs={{0,3},{1,2},{2,0},{3,1},{4,7},{5,6},{6,4},{7,5},{8,11},{9,10},{10,... | collective-permute-start | bytes 983048 | tf_op jit(solution)/shard_map/ppermute | solution.py:198
  7.6 48.8 %collective-permute-start.13 = (bf16[2,128,640]{2,1,0:T(8,128)(2,1)S(1)}, bf16[2,128,640]{2,1,0:T(8,128)(2,1)S(1)}, u32[]{:S(2)}, u32[]{:S(2)}) collective-permute-start(bf16[2,128,640]{2,1,0:T(8,128)(2,1)S(1)} %pack.19.refs_7_), channel_id=1, source_target_pairs={{0,3},{1,2},{2,0},{3,1},{4,7},{5,6},{6,4},{7,5},{8,11},{9,10},{10,... | collective-permute-start | bytes 983048 | tf_op jit(solution)/shard_map/ppermute | solution.py:198
  8.9 54.5 %collective-permute-start.14 = (bf16[2,128,640]{2,1,0:T(8,128)(2,1)S(1)}, bf16[2,128,640]{2,1,0:T(8,128)(2,1)S(1)}, u32[]{:S(2)}, u32[]{:S(2)}) collective-permute-start(bf16[2,128,640]{2,1,0:T(8,128)(2,1)S(1)} %pack.20.refs_8_), channel_id=1, source_target_pairs={{0,3},{1,2},{2,0},{3,1},{4,7},{5,6},{6,4},{7,5},{8,11},{9,10},{10,... | collective-permute-start | bytes 983048 | tf_op jit(solution)/shard_map/ppermute | solution.py:198
  11.5 52.0 %collective-permute-start.10 = (bf16[2,128,640]{2,1,0:T(8,128)(2,1)S(1)}, bf16[2,128,640]{2,1,0:T(8,128)(2,1)S(1)}, u32[]{:S(2)}, u32[]{:S(2)}) collective-permute-start(bf16[2,128,640]{2,1,0:T(8,128)(2,1)S(1)} %pack.26), channel_id=1, source_target_pairs={{0,2},{1,3},{2,1},{3,0},{4,6},{5,7},{6,5},{7,4},{8,10},{9,11},{10,... | collective-permute-start | bytes 983048 | tf_op jit(solution)/shard_map/ppermute | solution.py:198
  13.8 57.2 %collective-permute-start.11 = (bf16[2,128,640]{2,1,0:T(8,128)(2,1)S(1)}, bf16[2,128,640]{2,1,0:T(8,128)(2,1)S(1)}, u32[]{:S(2)}, u32[]{:S(2)}) collective-permute-start(bf16[2,128,640]{2,1,0:T(8,128)(2,1)S(1)} %pack.27), channel_id=1, source_target_pairs={{0,2},{1,3},{2,1},{3,0},{4,6},{5,7},{6,5},{7,4},{8,10},{9,11},{10,... | collective-permute-start | bytes 983048 | tf_op jit(solution)/shard_map/ppermute | solution.py:198
  49.3 40.3 %collective-permute-start.6 = (bf16[2,128,640]{2,1,0:T(8,128)(2,1)S(1)}, bf16[2,128,640]{2,1,0:T(8,128)(2,1)S(1)}, u32[]{:S(2)}, u32[]{:S(2)}) collective-permute-start(bf16[2,128,640]{2,1,0:T(8,128)(2,1)S(1)} %pack.22), channel_id=1, source_target_pairs={{0,1},{1,0},{2,3},{3,2},{4,5},{5,4},{6,7},{7,6},{8,9},{9,8},{10,11... | collective-permute-start | bytes 983048 | tf_op jit(solution)/shard_map/ppermute | solution.py:198
  56.4 33.3 %collective-permute-start.7 = (bf16[2,128,640]{2,1,0:T(8,128)(2,1)S(1)}, bf16[2,128,640]{2,1,0:T(8,128)(2,1)S(1)}, u32[]{:S(2)}, u32[]{:S(2)}) collective-permute-start(bf16[2,128,640]{2,1,0:T(8,128)(2,1)S(1)} %pack.23), channel_id=1, source_target_pairs={{0,1},{1,0},{2,3},{3,2},{4,5},{5,4},{6,7},{7,6},{8,9},{9,8},{10,11... | collective-permute-start | bytes 983048 | tf_op jit(solution)/shard_map/ppermute | solution.py:198
  63.4 28.0 %collective-permute-start.8 = (bf16[2,128,640]{2,1,0:T(8,128)(2,1)S(1)}, bf16[2,128,640]{2,1,0:T(8,128)(2,1)S(1)}, u32[]{:S(2)}, u32[]{:S(2)}) collective-permute-start(bf16[2,128,640]{2,1,0:T(8,128)(2,1)S(1)} %pack.24), channel_id=1, source_target_pairs={{0,1},{1,0},{2,3},{3,2},{4,5},{5,4},{6,7},{7,6},{8,9},{9,8},{10,11... | collective-permute-start | bytes 983048 | tf_op jit(solution)/shard_map/ppermute | solution.py:198
  63.5 28.0 %collective-permute-start.9 = (bf16[2,128,640]{2,1,0:T(8,128)(2,1)S(1)}, bf16[2,128,640]{2,1,0:T(8,128)(2,1)S(1)}, u32[]{:S(2)}, u32[]{:S(2)}) collective-permute-start(bf16[2,128,640]{2,1,0:T(8,128)(2,1)S(1)} %pack.25), channel_id=1, source_target_pairs={{0,2},{1,3},{2,1},{3,0},{4,6},{5,7},{6,5},{7,4},{8,10},{9,11},{10,... | collective-permute-start | bytes 983048 | tf_op jit(solution)/shard_map/ppermute | solution.py:198
  71.0 59.1 %collective-permute-start.2 = (bf16[6,128,384]{2,1,0:T(8,128)(2,1)S(1)}, bf16[6,128,384]{2,1,0:T(8,128)(2,1)S(1)}, u32[]{:S(2)}, u32[]{:S(2)}) collective-permute-start(bf16[6,128,384]{2,1,0:T(8,128)(2,1)S(1)} %pack.14.refs_6_), channel_id=1, source_target_pairs={{0,3},{1,2},{2,0},{3,1},{4,7},{5,6},{6,4},{7,5},{8,11},{9,10},{10,... | collective-permute-start | bytes 1769480 | tf_op jit(solution)/shard_map/ppermute | solution.py:198
  89.6 43.9 %collective-permute-start = (bf16[6,128,384]{2,1,0:T(8,128)(2,1)S(1)}, bf16[6,128,384]{2,1,0:T(8,128)(2,1)S(1)}, u32[]{:S(2)}, u32[]{:S(2)}) collective-permute-start(bf16[6,128,384]{2,1,0:T(8,128)(2,1)S(1)} %pack.16), channel_id=1, source_target_pairs={{0,1},{1,0},{2,3},{3,2},{4,5},{5,4},{6,7},{7,6},{8,9},{9,8},{10,11... | collective-permute-start | bytes 1769480 | tf_op jit(solution)/shard_map/ppermute | solution.py:198
  89.7 43.8 %collective-permute-start.1 = (bf16[6,128,384]{2,1,0:T(8,128)(2,1)S(1)}, bf16[6,128,384]{2,1,0:T(8,128)(2,1)S(1)}, u32[]{:S(2)}, u32[]{:S(2)}) collective-permute-start(bf16[6,128,384]{2,1,0:T(8,128)(2,1)S(1)} %pack.17), channel_id=1, source_target_pairs={{0,2},{1,3},{2,1},{3,0},{4,6},{5,7},{6,5},{7,4},{8,10},{9,11},{10,... | collective-permute-start | bytes 1769480 | tf_op jit(solution)/shard_map/ppermute | solution.py:198
  102.5 63.3 %collective-permute-start.17 = (bf16[2,128,640]{2,1,0:T(8,128)(2,1)S(1)}, bf16[2,128,640]{2,1,0:T(8,128)(2,1)S(1)}, u32[]{:S(2)}, u32[]{:S(2)}) collective-permute-start(bf16[2,128,640]{2,1,0:T(8,128)(2,1)S(1)} %get-tuple-element.30), channel_id=1, source_target_pairs={{1,0},{0,1},{3,2},{2,3},{5,4},{4,5},{7,6},{6,7},{9,8},{8,9},{11,10... | collective-permute-start | bytes 983048 | tf_op jit(solution)/shard_map/ppermute | solution.py:201
  115.8 52.1 %collective-permute-start.16 = (bf16[2,128,640]{2,1,0:T(8,128)(2,1)S(1)}, bf16[2,128,640]{2,1,0:T(8,128)(2,1)S(1)}, u32[]{:S(2)}, u32[]{:S(2)}) collective-permute-start(bf16[2,128,640]{2,1,0:T(8,128)(2,1)S(1)} %get-tuple-element.29), channel_id=1, source_target_pairs={{2,0},{3,1},{1,2},{0,3},{6,4},{7,5},{5,6},{4,7},{10,8},{11,9},{9,1... | collective-permute-start | bytes 983048 | tf_op jit(solution)/shard_map/ppermute | solution.py:201
  130.1 38.5 %collective-permute-start.15 = (bf16[2,128,640]{2,1,0:T(8,128)(2,1)S(1)}, bf16[2,128,640]{2,1,0:T(8,128)(2,1)S(1)}, u32[]{:S(2)}, u32[]{:S(2)}) collective-permute-start(bf16[2,128,640]{2,1,0:T(8,128)(2,1)S(1)} %get-tuple-element.28), channel_id=1, source_target_pairs={{3,0},{2,1},{0,2},{1,3},{7,4},{6,5},{4,6},{5,7},{11,8},{10,9},{8,1... | collective-permute-start | bytes 983048 | tf_op jit(solution)/shard_map/ppermute | solution.py:201
  140.1 30.0 %collective-permute-start.5 = (bf16[2,128,384]{2,1,0:T(8,128)(2,1)S(1)}, bf16[2,128,384]{2,1,0:T(8,128)(2,1)S(1)}, u32[]{:S(2)}, u32[]{:S(2)}) collective-permute-start(bf16[2,128,384]{2,1,0:T(8,128)(2,1)S(1)} %get-tuple-element.26), channel_id=1, source_target_pairs={{1,0},{0,1},{3,2},{2,3},{5,4},{4,5},{7,6},{6,7},{9,8},{8,9},{11,10... | collective-permute-start | bytes 589832 | tf_op jit(solution)/shard_map/ppermute | solution.py:201
  163.3 19.5 %collective-permute-start.4 = (bf16[2,128,384]{2,1,0:T(8,128)(2,1)S(1)}, bf16[2,128,384]{2,1,0:T(8,128)(2,1)S(1)}, u32[]{:S(2)}, u32[]{:S(2)}) collective-permute-start(bf16[2,128,384]{2,1,0:T(8,128)(2,1)S(1)} %get-tuple-element.25), channel_id=1, source_target_pairs={{2,0},{3,1},{1,2},{0,3},{6,4},{7,5},{5,6},{4,7},{10,8},{11,9},{9,1... | collective-permute-start | bytes 589832 | tf_op jit(solution)/shard_map/ppermute | solution.py:201
  165.8 17.7 %collective-permute-start.3 = (bf16[2,128,384]{2,1,0:T(8,128)(2,1)S(1)}, bf16[2,128,384]{2,1,0:T(8,128)(2,1)S(1)}, u32[]{:S(2)}, u32[]{:S(2)}) collective-permute-start(bf16[2,128,384]{2,1,0:T(8,128)(2,1)S(1)} %get-tuple-element.24), channel_id=1, source_target_pairs={{3,0},{2,1},{0,2},{1,3},{7,4},{6,5},{4,6},{5,7},{11,8},{10,9},{8,1... | collective-permute-start | bytes 589832 | tf_op jit(solution)/shard_map/ppermute | solution.py:201

commit v9 on v5

--- a/solution.py
+++ b/solution.py
@@ -211,7 +211,9 @@
     outs = ()
     for (base, width), messages in zip(chunks, received):
         own, *results = attend(messages)
-        returned = [back(m, r) for r, m in enumerate(results)]
+        order = range(len(groups)) if base else reversed(range(len(groups)))
+        sends = {r: back(results[r], r) for r in order}
+        returned = [sends[r] for r in range(len(groups))]
         outs = place(outs, [own], [own_group], span, base, shape)
         for group, message in zip(groups, returned):
             outs = place(outs, [message], [group], span, base, shape)

time: 185 us -> 185 us (level)
  no operation moved by 1% of the time
where the time goes in v9:
time: 185 us
  starting transfers between devices  84.6 us (46%)
  waiting for transfers between devices  65.8 us (36%)
  Pallas kernels  33.4 us (18%)
    ppermute x6, starting transfers between devices, back(): lax.ppermute(message, 'seq', [(b, a) for a, b in enumerate(rounds[r][1])])  73.8 us
    ppermute x6, waiting for transfers between devices, there(): return lax.ppermute(message, 'seq', list(enumerate(rounds[r][1])))  53.7 us
    pallas_call x2, Pallas kernels, attend(): pl.pallas_call(functools.partial(attend_kernel, layout), out_shape=[jax.S...  17.5 us
    ppermute x6, waiting for transfers between devices, back(): lax.ppermute(message, 'seq', [(b, a) for a, b in enumerate(rounds[r][1])])  12.1 us
    ppermute x6, starting transfers between devices, there(): return lax.ppermute(message, 'seq', list(enumerate(rounds[r][1])))  10.8 us
    pallas_call x8, Pallas kernels, pack(): pl.pallas_call(functools.partial(pack_kernel, groups, count, span, base,...  10.1 us
    pallas_call x8, Pallas kernels, place(): pl.pallas_call(functools.partial(place_kernel, groups, span, base, width)...  5.79 us
  transfers between devices with their start and end apart: 12, of which 3 were waited for; matrix products, arithmetic and copies ran while one was open for 0% of the time, Pallas kernels for 17%

profile of v9, /device:TPU:0, one launch (start us, length us, event | category | flops | bytes accessed | tf_op | source)
XLA Modules:
  0.0 184.6 jit_solution(8825302148363424965)
XLA Ops:
  0.6 1.4 pack.12.refs_6_
  2.0 5.1 %collective-permute-start.8 = (bf16[6,128,640]{2,1,0:T(8,128)(2,1)S(1)}, bf16[6,128,640]{2,1,0:T(8,128)(2,1)S(1)}, u32[]{:S(2)}, u32[]{:S(2)}) collective-permute-start(bf16[6,128,640]{2,1,0:T(8,128)(2,1)S(1)} %pack.12.refs_6_), channel_id=1, source_target_pairs={{0,3},{1,2},{2,0},{3,1},{4,7},{5,6},{6,4},{7,5},{8,11},{9,10},{10,... | collective-permute-start | bytes 2949128 | tf_op jit(solution)/shard_map/ppermute | solution.py:196
  7.1 1.3 pack.14
  8.4 0.1 collective-permute-start.6
  8.5 1.4 pack.15
  9.9 0.9 collective-permute-start.7
  10.8 1.2 pack.8.refs_6_
  12.0 3.0 %collective-permute-start.2 = (bf16[6,128,384]{2,1,0:T(8,128)(2,1)S(1)}, bf16[6,128,384]{2,1,0:T(8,128)(2,1)S(1)}, u32[]{:S(2)}, u32[]{:S(2)}) collective-permute-start(bf16[6,128,384]{2,1,0:T(8,128)(2,1)S(1)} %pack.8.refs_6_), channel_id=1, source_target_pairs={{0,3},{1,2},{2,0},{3,1},{4,7},{5,6},{6,4},{7,5},{8,11},{9,10},{10,... | collective-permute-start | bytes 1769480 | tf_op jit(solution)/shard_map/ppermute | solution.py:196
  15.0 1.2 pack.10
  16.2 0.3 collective-permute-start
  16.5 1.2 pack.11
  17.7 33.0 %collective-permute-done.8.refs_3_ = bf16[6,128,640]{2,1,0:T(8,128)(2,1)S(1)} collective-permute-done((bf16[6,128,640]{2,1,0:T(8,128)(2,1)S(1)}, bf16[6,128,640]{2,1,0:T(8,128)(2,1)S(1)}, u32[]{:S(2)}, u32[]{:S(2)}) %collective-permute-start.8) | collective-permute-done | bytes 983072 | tf_op jit(solution)/shard_map/ppermute | solution.py:196
  50.6 1.4 collective-permute-start.1
  52.1 1.3 pack.13.refs_0_
  53.4 20.7 %collective-permute-done.6.refs_1_ = bf16[6,128,640]{2,1,0:T(8,128)(2,1)S(1)} collective-permute-done((bf16[6,128,640]{2,1,0:T(8,128)(2,1)S(1)}, bf16[6,128,640]{2,1,0:T(8,128)(2,1)S(1)}, u32[]{:S(2)}, u32[]{:S(2)}) %collective-permute-start.6) | collective-permute-done | bytes 983072 | tf_op jit(solution)/shard_map/ppermute | solution.py:196
  74.2 0.0 collective-permute-done.7.refs_2_
  74.2 10.9 %attend.3 = (bf16[2,128,640]{2,1,0:T(8,128)(2,1)S(1)}, bf16[2,128,640]{2,1,0:T(8,128)(2,1)S(1)}, bf16[2,128,640]{2,1,0:T(8,128)(2,1)S(1)}, bf16[2,128,640]{2,1,0:T(8,128)(2,1)S(1)}) custom-call(bf16[6,128,640]{2,1,0:T(8,128)(2,1)S(1)} %pack.13.refs_0_, bf16[6,128,640]{2,1,0:T(8,128)(2,1)S(1)} %collective-permute-done.6.refs_1_, ...), custom_call_target="tpu_custom_call" | custom-call | flops 2013265920 | bytes 5242880 | tf_op jit(solution)/shard_map/attend/pallas_call | solution.py:170
  85.1 43.7 %collective-permute-start.11 = (bf16[2,128,640]{2,1,0:T(8,128)(2,1)S(1)}, bf16[2,128,640]{2,1,0:T(8,128)(2,1)S(1)}, u32[]{:S(2)}, u32[]{:S(2)}) collective-permute-start(bf16[2,128,640]{2,1,0:T(8,128)(2,1)S(1)} %get-tuple-element.30), channel_id=1, source_target_pairs={{1,0},{0,1},{3,2},{2,3},{5,4},{4,5},{7,6},{6,7},{9,8},{8,9},{11,10... | collective-permute-start | bytes 983048 | tf_op jit(solution)/shard_map/ppermute | solution.py:199
  128.8 2.4 %collective-permute-start.10 = (bf16[2,128,640]{2,1,0:T(8,128)(2,1)S(1)}, bf16[2,128,640]{2,1,0:T(8,128)(2,1)S(1)}, u32[]{:S(2)}, u32[]{:S(2)}) collective-permute-start(bf16[2,128,640]{2,1,0:T(8,128)(2,1)S(1)} %get-tuple-element.29), channel_id=1, source_target_pairs={{2,0},{3,1},{1,2},{0,3},{6,4},{7,5},{5,6},{4,7},{10,8},{11,9},{9,1... | collective-permute-start | bytes 983048 | tf_op jit(solution)/shard_map/ppermute | solution.py:199
  131.2 0.0 collective-permute-done.2.refs_3_
  131.2 0.7 collective-permute-start.9
  131.8 1.2 pack.9.refs_0_
  133.0 0.0 collective-permute-done.refs_1_
  133.0 0.0 collective-permute-done.1.refs_2_
  133.1 6.6 %attend.2 = (bf16[2,128,384]{2,1,0:T(8,128)(2,1)S(1)}, bf16[2,128,384]{2,1,0:T(8,128)(2,1)S(1)}, bf16[2,128,384]{2,1,0:T(8,128)(2,1)S(1)}, bf16[2,128,384]{2,1,0:T(8,128)(2,1)S(1)}) custom-call(bf16[6,128,384]{2,1,0:T(8,128)(2,1)S(1)} %pack.9.refs_0_, bf16[6,128,384]{2,1,0:T(8,128)(2,1)S(1)} %collective-permute-done.refs_1_, ...), custom_call_target="tpu_custom_call" | custom-call | flops 1207959552 | bytes 3145728 | tf_op jit(solution)/shard_map/attend/pallas_call | solution.py:170
  139.7 24.1 %collective-permute-start.5 = (bf16[2,128,384]{2,1,0:T(8,128)(2,1)S(1)}, bf16[2,128,384]{2,1,0:T(8,128)(2,1)S(1)}, u32[]{:S(2)}, u32[]{:S(2)}) collective-permute-start(bf16[2,128,384]{2,1,0:T(8,128)(2,1)S(1)} %get-tuple-element.26), channel_id=1, source_target_pairs={{1,0},{0,1},{3,2},{2,3},{5,4},{4,5},{7,6},{6,7},{9,8},{8,9},{11,10... | collective-permute-start | bytes 589832 | tf_op jit(solution)/shard_map/ppermute | solution.py:199
  163.7 2.5 %collective-permute-start.4 = (bf16[2,128,384]{2,1,0:T(8,128)(2,1)S(1)}, bf16[2,128,384]{2,1,0:T(8,128)(2,1)S(1)}, u32[]{:S(2)}, u32[]{:S(2)}) collective-permute-start(bf16[2,128,384]{2,1,0:T(8,128)(2,1)S(1)} %get-tuple-element.25), channel_id=1, source_target_pairs={{2,0},{3,1},{1,2},{0,3},{6,4},{7,5},{5,6},{4,7},{10,8},{11,9},{9,1... | collective-permute-start | bytes 589832 | tf_op jit(solution)/shard_map/ppermute | solution.py:199
  166.2 0.0 collective-permute-done.11.refs_0_
  166.2 0.5 collective-permute-start.3
  166.7 0.7 place.8
  167.4 0.8 place.9
  168.2 0.0 collective-permute-done.10.refs_0_
  168.2 0.8 place.10
  169.0 0.0 collective-permute-done.9.refs_0_
  169.0 0.8 place.11
  169.7 0.7 place.12
  170.4 0.0 collective-permute-done.5.refs_0_
  170.4 0.7 place.13
  171.2 12.0 %collective-permute-done.4.refs_0_ = bf16[2,128,384]{2,1,0:T(8,128)(2,1)S(1)} collective-permute-done((bf16[2,128,384]{2,1,0:T(8,128)(2,1)S(1)}, bf16[2,128,384]{2,1,0:T(8,128)(2,1)S(1)}, u32[]{:S(2)}, u32[]{:S(2)}) %collective-permute-start.4) | collective-permute-done | bytes 196640 | tf_op jit(solution)/shard_map/ppermute | solution.py:199
  183.2 0.7 place.14
  183.9 0.0 collective-permute-done.3.refs_0_
  183.9 0.7 place.15
Async XLA Ops:
  2.0 48.7 %collective-permute-start.8 = (bf16[6,128,640]{2,1,0:T(8,128)(2,1)S(1)}, bf16[6,128,640]{2,1,0:T(8,128)(2,1)S(1)}, u32[]{:S(2)}, u32[]{:S(2)}) collective-permute-start(bf16[6,128,640]{2,1,0:T(8,128)(2,1)S(1)} %pack.12.refs_6_), channel_id=1, source_target_pairs={{0,3},{1,2},{2,0},{3,1},{4,7},{5,6},{6,4},{7,5},{8,11},{9,10},{10,... | collective-permute-start | bytes 2949128 | tf_op jit(solution)/shard_map/ppermute | solution.py:196
  8.4 65.7 %collective-permute-start.6 = (bf16[6,128,640]{2,1,0:T(8,128)(2,1)S(1)}, bf16[6,128,640]{2,1,0:T(8,128)(2,1)S(1)}, u32[]{:S(2)}, u32[]{:S(2)}) collective-permute-start(bf16[6,128,640]{2,1,0:T(8,128)(2,1)S(1)} %pack.14), channel_id=1, source_target_pairs={{0,1},{1,0},{2,3},{3,2},{4,5},{5,4},{6,7},{7,6},{8,9},{9,8},{10,11... | collective-permute-start | bytes 2949128 | tf_op jit(solution)/shard_map/ppermute | solution.py:196
  9.9 64.3 %collective-permute-start.7 = (bf16[6,128,640]{2,1,0:T(8,128)(2,1)S(1)}, bf16[6,128,640]{2,1,0:T(8,128)(2,1)S(1)}, u32[]{:S(2)}, u32[]{:S(2)}) collective-permute-start(bf16[6,128,640]{2,1,0:T(8,128)(2,1)S(1)} %pack.15), channel_id=1, source_target_pairs={{0,2},{1,3},{2,1},{3,0},{4,6},{5,7},{6,5},{7,4},{8,10},{9,11},{10,... | collective-permute-start | bytes 2949128 | tf_op jit(solution)/shard_map/ppermute | solution.py:196
  12.0 119.2 %collective-permute-start.2 = (bf16[6,128,384]{2,1,0:T(8,128)(2,1)S(1)}, bf16[6,128,384]{2,1,0:T(8,128)(2,1)S(1)}, u32[]{:S(2)}, u32[]{:S(2)}) collective-permute-start(bf16[6,128,384]{2,1,0:T(8,128)(2,1)S(1)} %pack.8.refs_6_), channel_id=1, source_target_pairs={{0,3},{1,2},{2,0},{3,1},{4,7},{5,6},{6,4},{7,5},{8,11},{9,10},{10,... | collective-permute-start | bytes 1769480 | tf_op jit(solution)/shard_map/ppermute | solution.py:196
  16.2 116.8 %collective-permute-start = (bf16[6,128,384]{2,1,0:T(8,128)(2,1)S(1)}, bf16[6,128,384]{2,1,0:T(8,128)(2,1)S(1)}, u32[]{:S(2)}, u32[]{:S(2)}) collective-permute-start(bf16[6,128,384]{2,1,0:T(8,128)(2,1)S(1)} %pack.10), channel_id=1, source_target_pairs={{0,1},{1,0},{2,3},{3,2},{4,5},{5,4},{6,7},{7,6},{8,9},{9,8},{10,11... | collective-permute-start | bytes 1769480 | tf_op jit(solution)/shard_map/ppermute | solution.py:196
  50.6 82.4 %collective-permute-start.1 = (bf16[6,128,384]{2,1,0:T(8,128)(2,1)S(1)}, bf16[6,128,384]{2,1,0:T(8,128)(2,1)S(1)}, u32[]{:S(2)}, u32[]{:S(2)}) collective-permute-start(bf16[6,128,384]{2,1,0:T(8,128)(2,1)S(1)} %pack.11), channel_id=1, source_target_pairs={{0,2},{1,3},{2,1},{3,0},{4,6},{5,7},{6,5},{7,4},{8,10},{9,11},{10,... | collective-permute-start | bytes 1769480 | tf_op jit(solution)/shard_map/ppermute | solution.py:196
  85.1 81.1 %collective-permute-start.11 = (bf16[2,128,640]{2,1,0:T(8,128)(2,1)S(1)}, bf16[2,128,640]{2,1,0:T(8,128)(2,1)S(1)}, u32[]{:S(2)}, u32[]{:S(2)}) collective-permute-start(bf16[2,128,640]{2,1,0:T(8,128)(2,1)S(1)} %get-tuple-element.30), channel_id=1, source_target_pairs={{1,0},{0,1},{3,2},{2,3},{5,4},{4,5},{7,6},{6,7},{9,8},{8,9},{11,10... | collective-permute-start | bytes 983048 | tf_op jit(solution)/shard_map/ppermute | solution.py:199
  128.8 39.4 %collective-permute-start.10 = (bf16[2,128,640]{2,1,0:T(8,128)(2,1)S(1)}, bf16[2,128,640]{2,1,0:T(8,128)(2,1)S(1)}, u32[]{:S(2)}, u32[]{:S(2)}) collective-permute-start(bf16[2,128,640]{2,1,0:T(8,128)(2,1)S(1)} %get-tuple-element.29), channel_id=1, source_target_pairs={{2,0},{3,1},{1,2},{0,3},{6,4},{7,5},{5,6},{4,7},{10,8},{11,9},{9,1... | collective-permute-start | bytes 983048 | tf_op jit(solution)/shard_map/ppermute | solution.py:199
  131.2 37.8 %collective-permute-start.9 = (bf16[2,128,640]{2,1,0:T(8,128)(2,1)S(1)}, bf16[2,128,640]{2,1,0:T(8,128)(2,1)S(1)}, u32[]{:S(2)}, u32[]{:S(2)}) collective-permute-start(bf16[2,128,640]{2,1,0:T(8,128)(2,1)S(1)} %get-tuple-element.28), channel_id=1, source_target_pairs={{3,0},{2,1},{0,2},{1,3},{7,4},{6,5},{4,6},{5,7},{11,8},{10,9},{8,1... | collective-permute-start | bytes 983048 | tf_op jit(solution)/shard_map/ppermute | solution.py:199
  139.7 30.8 %collective-permute-start.5 = (bf16[2,128,384]{2,1,0:T(8,128)(2,1)S(1)}, bf16[2,128,384]{2,1,0:T(8,128)(2,1)S(1)}, u32[]{:S(2)}, u32[]{:S(2)}) collective-permute-start(bf16[2,128,384]{2,1,0:T(8,128)(2,1)S(1)} %get-tuple-element.26), channel_id=1, source_target_pairs={{1,0},{0,1},{3,2},{2,3},{5,4},{4,5},{7,6},{6,7},{9,8},{8,9},{11,10... | collective-permute-start | bytes 589832 | tf_op jit(solution)/shard_map/ppermute | solution.py:199
  163.7 19.5 %collective-permute-start.4 = (bf16[2,128,384]{2,1,0:T(8,128)(2,1)S(1)}, bf16[2,128,384]{2,1,0:T(8,128)(2,1)S(1)}, u32[]{:S(2)}, u32[]{:S(2)}) collective-permute-start(bf16[2,128,384]{2,1,0:T(8,128)(2,1)S(1)} %get-tuple-element.25), channel_id=1, source_target_pairs={{2,0},{3,1},{1,2},{0,3},{6,4},{7,5},{5,6},{4,7},{10,8},{11,9},{9,1... | collective-permute-start | bytes 589832 | tf_op jit(solution)/shard_map/ppermute | solution.py:199
  166.2 17.7 %collective-permute-start.3 = (bf16[2,128,384]{2,1,0:T(8,128)(2,1)S(1)}, bf16[2,128,384]{2,1,0:T(8,128)(2,1)S(1)}, u32[]{:S(2)}, u32[]{:S(2)}) collective-permute-start(bf16[2,128,384]{2,1,0:T(8,128)(2,1)S(1)} %get-tuple-element.24), channel_id=1, source_target_pairs={{3,0},{2,1},{0,2},{1,3},{7,4},{6,5},{4,6},{5,7},{11,8},{10,9},{8,1... | collective-permute-start | bytes 589832 | tf_op jit(solution)/shard_map/ppermute | solution.py:199
